TPU v7x, 32 devices: a whole 2x2x4 slice. The times are simulated.
32 devices in a mesh: sec: 8 (over z, y), slab: 4 (over x, core).
Axes of the slice: x: 2, y: 2, z: 4, core: 2. Of those that a mesh axis runs over, the one named last changes fastest.
Arguments:
- basis: bfloat16 [16, 1024, 1024], P('sec'), may hold values from -0.1875 to 0.1875
- fermion: bfloat16 [3, 16, 1024, 1024], P(None, 'sec', None, 'slab'), may hold values from -6 to 6
- partner: int32 [3, 16], P(None, 'sec'), may hold values from 0 to 15, as said below
Outputs:
- rotated: bfloat16 [3, 16, 1024, 1024], P(None, 'sec', 'slab')
Inputs may be any that keep to these rules, and one draw needn't show every extreme that they name: partner[f, Q] // 2 equals Q // 2 or (Q // 2 + 1) % 8, so a partner lies in the block of 2 sectors that holds Q or in the next block, the last block's next being the first.
All inputs are finite; a program needn't handle non-finite values.
Results may differ from a plain program's by a relative error of at most 0.0049.
Values may be sent and summed in bfloat16 or wider, within the bound.
No kernel may reach another device: no remote copies, remote signals or barrier semaphores. Data moves between devices by JAX's collectives and lax.ppermute only.
A program may use at most 64 MiB of HBM per device.

v0:
```python
import jax
import jax.numpy as jnp
from jax import lax
from jax.sharding import PartitionSpec as P


def shifted(block, axis, distance):
    devices = range(lax.axis_size(axis))
    route = [((i - distance) % len(devices), i) for i in devices]
    return lax.ppermute(block, axis, route)


def left_product(left_block, right_block):
    return lax.dot_general(
        left_block, right_block, (((0,), (0,)), ((), ())), preferred_element_type=jnp.float32
    ).astype(jnp.bfloat16)


def local(basis, fermion, partner):
    sectors_here = basis.shape[0]
    flavours = fermion.shape[0]
    all_sectors = sectors_here * lax.axis_size("sec")
    first_sector = lax.axis_index("sec") * sectors_here
    following = shifted(basis, "sec", -1)
    half_blocks = []
    for flavour in range(flavours):
        per_sector = []
        for sector in range(sectors_here):
            per_sector.append(left_product(basis[sector], fermion[flavour, sector]))
        half_blocks.append(jnp.stack(per_sector))
    half_rotated = jnp.stack(half_blocks)
    row_slabs = lax.all_to_all(half_rotated, "slab", split_axis=2, concat_axis=3, tiled=True)
    local_index = (partner - first_sector) % all_sectors
    out_blocks = []
    for flavour in range(flavours):
        per_sector = []
        for sector in range(sectors_here):
            where_index = local_index[flavour, sector]
            rows_here = row_slabs[flavour, sector]

            def from_own(operand):
                chosen = lax.dynamic_index_in_dim(
                    basis, jnp.minimum(where_index, sectors_here - 1), 0, keepdims=False
                )
                return jnp.dot(operand, chosen, preferred_element_type=jnp.float32)

            def from_next(operand):
                chosen = lax.dynamic_index_in_dim(
                    following, jnp.maximum(where_index - sectors_here, 0), 0, keepdims=False
                )
                return jnp.dot(operand, chosen, preferred_element_type=jnp.float32)

            product = lax.cond(where_index < sectors_here, from_own, from_next, rows_here)
            per_sector.append(product.astype(jnp.bfloat16))
        out_blocks.append(jnp.stack(per_sector))
    return jnp.stack(out_blocks)


def solution(mesh):
    placed = (P("sec", None, None), P(None, "sec", None, "slab"), P(None, "sec"))
    return jax.shard_map(
        local, mesh=mesh, in_specs=placed, out_specs=P(None, "sec", "slab", None), check_vma=False
    )
```

profile of v0, /device:TPU:0, one launch (start us, length us, event | category | flops | bytes accessed | tf_op | source)
XLA Modules:
  0.0 122.1 jit_solution(4679438172877214783)
XLA Ops:
  0.0 6.0 %collective-permute-start = (bf16[2,1024,1024]{2,1,0:T(8,128)(2,1)}, bf16[2,1024,1024]{2,1,0:T(8,128)(2,1)}, u32[]{:S(2)}, u32[]{:S(2)}) collective-permute-start(bf16[2,1024,1024]{2,1,0:T(8,128)(2,1)} %param.15), channel_id=1, source_target_pairs={{4,0},{8,4},{12,8},{16,12},{20,16},{24,20},{28,24},{0,28},{5,1},{9... | collective-permute-start | bytes 12582920 | tf_op jit(solution)/shard_map/ppermute | solution.py:10
  6.0 2.4 %fusion.159 = bf16[1,1024,256]{2,1,0:T(8,128)(2,1)S(1)} fusion(bf16[2,1024,1024]{2,1,0:T(8,128)(2,1)} %param.15, bf16[3,2,1024,256]{3,2,1,0:T(8,128)(2,1)} %param.16), kind=kOutput, calls=%fused_computation.99 | convolution fusion | flops 537133056 | bytes 3145728 | tf_op jit(solution)/shard_map/dot_general | solution.py:14
  8.4 0.0 copy-done.5
  8.5 0.0 copy-done.6
  8.5 0.8 fusion.156
  9.3 0.8 fusion.165
  10.0 0.1 maximum_bitcast_fusion.2
  10.1 0.8 fusion.162
  10.9 0.8 fusion.168
  11.7 0.8 fusion.171
  12.5 0.2 maximum_bitcast_fusion
  12.7 0.3 pad_maximum_fusion
  13.0 4.9 %copy.11 = bf16[3,2,1024,256]{3,1,0,2:T(2,128)(2,1)} copy(bf16[3,2,1024,256]{3,2,1,0:T(8,128)(2,1)S(1)} %pad_maximum_fusion) | data formatting | bytes 6291456 | tf_op jit(solution)/shard_map/stack | solution.py:31
  17.9 4.0 %all-to-all-start = ((bf16[3,2,1024,256]{3,1,0,2:T(2,128)(2,1)}), bf16[3,2,1024,256]{3,1,0,2:T(2,128)(2,1)S(1)}, u32[]{:S(2)}, u32[]{:S(2)}) async-start(bf16[3,2,1024,256]{3,1,0,2:T(2,128)(2,1)} %copy.11), calls=%async_computation | async-start | bytes 6291456 | tf_op jit(solution)/shard_map/all_to_all | solution.py:32
  22.0 0.0 copy-done.4
  22.0 0.7 fusion.187
  26.4 32.3 %all-to-all-done = bf16[3,2,1024,256]{3,1,0,2:T(2,128)(2,1)S(1)} async-done(((bf16[3,2,1024,256]{3,1,0,2:T(2,128)(2,1)}), bf16[3,2,1024,256]{3,1,0,2:T(2,128)(2,1)S(1)}, u32[]{:S(2)}, u32[]{:S(2)}) %all-to-all-start) | async-done | bytes 3145760 | tf_op jit(solution)/shard_map/all_to_all | solution.py:32
  58.7 4.1 %copy.12 = bf16[3,2,256,4,256]{4,3,2,1,0:T(4,128)(2,1)} copy(bf16[3,2,256,4,256]{4,1,0,2,3:T(2,128)(2,1)S(1)} %bitcast.245) | data formatting | bytes 6291456 | tf_op jit(solution)/shard_map/all_to_all | solution.py:32
  62.8 4.7 %all_to_all.16 = bf16[3,2,256,1024]{3,2,1,0:T(8,128)(2,1)S(1)} reshape(bf16[3,2,256,4,256]{4,3,2,1,0:T(4,128)(2,1)} %copy.12) | data formatting | bytes 6291456 | tf_op jit(solution)/shard_map/all_to_all | solution.py:32
  67.5 1.7 %slice_bitcast_fusion.5 = (bf16[256,1024]{1,0:T(8,128)(2,1)}, bf16[256,1024]{1,0:T(8,128)(2,1)}, bf16[256,1024]{1,0:T(8,128)(2,1)}, bf16[256,1024]{1,0:T(8,128)(...) fusion(bf16[3,2,256,1024]{3,2,1,0:T(8,128)(2,1)S(1)} %all_to_all.16), kind=kLoop, calls=%fused_computation.115 | loop fusion | bytes 6291456 | tf_op jit(solution)/shard_map/squeeze | solution.py:39
  69.2 27.0 %collective-permute-done = bf16[2,1024,1024]{2,1,0:T(8,128)(2,1)} collective-permute-done((bf16[2,1024,1024]{2,1,0:T(8,128)(2,1)}, bf16[2,1024,1024]{2,1,0:T(8,128)(2,1)}, u32[]{:S(2)}, u32[]{:S(2)}) %collective-permute-start) | collective-permute-done | bytes 4194336 | tf_op jit(solution)/shard_map/ppermute | solution.py:10
  96.2 3.3 %conditional.6 = (bf16[1,256,1024]{2,1,0:T(8,128)(2,1)S(1)}) conditional(s32[]{:T(128)} %convert_element_type.114, (s32[]{:T(128)}, bf16[2,1024,1024]{2,1,0:T(8,128)(2,1)}, bf16[256,1024]{1,0:T(8,128)(2,1)}) %tuple.53, (s32[]{:T(128)}, bf16[2,1024,1024]{2,1,0:T(8,128)(2,1)}, bf16[256,1024]{1,0:T(8,128)(2,1)}) %tuple.54), branch_computations={%region_0.1_spmd, %region_1.2_spmd} | conditional | flops 537133056 | bytes 4194362 | solution.py:53
  96.8 2.4 %fusion.6 = bf16[1,256,1024]{1,2,0:T(8,128)(2,1)S(1)} fusion(bf16[256,1024]{1,0:T(8,128)(2,1)} %get-tuple-element.103, bf16[2,1024,1024]{2,1,0:T(8,128)(2,1)} %get-tuple-element.101, s32[]{:T(128)S(6)} %max.12), kind=kOutput, calls=%fused_computation.4 | convolution fusion | flops 537133056 | bytes 3145732 | tf_op jit(solution)/shard_map/cond/branch_0_fun/dot_general | solution.py:51
  99.3 0.2 copy.19
  99.5 0.0 copy-done.3
  99.5 0.0 copy-start.2
  99.5 3.3 %conditional.7 = (bf16[1,256,1024]{2,1,0:T(8,128)(2,1)S(1)}) conditional(s32[]{:T(128)} %convert_element_type.121, (s32[]{:T(128)}, bf16[2,1024,1024]{2,1,0:T(8,128)(2,1)}, bf16[256,1024]{1,0:T(8,128)(2,1)S(1)}) %tuple.106, (s32[]{:T(128)}, bf16[2,1024,1024]{2,1,0:T(8,128)(2,1)}, bf16[256,1024]{1,0:T(8,128)(2,1)S(1)}) %tuple.107), branch_computations={%region_2.3_spmd, %region_3.4_spmd} | conditional | flops 537133056 | bytes 4194362 | solution.py:53
  100.2 2.4 %fusion.26 = bf16[1,256,1024]{1,2,0:T(8,128)(2,1)S(1)} fusion(bf16[256,1024]{1,0:T(8,128)(2,1)S(1)} %get-tuple-element.109, bf16[2,1024,1024]{2,1,0:T(8,128)(2,1)} %get-tuple-element.107, s32[]{:T(128)S(6)} %max.13), kind=kOutput, calls=%fused_computation.16 | convolution fusion | flops 537133056 | bytes 3145732 | tf_op jit(solution)/shard_map/cond/branch_0_fun/dot_general | solution.py:51
  102.6 0.2 copy.21
  102.8 0.1 maximum_bitcast_fusion.3
  102.9 0.0 copy-done.2
  103.0 3.3 %conditional.8 = (bf16[1,256,1024]{2,1,0:T(8,128)(2,1)S(1)}) conditional(s32[]{:T(128)} %convert_element_type.122, (s32[]{:T(128)}, bf16[2,1024,1024]{2,1,0:T(8,128)(2,1)}, bf16[256,1024]{1,0:T(8,128)(2,1)S(1)}) %tuple.104, (s32[]{:T(128)}, bf16[2,1024,1024]{2,1,0:T(8,128)(2,1)}, bf16[256,1024]{1,0:T(8,128)(2,1)S(1)}) %tuple.105), branch_computations={%region_4.5_spmd, %region_5.6_spmd} | conditional | flops 537133056 | bytes 4194362 | solution.py:53
  103.7 2.4 %fusion.56 = bf16[1,256,1024]{1,2,0:T(8,128)(2,1)S(1)} fusion(bf16[256,1024]{1,0:T(8,128)(2,1)S(1)} %get-tuple-element.118, bf16[2,1024,1024]{2,1,0:T(8,128)(2,1)} %get-tuple-element.116, s32[]{:T(128)S(6)} %select_n.27), kind=kOutput, calls=%fused_computation.34 | convolution fusion | flops 537133056 | bytes 3145732 | tf_op jit(solution)/shard_map/cond/branch_1_fun/dot_general | solution.py:45
  106.1 0.2 copy.24
  106.3 0.0 copy-done.1
  106.3 3.2 %conditional.9 = (bf16[1,256,1024]{2,1,0:T(8,128)(2,1)S(1)}) conditional(s32[]{:T(128)} %convert_element_type.123, (s32[]{:T(128)}, bf16[2,1024,1024]{2,1,0:T(8,128)(2,1)}, bf16[256,1024]{1,0:T(8,128)(2,1)S(1)}) %tuple.102, (s32[]{:T(128)}, bf16[2,1024,1024]{2,1,0:T(8,128)(2,1)}, bf16[256,1024]{1,0:T(8,128)(2,1)S(1)}) %tuple.103), branch_computations={%region_6.7_spmd, %region_7.8_spmd} | conditional | flops 537133056 | bytes 4194362 | solution.py:53
  106.9 2.4 %fusion.66 = bf16[1,256,1024]{1,2,0:T(8,128)(2,1)S(1)} fusion(bf16[256,1024]{1,0:T(8,128)(2,1)S(1)} %get-tuple-element.121, bf16[2,1024,1024]{2,1,0:T(8,128)(2,1)} %get-tuple-element.119, s32[]{:T(128)S(6)} %max.15), kind=kOutput, calls=%fused_computation.40 | convolution fusion | flops 537133056 | bytes 3145732 | tf_op jit(solution)/shard_map/cond/branch_0_fun/dot_general | solution.py:51
  109.2 0.2 copy.25
  109.5 0.1 maximum_bitcast_fusion.4
  109.6 5.4 %conditional.10 = (bf16[1,256,1024]{2,1,0:T(8,128)(2,1)S(1)}) conditional(s32[]{:T(128)} %convert_element_type.124, (s32[]{:T(128)}, bf16[2,1024,1024]{2,1,0:T(8,128)(2,1)}, bf16[256,1024]{1,0:T(8,128)(2,1)}) %tuple.61, (s32[]{:T(128)}, bf16[2,1024,1024]{2,1,0:T(8,128)(2,1)}, bf16[256,1024]{1,0:T(8,128)(2,1)}) %tuple.62), branch_computations={%region_8.9_spmd, %region_9.10_spmd} | conditional | flops 537133056 | bytes 4194362 | solution.py:53
  110.5 3.2 %fusion.86 = bf16[1,256,1024]{1,2,0:T(8,128)(2,1)} fusion(bf16[256,1024]{1,0:T(8,128)(2,1)} %get-tuple-element.127, bf16[2,1024,1024]{2,1,0:T(8,128)(2,1)} %get-tuple-element.125, s32[]{:T(128)S(6)} %max.16), kind=kOutput, calls=%fused_computation.52 | convolution fusion | flops 537133056 | bytes 3145732 | tf_op jit(solution)/shard_map/cond/branch_0_fun/dot_general | solution.py:51
  113.7 1.2 %copy.27 = bf16[1,256,1024]{2,1,0:T(8,128)(2,1)S(1)} copy(bf16[1,256,1024]{1,2,0:T(8,128)(2,1)} %fusion.86) | data formatting | bytes 1048576 | tf_op jit(solution)/shard_map/cond | solution.py:53
  115.0 0.0 copy-done
  115.0 5.0 %conditional.11 = (bf16[1,256,1024]{2,1,0:T(8,128)(2,1)S(1)}) conditional(s32[]{:T(128)} %convert_element_type.125, (s32[]{:T(128)}, bf16[2,1024,1024]{2,1,0:T(8,128)(2,1)}, bf16[256,1024]{1,0:T(8,128)(2,1)S(1)}) %tuple.100, (s32[]{:T(128)}, bf16[2,1024,1024]{2,1,0:T(8,128)(2,1)}, bf16[256,1024]{1,0:T(8,128)(2,1)S(1)}) %tuple.101), branch_computations={%region_10.11_spmd, %region_11.12_spmd} | conditional | flops 537133056 | bytes 4194362 | solution.py:53
  115.6 3.2 %fusion.106 = bf16[1,256,1024]{1,2,0:T(8,128)(2,1)} fusion(bf16[256,1024]{1,0:T(8,128)(2,1)S(1)} %get-tuple-element.133, bf16[2,1024,1024]{2,1,0:T(8,128)(2,1)} %get-tuple-element.131, s32[]{:T(128)S(6)} %max.17), kind=kOutput, calls=%fused_computation.64 | convolution fusion | flops 537133056 | bytes 3145732 | tf_op jit(solution)/shard_map/cond/branch_0_fun/dot_general | solution.py:51
  118.7 1.2 %copy.29 = bf16[1,256,1024]{2,1,0:T(8,128)(2,1)S(1)} copy(bf16[1,256,1024]{1,2,0:T(8,128)(2,1)} %fusion.106) | data formatting | bytes 1048576 | tf_op jit(solution)/shard_map/cond | solution.py:53
  120.0 0.1 maximum_bitcast_fusion.5
  120.1 2.0 %pad_maximum_fusion.1 = bf16[3,2,256,1024]{3,2,1,0:T(8,128)(2,1)} fusion(bf16[1,2,256,1024]{3,2,1,0:T(8,128)(2,1)S(1)} %maximum_bitcast_fusion.5, bf16[1,2,256,1024]{3,2,1,0:T(8,128)(2,1)S(1)} %maximum_bitcast_fusion.4, bf16[1,2,256,1024]{3,2,1,0:T(8,128)(2,1)S(1)} %maximum_bitcast_fusion.3), kind=kLoop, calls=%fused_computation.73 | loop fusion | flops 3145728 | bytes 6291456 | tf_op jit(solution)/shard_map/stack | solution.py:56
  (7 shorter events, 0.0 us)
Async XLA Ops:
  0.0 8.4 %copy-start.5 = (bf16[2,1024,1024]{2,1,0:T(8,128)(2,1)S(1)}, bf16[2,1024,1024]{2,1,0:T(8,128)(2,1)}, u32[]{:S(2)}) copy-start(bf16[2,1024,1024]{2,1,0:T(8,128)(2,1)} %param.15) | copy-start | bytes 12582916
  0.0 8.5 %copy-start.6 = (bf16[3,2,1024,256]{3,2,1,0:T(8,128)(2,1)S(1)}, bf16[3,2,1024,256]{3,2,1,0:T(8,128)(2,1)}, u32[]{:S(2)}) copy-start(bf16[3,2,1024,256]{3,2,1,0:T(8,128)(2,1)} %param.16) | copy-start | bytes 9437188
  0.0 96.2 %collective-permute-start = (bf16[2,1024,1024]{2,1,0:T(8,128)(2,1)}, bf16[2,1024,1024]{2,1,0:T(8,128)(2,1)}, u32[]{:S(2)}, u32[]{:S(2)}) collective-permute-start(bf16[2,1024,1024]{2,1,0:T(8,128)(2,1)} %param.15), channel_id=1, source_target_pairs={{4,0},{8,4},{12,8},{16,12},{20,16},{24,20},{28,24},{0,28},{5,1},{9... | collective-permute-start | bytes 12582920 | tf_op jit(solution)/shard_map/ppermute | solution.py:10
  17.9 4.0 %copy-start.4 = (s32[3,2]{0,1:T(2,128)S(1)}, s32[3,2]{0,1:T(2,128)}, u32[]{:S(2)}) copy-start(s32[3,2]{0,1:T(2,128)} %param.17) | copy-start | bytes 76
  17.9 40.7 %all-to-all-start = ((bf16[3,2,1024,256]{3,1,0,2:T(2,128)(2,1)}), bf16[3,2,1024,256]{3,1,0,2:T(2,128)(2,1)S(1)}, u32[]{:S(2)}, u32[]{:S(2)}) async-start(bf16[3,2,1024,256]{3,1,0,2:T(2,128)(2,1)} %copy.11), calls=%async_computation | async-start | bytes 6291456 | tf_op jit(solution)/shard_map/all_to_all | solution.py:32
  96.2 3.4 %copy-start.3 = (bf16[256,1024]{1,0:T(8,128)(2,1)S(1)}, bf16[256,1024]{1,0:T(8,128)(2,1)}, u32[]{:S(2)}) copy-start(bf16[256,1024]{1,0:T(8,128)(2,1)} %get-tuple-element.148) | copy-start | bytes 1572868
  99.5 3.4 %copy-start.2 = (bf16[256,1024]{1,0:T(8,128)(2,1)S(1)}, bf16[256,1024]{1,0:T(8,128)(2,1)}, u32[]{:S(2)}) copy-start(bf16[256,1024]{1,0:T(8,128)(2,1)} %get-tuple-element.147) | copy-start | bytes 1572868
  102.9 3.3 %copy-start.1 = (bf16[256,1024]{1,0:T(8,128)(2,1)S(1)}, bf16[256,1024]{1,0:T(8,128)(2,1)}, u32[]{:S(2)}) copy-start(bf16[256,1024]{1,0:T(8,128)(2,1)} %get-tuple-element.146) | copy-start | bytes 1572868
  109.6 5.4 %copy-start = (bf16[256,1024]{1,0:T(8,128)(2,1)S(1)}, bf16[256,1024]{1,0:T(8,128)(2,1)}, u32[]{:S(2)}) copy-start(bf16[256,1024]{1,0:T(8,128)(2,1)} %get-tuple-element.144) | copy-start | bytes 1572868
where the time goes:
time: 123 us; the launch traced here: 122 us
  waiting for transfers between devices  59.2 us (48%)
  matrix products  22.2 us (18%)
  local copies, waits for them, and re-layouts  19.4 us (16%)
  starting transfers between devices  10 us (8%)
  loops' own time  4.28 us (3%)
  between operations  3.99 us (3%)
  other arithmetic  2.94 us (2%)
    all_to_all x1, waiting for transfers between devices, local(): lax.all_to_all(half_rotated, 'slab', split_axis=2, concat_axis=3, tiled=T...  32.3 us
    ppermute x1, waiting for transfers between devices, shifted(): return lax.ppermute(block, axis, route)  27 us
    dot_general x5, matrix products, from_next(): return jnp.dot(operand, chosen, preferred_element_type=jnp.float32)  13.5 us
    all_to_all x2, local copies, waits for them, and re-layouts, local(): lax.all_to_all(half_rotated, 'slab', split_axis=2, concat_axis=3, tiled=T...  8.77 us
    dot_general x6, matrix products, left_product(): lax.dot_general(left_block, right_block, (((0,), (0,)), ((), ())), prefer...  6.34 us
    ppermute x1, starting transfers between devices, shifted(): return lax.ppermute(block, axis, route)  6 us
    another operation x1, local copies, waits for them, and re-layouts, local(): half_rotated = jnp.stack(half_blocks)  4.9 us
    another operation x6, loops' own time, local(): lax.cond(where_index < sectors_here, from_own, from_next, rows_here)  4.28 us
  transfers between devices with their start and end apart: 2, of which 2 were waited for; matrix products, arithmetic and copies ran while one was open for 15% of the time, Pallas kernels for 0%

commit v1 on v0

v1 whole, which is shorter than its diff:
```python
import functools

import jax
import jax.numpy as jnp
from jax import lax
from jax.experimental import pallas as pl
from jax.experimental.pallas import tpu as pltpu
from jax.sharding import PartitionSpec as P

ANY = pl.BlockSpec(memory_space=pl.ANY)
SCALAR = pl.BlockSpec(memory_space=pltpu.SMEM)
WHOLE = pl.BlockSpec(memory_space=pltpu.VMEM)
OWN, OTHER = -1, -2
KERNEL_BYTES = 14 * 1024 * 1024
LONG = pl.CostEstimate(flops=10**12, bytes_accessed=0, transcendentals=0)
BRIEF = pl.CostEstimate(flops=0, bytes_accessed=0, transcendentals=0)


def in_hbm(array):
    return pltpu.with_memory_space_constraint(array, pltpu.HBM)


def in_vmem(array):
    return pltpu.with_memory_space_constraint(array, pltpu.VMEM)


def first_column(start, columns, place):
    if start == OWN:
        return pl.multiple_of(place[3] + (place[0] // 2) * columns, columns)
    if start == OTHER:
        return pl.multiple_of(place[3] + (1 - place[0] // 2) * columns, columns)
    return start


def previous(block):
    count = lax.axis_size("sec")
    return lax.ppermute(block, "sec", [((i + 1) % count, i) for i in range(count)])


def swapped(block, distance):
    return lax.ppermute(block, "slab", [(i, i ^ distance) for i in range(lax.axis_size("slab"))])


def send_copies(parts, place, basis, sent, sems):
    width = basis.shape[1] // lax.axis_size("slab")
    here = place[0]
    copies = []
    for at, spans in enumerate(parts):
        column = 0
        for start, columns in spans:
            start = first_column(start, columns, place)
            for block in range(basis.shape[1] // width // 2):
                row = pl.multiple_of((2 * block + here % 2) * width, width)
                copies.append(
                    pltpu.make_async_copy(
                        basis.at[:, pl.ds(row, width), pl.ds(start, columns)],
                        sent[at].at[:, pl.ds(block * width, width), pl.ds(column, columns)],
                        sems.at[len(copies)],
                    )
                )
            column += columns
    return copies


def half_products(distances, place, basis, fermion, pieces, ready):
    flavours, sectors, _, width = fermion.shape
    for sector in range(sectors):
        ready(sector)
        right = jnp.concatenate([fermion[flavour, sector] for flavour in range(flavours)], axis=1)
        for slot, distance in enumerate(distances):
            column = pl.multiple_of((place[0] ^ distance) * width, width)
            block = lax.dot_general(
                basis[sector, :, pl.ds(column, width)],
                right,
                (((0,), (0,)), ((), ())),
                preferred_element_type=jnp.float32,
            ).astype(jnp.bfloat16)
            for flavour in range(flavours):
                pieces[slot][sector, flavour] = block[:, flavour * width : (flavour + 1) * width]


def first_kernel(parts, distances, place, basis, fermion, *refs):
    sent, refs = refs[: len(parts)], refs[len(parts) :]
    *pieces, left, right, sems, left_sems, right_sems = refs
    flavours, sectors, _, width = fermion.shape
    sent_copies = send_copies(parts, place, basis, sent, sems)
    for copy in sent_copies:
        copy.start()

    @pl.when(place[1] == 0)
    def _():
        copies = []
        for sector in range(sectors):
            copies.append([pltpu.make_async_copy(basis.at[sector], left.at[sector], left_sems.at[sector])])
            for flavour in range(flavours):
                copies[-1].append(
                    pltpu.make_async_copy(
                        fermion.at[flavour, sector], right.at[flavour, sector], right_sems.at[sector, flavour]
                    )
                )
        for group in copies:
            for copy in group:
                copy.start()

        def ready(sector):
            for copy in copies[sector]:
                copy.wait()

        half_products(distances, place, left, right, pieces, ready)

    for copy in sent_copies:
        copy.wait()


def first_call(place, basis, fermion, parts, distances):
    flavours, sectors, depth, width = fermion.shape
    copies = sum(len(spans) for spans in parts) * lax.axis_size("slab") // 2
    return pl.pallas_call(
        functools.partial(first_kernel, parts, distances),
        out_shape=[
            pltpu.VMEM((sectors, depth // 2, sum(columns for _, columns in spans)), jnp.bfloat16) for spans in parts
        ]
        + [pltpu.VMEM((sectors, flavours, width, width), jnp.bfloat16)] * len(distances),
        in_specs=[SCALAR, ANY, ANY],
        out_specs=[WHOLE] * (len(parts) + len(distances)),
        scratch_shapes=[
            pltpu.VMEM((sectors, depth, depth), jnp.bfloat16),
            pltpu.VMEM((flavours, sectors, depth, width), jnp.bfloat16),
            pltpu.SemaphoreType.DMA((copies,)),
            pltpu.SemaphoreType.DMA((sectors,)),
            pltpu.SemaphoreType.DMA((sectors, flavours)),
        ],
        compiler_params=pltpu.CompilerParams(vmem_limit_bytes=KERNEL_BYTES),
        cost_estimate=BRIEF,
        name="first",
    )(place, in_hbm(basis), in_hbm(fermion))


def other_half_kernel(distances, place, basis, fermion, *refs):
    @pl.when(place[1] != 0)
    def _():
        half_products(distances, place, basis, fermion, refs[len(distances) :], lambda sector: None)


def half_blocks(place, basis, fermion, distances, earlier):
    flavours, sectors, depth, width = fermion.shape
    return pl.pallas_call(
        functools.partial(other_half_kernel, distances),
        out_shape=[pltpu.VMEM((sectors, flavours, width, width), jnp.bfloat16)] * len(distances),
        in_specs=[SCALAR] + [WHOLE] * (2 + len(earlier)),
        out_specs=[WHOLE] * len(distances),
        input_output_aliases={3 + i: i for i in range(len(earlier))},
        compiler_params=pltpu.CompilerParams(vmem_limit_bytes=KERNEL_BYTES),
        cost_estimate=BRIEF,
        name="half",
    )(place, *map(in_vmem, (basis, fermion, *earlier)))


def cut_kernel(cuts, given, *refs):
    for cut, piece in zip(cuts, refs[-len(cuts) :]):
        piece[...] = given[cut]


def cut_out(array, cuts, after=()):
    shapes = [jax.eval_shape(lambda x, cut=cut: x[cut], array).shape for cut in cuts]
    return pl.pallas_call(
        functools.partial(cut_kernel, cuts),
        out_shape=[pltpu.VMEM(shape, array.dtype) for shape in shapes],
        in_specs=[WHOLE] * (1 + len(after)),
        out_specs=[WHOLE] * len(cuts),
        compiler_params=pltpu.CompilerParams(vmem_limit_bytes=KERNEL_BYTES),
        cost_estimate=BRIEF,
        name="cut",
    )(in_vmem(array), *map(in_vmem, after))


def span_copies(spans, first, place, basis, right, sems):
    sectors = basis.shape[0]
    copies, at = [], 0
    for start, columns in spans:
        copies.append(
            pltpu.make_async_copy(
                basis.at[:, :, pl.ds(first_column(start, columns, place), columns)],
                right.at[pl.ds(0, sectors), :, pl.ds(at, columns)],
                sems.at[first + len(copies)],
            )
        )
        at += columns
    return copies


def next_copies(nexts, first, place, right, sems):
    here = place[0]
    sectors = right.shape[0] // 2
    width = right.shape[1] // lax.axis_size("slab")
    copies, at = [], 0
    for pair in nexts:
        columns = pair[0].shape[2]
        for side in range(2):
            for block in range(right.shape[1] // width // 2):
                row = pl.multiple_of((2 * block + (here + side) % 2) * width, width)
                copies.append(
                    pltpu.make_async_copy(
                        pair[side].at[:, pl.ds(block * width, width)],
                        right.at[pl.ds(sectors, sectors), pl.ds(row, width), pl.ds(at, columns)],
                        sems.at[first + len(copies)],
                    )
                )
        at += columns
    return copies


def multiply(spans, place, partner, left, right, stage, out, sems):
    flavours, sectors = stage.shape[:2]
    copies = []
    for sector in range(sectors):
        for flavour in range(flavours):
            index = (partner[sector, flavour] - place[1] + place[2]) % place[2]
            stage[flavour, sector] = jnp.dot(
                left[sector, flavour], right[index], preferred_element_type=jnp.float32
            ).astype(jnp.bfloat16)
            at = 0
            for start, columns in spans:
                copy = pltpu.make_async_copy(
                    stage.at[flavour, sector, :, pl.ds(at, columns)],
                    out.at[flavour, sector, :, pl.ds(first_column(start, columns, place), columns)],
                    sems.at[len(copies)],
                )
                copy.start()
                copies.append(copy)
                at += columns
    for copy in copies:
        copy.wait()


def early_kernel(spans, pairs, distances, place, partner, basis, *refs):
    halves, refs = refs[: len(distances)], refs[len(distances) :]
    nexts, refs = [refs[2 * i : 2 * i + 2] for i in range(pairs)], refs[2 * pairs :]
    out, left, right, stage, in_sems, out_sems = refs
    width = stage.shape[2]
    copies = span_copies(spans, 0, place, basis, right, in_sems)
    copies += next_copies(nexts, len(copies), place, right, in_sems)
    for half, (sector, many, distance) in zip(halves, distances):
        column = pl.multiple_of((place[0] ^ distance) * width, width)
        copies.append(
            pltpu.make_async_copy(
                half, left.at[pl.ds(sector, many), :, :, pl.ds(column, width)], in_sems.at[len(copies)]
            )
        )
    for copy in copies:
        copy.start()
    for copy in copies:
        copy.wait()
    multiply(spans, place, partner, left, right, stage, out, out_sems)


def late_kernel(spans, pairs, place, partner, basis, *refs):
    nexts, refs = [refs[2 * i : 2 * i + 2] for i in range(pairs)], refs[2 * pairs :]
    left, _, out, right, stage, in_sems, out_sems = refs
    copies = span_copies(spans, 0, place, basis, right, in_sems)
    copies += next_copies(nexts, len(copies), place, right, in_sems)
    for copy in copies:
        copy.start()
    for copy in copies:
        copy.wait()
    multiply(spans, place, partner, left, right, stage, out, out_sems)


def early_products(place, partner, basis, spans, nexts, halves, distances):
    sectors, depth, _ = basis.shape
    flavours, width = halves[0].shape[1:3]
    columns = sum(span[1] for span in spans)
    given = [in_vmem(array) for array in (basis, *halves, *(array for pair in nexts for array in pair))]
    copies = len(spans) + len(nexts) * lax.axis_size("slab") + len(halves)
    return pl.pallas_call(
        functools.partial(early_kernel, spans, len(nexts), distances),
        out_shape=[
            pltpu.HBM((flavours, sectors, width, depth), jnp.bfloat16),
            pltpu.VMEM((sectors, flavours, width, depth), jnp.bfloat16),
        ],
        in_specs=[SCALAR, SCALAR] + [WHOLE] * len(given),
        out_specs=[ANY, WHOLE],
        scratch_shapes=[
            pltpu.VMEM((2 * sectors, depth, columns), jnp.bfloat16),
            pltpu.VMEM((flavours, sectors, width, columns), jnp.bfloat16),
            pltpu.SemaphoreType.DMA((copies,)),
            pltpu.SemaphoreType.DMA((flavours * sectors * len(spans),)),
        ],
        compiler_params=pltpu.CompilerParams(vmem_limit_bytes=KERNEL_BYTES),
        cost_estimate=BRIEF,
        name="early",
    )(place, partner, *given)


def late_products(place, partner, basis, spans, nexts, out, left):
    sectors, flavours, width, depth = left.shape
    columns = sum(span[1] for span in spans)
    given = [in_vmem(array) for array in (basis, *(array for pair in nexts for array in pair), left)]
    return pl.pallas_call(
        functools.partial(late_kernel, spans, len(nexts)),
        out_shape=pltpu.HBM(out.shape, out.dtype),
        in_specs=[SCALAR, SCALAR] + [WHOLE] * len(given) + [ANY],
        out_specs=ANY,
        scratch_shapes=[
            pltpu.VMEM((2 * sectors, depth, columns), jnp.bfloat16),
            pltpu.VMEM((flavours, sectors, width, columns), jnp.bfloat16),
            pltpu.SemaphoreType.DMA((len(spans) + len(nexts) * lax.axis_size("slab"),)),
            pltpu.SemaphoreType.DMA((flavours * sectors * len(spans),)),
        ],
        input_output_aliases={2 + len(given): 0},
        compiler_params=pltpu.CompilerParams(vmem_limit_bytes=KERNEL_BYTES),
        cost_estimate=BRIEF,
        name="late",
    )(place, partner, *given, out)


def local(basis, fermion, partner):
    sectors, depth, _ = basis.shape
    every = sectors * lax.axis_size("sec")
    here = lax.axis_index("slab")
    unit = depth // 8
    place = jnp.stack([here, lax.axis_index("sec") * sectors, every, depth - 2 * unit]).astype(jnp.int32)
    spans, middle_spans, late_spans = ((0, 3 * unit), (OWN, unit)), ((3 * unit, 3 * unit),), ((OTHER, unit),)
    distances = (0, 1, 2, 3)
    first_part, last_part, *halves = first_call(place, basis, fermion, (spans, middle_spans), distances)
    first, last = previous(first_part), previous(last_part)
    near, mine, far2, far3 = half_blocks(place, basis, fermion, distances, halves)
    got2, got3, beside = swapped(far2, 2), swapped(far3, 3), swapped(mine, 1)
    *rest, own = cut_out(
        first,
        [(slice(None), slice(None), slice(at * unit, at * unit + unit)) for at in range(4)],
        (beside, got2),
    )
    shared = swapped(own, 2)
    nexts = [(piece, swapped(piece, 1)) for piece in (*rest, own)]
    blocks = [(0, sectors, distance) for distance in distances[::-1]]
    earlier = early_products(place, partner.T, basis, spans, nexts, [got3, got2, beside, near], blocks)
    shared, last, out = lax.optimization_barrier((shared, last, earlier[0]))
    nexts = [(last, swapped(last, 1)), (shared, swapped(shared, 1))]
    return late_products(place, partner.T, basis, middle_spans + late_spans, nexts, out, earlier[1])


def solution(mesh):
    placed = (P("sec", None, None), P(None, "sec", None, "slab"), P(None, "sec"))
    return jax.shard_map(
        local, mesh=mesh, in_specs=placed, out_specs=P(None, "sec", "slab", None), check_vma=False
    )
```

time: 123 us -> 64.9 us (0.53)
  the two profiles are of different devices: /device:TPU:0 before, /device:TPU:7 now
where the time goes in v1:
time: 64.9 us; the launch traced here: 64.8 us
  waiting for transfers between devices  37.5 us (58%)
  Pallas kernels  15.2 us (23%)
  starting transfers between devices  12 us (18%)
    ppermute x10, waiting for transfers between devices, swapped(): lax.ppermute(block, 'slab', [(i, i ^ distance) for i in range(lax.axis_si...  37.5 us
    ppermute x10, starting transfers between devices, swapped(): lax.ppermute(block, 'slab', [(i, i ^ distance) for i in range(lax.axis_si...  6.11 us
    ppermute x2, starting transfers between devices, previous(): lax.ppermute(block, 'sec', [((i + 1) % count, i) for i in range(count)])  5.9 us
    pallas_call x1, Pallas kernels, early_products(): pl.pallas_call(functools.partial(early_kernel, spans, len(nexts), distanc...  4.6 us
    pallas_call x1, Pallas kernels, half_blocks(): pl.pallas_call(functools.partial(other_half_kernel, distances), out_shape...  4.1 us
    pallas_call x1, Pallas kernels, late_products(): pl.pallas_call(functools.partial(late_kernel, spans, len(nexts)), out_sha...  3.91 us
    pallas_call x1, Pallas kernels, first_call(): pl.pallas_call(functools.partial(first_kernel, parts, distances), out_sha...  2.4 us
  transfers between devices with their start and end apart: 12, of which 6 were waited for; matrix products, arithmetic and copies ran while one was open for 0% of the time, Pallas kernels for 14%

profile of v1, /device:TPU:7, one launch (start us, length us, event | category | flops | bytes accessed | tf_op | source)
XLA Modules:
  0.0 64.8 jit_solution(27646046331360464)
XLA Ops:
  0.0 0.1 pad_add_fusion.place
  0.1 0.0 copy-start
  0.1 0.0 copy-start.1
  0.1 2.4 %first.1 = (bf16[2,512,512]{2,1,0:T(8,128)(2,1)S(1)}, bf16[2,512,384]{2,1,0:T(8,128)(2,1)S(1)}, bf16[2,3,256,256]{3,2,1,0:T(8,128)(2,1)S(1)}, bf16[2,3,256,256]{...) custom-call(s32[4]{0:T(128)S(1)} %pad_add_fusion.place, ...), custom_call_target="tpu_custom_call" | custom-call | tf_op jit(solution)/shard_map/first/pallas_call | solution.py:118
  2.5 5.9 %collective-permute-start = (bf16[2,512,512]{2,1,0:T(8,128)(2,1)S(1)}, bf16[2,512,512]{2,1,0:T(8,128)(2,1)S(1)}, u32[]{:S(2)}, u32[]{:S(2)}) collective-permute-start(bf16[2,512,512]{2,1,0:T(8,128)(2,1)S(1)} %get-tuple-element.24), channel_id=1, source_target_pairs={{4,0},{8,4},{12,8},{16,12},{20,16},{24,20},{28,24},{0,28},{5,1},{9... | collective-permute-start | bytes 3145736 | tf_op jit(solution)/shard_map/ppermute | solution.py:37
  8.4 0.0 copy-done
  8.4 0.0 copy-done.1
  8.4 0.0 copy-start.2
  8.4 4.1 %half.1 = (bf16[2,3,256,256]{3,2,1,0:T(8,128)(2,1)S(1)}, bf16[2,3,256,256]{3,2,1,0:T(8,128)(2,1)S(1)}, bf16[2,3,256,256]{3,2,1,0:T(8,128)(2,1)S(1)}, bf16[2,3,256,256]{3,2,1,0:T(8,128)(2,1)S(1)}) custom-call(s32[4]{0:T(128)S(1)} %pad_add_fusion.place, ...), custom_call_target="tpu_custom_call", output_to_operand_aliasing={{0}: (3, {}), {1}: (4, {}), {2}: (5, {}), {3}: (6, {})} | custom-call | tf_op jit(solution)/shard_map/half/pallas_call | solution.py:147
  12.5 1.0 %collective-permute-start.1 = (bf16[2,3,256,256]{3,2,1,0:T(8,128)(2,1)S(1)}, bf16[2,3,256,256]{3,2,1,0:T(8,128)(2,1)S(1)}, u32[]{:S(2)}, u32[]{:S(2)}) collective-permute-start(bf16[2,3,256,256]{3,2,1,0:T(8,128)(2,1)S(1)} %get-tuple-element.29), channel_id=1, source_target_pairs={{0,1},{1,0},{2,3},{3,2},{4,5},{5,4},{6,7},{7,6},{8,9},{9,8},{10,11... | collective-permute-start | bytes 2359304 | tf_op jit(solution)/shard_map/ppermute | solution.py:41
  13.5 0.0 collective-permute-start.2
  13.5 1.7 %collective-permute-start.5 = (bf16[2,3,256,256]{3,2,1,0:T(8,128)(2,1)S(1)}, bf16[2,3,256,256]{3,2,1,0:T(8,128)(2,1)S(1)}, u32[]{:S(2)}, u32[]{:S(2)}) collective-permute-start(bf16[2,3,256,256]{3,2,1,0:T(8,128)(2,1)S(1)} %get-tuple-element.33), channel_id=1, source_target_pairs={{0,3},{1,2},{2,1},{3,0},{4,7},{5,6},{6,5},{7,4},{8,11},{9,10},{10,... | collective-permute-start | bytes 2359304 | tf_op jit(solution)/shard_map/ppermute | solution.py:41
  15.2 0.0 collective-permute-start.4
  15.2 0.2 collective-permute-done.1.refs_0_.refs_2_
  15.4 17.2 %collective-permute-done.2.refs_1_ = bf16[2,3,256,256]{3,2,1,0:T(8,128)(2,1)S(1)} collective-permute-done((bf16[2,3,256,256]{3,2,1,0:T(8,128)(2,1)S(1)}, bf16[2,3,256,256]{3,2,1,0:T(8,128)(2,1)S(1)}, u32[]{:S(2)}, u32[]{:S(2)}) %collective-permute-start.2) | collective-permute-done | bytes 786464 | tf_op jit(solution)/shard_map/ppermute | solution.py:41
  32.6 0.0 collective-permute-done.given
  32.6 0.2 cut.1
  32.8 1.4 %collective-permute-start.6 = (bf16[2,512,128]{2,1,0:T(8,128)(2,1)S(1)}, bf16[2,512,128]{2,1,0:T(8,128)(2,1)S(1)}, u32[]{:S(2)}, u32[]{:S(2)}) collective-permute-start(bf16[2,512,128]{2,1,0:T(8,128)(2,1)S(1)} %get-tuple-element.35.refs_4_), channel_id=1, source_target_pairs={{0,1},{1,0},{2,3},{3,2},{4,5},{5,4},{6,7},{7,6},{8,9},{9,8},{10,11... | collective-permute-start | bytes 786440 | tf_op jit(solution)/shard_map/ppermute | solution.py:41
  34.2 0.1 collective-permute-start.7
  34.3 0.4 collective-permute-start.8
  34.7 14.9 %collective-permute-done.5.refs_0_ = bf16[2,3,256,256]{3,2,1,0:T(8,128)(2,1)S(1)} collective-permute-done((bf16[2,3,256,256]{3,2,1,0:T(8,128)(2,1)S(1)}, bf16[2,3,256,256]{3,2,1,0:T(8,128)(2,1)S(1)}, u32[]{:S(2)}, u32[]{:S(2)}) %collective-permute-start.5) | collective-permute-done | bytes 786464 | tf_op jit(solution)/shard_map/ppermute | solution.py:41
  49.6 0.2 collective-permute-start.9
  49.9 0.0 collective-permute-done.6.refs_5_
  49.9 0.2 collective-permute-start.3
  50.1 0.0 collective-permute-done.7.refs_7_
  50.1 0.0 collective-permute-done.8.refs_9_
  50.1 1.1 %collective-permute-done.9.refs_11_ = bf16[2,512,128]{2,1,0:T(8,128)(2,1)S(1)} collective-permute-done((bf16[2,512,128]{2,1,0:T(8,128)(2,1)S(1)}, bf16[2,512,128]{2,1,0:T(8,128)(2,1)S(1)}, u32[]{:S(2)}, u32[]{:S(2)}) %collective-permute-start.9) | collective-permute-done | bytes 262176 | tf_op jit(solution)/shard_map/ppermute | solution.py:41
  51.2 0.0 copy-done.2
  51.2 4.6 %early.1 = (bf16[3,2,256,1024]{3,2,1,0:T(8,128)(2,1)}, bf16[2,3,256,1024]{3,2,1,0:T(8,128)(2,1)S(1)}) custom-call(s32[4]{0:T(128)S(1)} %pad_add_fusion.place, s32[2,3]{1,0:T(2,128)S(1)} %bitcast.3, bf16[2,1024,1024]{2,1,0:T(8,128)(2,1)S(1)} %copy-done, bf16[2,3,256,256]{3,2,1,0:T(8,128)(2,1)S(1)} %collective-permute-done.5.refs_0_, ...), custom_call_target="tpu_custom_call" | custom-call | tf_op jit(solution)/shard_map/early/pallas_call | solution.py:275
  55.8 0.0 collective-permute-done.4.refs_0_
  55.8 1.7 %collective-permute-done.3.refs_2_ = bf16[2,512,128]{2,1,0:T(8,128)(2,1)S(1)} collective-permute-done((bf16[2,512,128]{2,1,0:T(8,128)(2,1)S(1)}, bf16[2,512,128]{2,1,0:T(8,128)(2,1)S(1)}, u32[]{:S(2)}, u32[]{:S(2)}) %collective-permute-start.3) | collective-permute-done | bytes 262176 | tf_op jit(solution)/shard_map/ppermute | solution.py:41
  57.5 1.1 %collective-permute-start.10 = (bf16[2,512,384]{2,1,0:T(8,128)(2,1)S(1)}, bf16[2,512,384]{2,1,0:T(8,128)(2,1)S(1)}, u32[]{:S(2)}, u32[]{:S(2)}) collective-permute-start(bf16[2,512,384]{2,1,0:T(8,128)(2,1)S(1)} %collective-permute-done.4.refs_0_), channel_id=1, source_target_pairs={{0,1},{1,0},{2,3},{3,2},{4,5},{5,4},{6,7},{7,6},{8,9},{9,8},{10,11... | collective-permute-start | bytes 2359304 | tf_op jit(solution)/shard_map/ppermute | solution.py:41
  58.6 0.0 collective-permute-start.11
  58.6 2.3 %collective-permute-done.11.refs_3_ = bf16[2,512,128]{2,1,0:T(8,128)(2,1)S(1)} collective-permute-done((bf16[2,512,128]{2,1,0:T(8,128)(2,1)S(1)}, bf16[2,512,128]{2,1,0:T(8,128)(2,1)S(1)}, u32[]{:S(2)}, u32[]{:S(2)}) %collective-permute-start.11) | collective-permute-done | bytes 262176 | tf_op jit(solution)/shard_map/ppermute | solution.py:41
  60.9 0.0 collective-permute-done.10.refs_1_
  60.9 3.9 %late.1 = bf16[3,2,256,1024]{3,2,1,0:T(8,128)(2,1)} custom-call(s32[4]{0:T(128)S(1)} %pad_add_fusion.place, s32[2,3]{1,0:T(2,128)S(1)} %bitcast.4, bf16[2,1024,1024]{2,1,0:T(8,128)(2,1)S(1)} %copy-done, bf16[2,512,384]{2,1,0:T(8,128)(2,1)S(1)} %collective-permute-done.4.refs_0_, ...), custom_call_target="tpu_custom_call", output_to_operand_aliasing={{}: (8, {})} | custom-call | tf_op jit(solution)/shard_map/late/pallas_call | solution.py:299
Async XLA Ops:
  0.1 8.3 %copy-start = (bf16[2,1024,1024]{2,1,0:T(8,128)(2,1)S(1)}, bf16[2,1024,1024]{2,1,0:T(8,128)(2,1)}, u32[]{:S(2)}) copy-start(bf16[2,1024,1024]{2,1,0:T(8,128)(2,1)} %basis.7) | copy-start | bytes 12582916
  0.1 8.3 %copy-start.1 = (bf16[3,2,1024,256]{3,2,1,0:T(8,128)(2,1)S(1)}, bf16[3,2,1024,256]{3,2,1,0:T(8,128)(2,1)}, u32[]{:S(2)}) copy-start(bf16[3,2,1024,256]{3,2,1,0:T(8,128)(2,1)} %fermion.3) | copy-start | bytes 9437188
  2.5 30.1 %collective-permute-start = (bf16[2,512,512]{2,1,0:T(8,128)(2,1)S(1)}, bf16[2,512,512]{2,1,0:T(8,128)(2,1)S(1)}, u32[]{:S(2)}, u32[]{:S(2)}) collective-permute-start(bf16[2,512,512]{2,1,0:T(8,128)(2,1)S(1)} %get-tuple-element.24), channel_id=1, source_target_pairs={{4,0},{8,4},{12,8},{16,12},{20,16},{24,20},{28,24},{0,28},{5,1},{9... | collective-permute-start | bytes 3145736 | tf_op jit(solution)/shard_map/ppermute | solution.py:37
  8.4 42.8 %copy-start.2 = (s32[3,2]{0,1:T(2,128)S(1)}, s32[3,2]{0,1:T(2,128)}, u32[]{:S(2)}) copy-start(s32[3,2]{0,1:T(2,128)} %param.5) | copy-start | bytes 76
  12.5 2.9 %collective-permute-start.1 = (bf16[2,3,256,256]{3,2,1,0:T(8,128)(2,1)S(1)}, bf16[2,3,256,256]{3,2,1,0:T(8,128)(2,1)S(1)}, u32[]{:S(2)}, u32[]{:S(2)}) collective-permute-start(bf16[2,3,256,256]{3,2,1,0:T(8,128)(2,1)S(1)} %get-tuple-element.29), channel_id=1, source_target_pairs={{0,1},{1,0},{2,3},{3,2},{4,5},{5,4},{6,7},{7,6},{8,9},{9,8},{10,11... | collective-permute-start | bytes 2359304 | tf_op jit(solution)/shard_map/ppermute | solution.py:41
  13.5 19.1 %collective-permute-start.2 = (bf16[2,3,256,256]{3,2,1,0:T(8,128)(2,1)S(1)}, bf16[2,3,256,256]{3,2,1,0:T(8,128)(2,1)S(1)}, u32[]{:S(2)}, u32[]{:S(2)}) collective-permute-start(bf16[2,3,256,256]{3,2,1,0:T(8,128)(2,1)S(1)} %get-tuple-element.30), channel_id=1, source_target_pairs={{0,2},{1,3},{2,0},{3,1},{4,6},{5,7},{6,4},{7,5},{8,10},{9,11},{10,... | collective-permute-start | bytes 2359304 | tf_op jit(solution)/shard_map/ppermute | solution.py:41
  13.5 36.1 %collective-permute-start.5 = (bf16[2,3,256,256]{3,2,1,0:T(8,128)(2,1)S(1)}, bf16[2,3,256,256]{3,2,1,0:T(8,128)(2,1)S(1)}, u32[]{:S(2)}, u32[]{:S(2)}) collective-permute-start(bf16[2,3,256,256]{3,2,1,0:T(8,128)(2,1)S(1)} %get-tuple-element.33), channel_id=1, source_target_pairs={{0,3},{1,2},{2,1},{3,0},{4,7},{5,6},{6,5},{7,4},{8,11},{9,10},{10,... | collective-permute-start | bytes 2359304 | tf_op jit(solution)/shard_map/ppermute | solution.py:41
  15.2 40.6 %collective-permute-start.4 = (bf16[2,512,384]{2,1,0:T(8,128)(2,1)S(1)}, bf16[2,512,384]{2,1,0:T(8,128)(2,1)S(1)}, u32[]{:S(2)}, u32[]{:S(2)}) collective-permute-start(bf16[2,512,384]{2,1,0:T(8,128)(2,1)S(1)} %get-tuple-element.32), channel_id=1, source_target_pairs={{4,0},{8,4},{12,8},{16,12},{20,16},{24,20},{28,24},{0,28},{5,1},{9... | collective-permute-start | bytes 2359304 | tf_op jit(solution)/shard_map/ppermute | solution.py:37
  32.8 17.1 %collective-permute-start.6 = (bf16[2,512,128]{2,1,0:T(8,128)(2,1)S(1)}, bf16[2,512,128]{2,1,0:T(8,128)(2,1)S(1)}, u32[]{:S(2)}, u32[]{:S(2)}) collective-permute-start(bf16[2,512,128]{2,1,0:T(8,128)(2,1)S(1)} %get-tuple-element.35.refs_4_), channel_id=1, source_target_pairs={{0,1},{1,0},{2,3},{3,2},{4,5},{5,4},{6,7},{7,6},{8,9},{9,8},{10,11... | collective-permute-start | bytes 786440 | tf_op jit(solution)/shard_map/ppermute | solution.py:41
  34.2 15.9 %collective-permute-start.7 = (bf16[2,512,128]{2,1,0:T(8,128)(2,1)S(1)}, bf16[2,512,128]{2,1,0:T(8,128)(2,1)S(1)}, u32[]{:S(2)}, u32[]{:S(2)}) collective-permute-start(bf16[2,512,128]{2,1,0:T(8,128)(2,1)S(1)} %get-tuple-element.36.refs_6_), channel_id=1, source_target_pairs={{0,1},{1,0},{2,3},{3,2},{4,5},{5,4},{6,7},{7,6},{8,9},{9,8},{10,11... | collective-permute-start | bytes 786440 | tf_op jit(solution)/shard_map/ppermute | solution.py:41
  34.3 15.8 %collective-permute-start.8 = (bf16[2,512,128]{2,1,0:T(8,128)(2,1)S(1)}, bf16[2,512,128]{2,1,0:T(8,128)(2,1)S(1)}, u32[]{:S(2)}, u32[]{:S(2)}) collective-permute-start(bf16[2,512,128]{2,1,0:T(8,128)(2,1)S(1)} %get-tuple-element.37.refs_8_), channel_id=1, source_target_pairs={{0,1},{1,0},{2,3},{3,2},{4,5},{5,4},{6,7},{7,6},{8,9},{9,8},{10,11... | collective-permute-start | bytes 786440 | tf_op jit(solution)/shard_map/ppermute | solution.py:41
  49.6 1.5 %collective-permute-start.9 = (bf16[2,512,128]{2,1,0:T(8,128)(2,1)S(1)}, bf16[2,512,128]{2,1,0:T(8,128)(2,1)S(1)}, u32[]{:S(2)}, u32[]{:S(2)}) collective-permute-start(bf16[2,512,128]{2,1,0:T(8,128)(2,1)S(1)} %get-tuple-element.31.refs_10_), channel_id=1, source_target_pairs={{0,1},{1,0},{2,3},{3,2},{4,5},{5,4},{6,7},{7,6},{8,9},{9,8},{10,11... | collective-permute-start | bytes 786440 | tf_op jit(solution)/shard_map/ppermute | solution.py:41
  49.9 7.6 %collective-permute-start.3 = (bf16[2,512,128]{2,1,0:T(8,128)(2,1)S(1)}, bf16[2,512,128]{2,1,0:T(8,128)(2,1)S(1)}, u32[]{:S(2)}, u32[]{:S(2)}) collective-permute-start(bf16[2,512,128]{2,1,0:T(8,128)(2,1)S(1)} %get-tuple-element.31.refs_10_), channel_id=1, source_target_pairs={{0,2},{1,3},{2,0},{3,1},{4,6},{5,7},{6,4},{7,5},{8,10},{9,11},{10,... | collective-permute-start | bytes 786440 | tf_op jit(solution)/shard_map/ppermute | solution.py:41
  57.5 3.4 %collective-permute-start.10 = (bf16[2,512,384]{2,1,0:T(8,128)(2,1)S(1)}, bf16[2,512,384]{2,1,0:T(8,128)(2,1)S(1)}, u32[]{:S(2)}, u32[]{:S(2)}) collective-permute-start(bf16[2,512,384]{2,1,0:T(8,128)(2,1)S(1)} %collective-permute-done.4.refs_0_), channel_id=1, source_target_pairs={{0,1},{1,0},{2,3},{3,2},{4,5},{5,4},{6,7},{7,6},{8,9},{9,8},{10,11... | collective-permute-start | bytes 2359304 | tf_op jit(solution)/shard_map/ppermute | solution.py:41
  58.6 2.3 %collective-permute-start.11 = (bf16[2,512,128]{2,1,0:T(8,128)(2,1)S(1)}, bf16[2,512,128]{2,1,0:T(8,128)(2,1)S(1)}, u32[]{:S(2)}, u32[]{:S(2)}) collective-permute-start(bf16[2,512,128]{2,1,0:T(8,128)(2,1)S(1)} %collective-permute-done.3.refs_2_), channel_id=1, source_target_pairs={{0,1},{1,0},{2,3},{3,2},{4,5},{5,4},{6,7},{7,6},{8,9},{9,8},{10,11... | collective-permute-start | bytes 786440 | tf_op jit(solution)/shard_map/ppermute | solution.py:41

commit v2 on v0

v2 whole, which is shorter than its diff:
```python
import functools

import jax
import jax.numpy as jnp
from jax import lax
from jax.experimental import pallas as pl
from jax.experimental.pallas import tpu as pltpu
from jax.sharding import PartitionSpec as P

ANY = pl.BlockSpec(memory_space=pl.ANY)
SCALAR = pl.BlockSpec(memory_space=pltpu.SMEM)
WHOLE = pl.BlockSpec(memory_space=pltpu.VMEM)
OWN, OTHER = -1, -2
KERNEL_BYTES = 16 * 1024 * 1024
BRIEF = pl.CostEstimate(flops=0, bytes_accessed=0, transcendentals=0)


def in_hbm(array):
    return pltpu.with_memory_space_constraint(array, pltpu.HBM)


def in_vmem(array):
    return pltpu.with_memory_space_constraint(array, pltpu.VMEM)


def kernel_call(body, name, given, specs, shapes, out_specs, scratch=(), aliases={}, cost=BRIEF):
    return pl.pallas_call(
        body,
        out_shape=shapes,
        in_specs=specs,
        out_specs=out_specs,
        scratch_shapes=list(scratch),
        input_output_aliases=aliases,
        compiler_params=pltpu.CompilerParams(vmem_limit_bytes=KERNEL_BYTES),
        cost_estimate=cost,
        name=name,
    )(*given)


def first_column(unit, place, width):
    if unit == OWN:
        return pl.multiple_of(place[3] + (place[0] // 2) * width, width)
    if unit == OTHER:
        return pl.multiple_of(place[3] + (1 - place[0] // 2) * width, width)
    return unit * width


def run(copies):
    for copy in copies:
        copy.start()
    for copy in copies:
        copy.wait()


def previous(block):
    count = lax.axis_size("sec")
    return lax.ppermute(block, "sec", [((i + 1) % count, i) for i in range(count)])


def swapped(block, distance):
    return lax.ppermute(block, "slab", [(i, i ^ distance) for i in range(lax.axis_size("slab"))])


def part_kernel(lists, unit, distances, place, basis, fermion, *refs):
    sent, refs = refs[: len(lists)], refs[len(lists) :]
    *pieces, left, right, sems, half_sems = refs
    slabs = lax.axis_size("slab")
    rows = basis.shape[1] // slabs
    copies = []
    for array, blocks in zip(sent, lists):
        for at, (sector, count, start) in enumerate(blocks):
            for slab in range(slabs // 2):
                row = pl.multiple_of((2 * slab + place[0] % 2) * rows, rows)
                copies.append(
                    pltpu.make_async_copy(
                        basis.at[sector, pl.ds(row, rows), pl.ds(first_column(start, place, unit), count * unit)],
                        array.at[at, pl.ds(slab * rows, rows)],
                        sems.at[len(copies)],
                    )
                )
    for copy in copies:
        copy.start()

    @pl.when(place[1] == 0)
    def _():
        run(
            [
                pltpu.make_async_copy(basis.at[pl.ds(0, 1)], left, half_sems.at[0]),
                pltpu.make_async_copy(fermion.at[:, pl.ds(0, 1)], right, half_sems.at[1]),
            ]
        )
        half_products(0, distances, place, left, right, pieces)

    for copy in copies:
        copy.wait()


def basis_parts(place, basis, fermion, lists, unit, distances):
    flavours, sectors, depth, width = fermion.shape
    copies = sum(len(blocks) for blocks in lists) * lax.axis_size("slab") // 2
    shapes = [pltpu.VMEM((len(blocks), depth // 2, blocks[0][1] * unit), jnp.bfloat16) for blocks in lists]
    shapes += [pltpu.VMEM((sectors, flavours, width, width), jnp.bfloat16)] * len(distances)
    return kernel_call(
        functools.partial(part_kernel, lists, unit, distances),
        "part",
        [place, in_hbm(basis), in_hbm(fermion)],
        [SCALAR, ANY, ANY],
        shapes,
        [WHOLE] * len(shapes),
        [
            pltpu.VMEM((1, depth, depth), jnp.bfloat16),
            pltpu.VMEM((flavours, 1, depth, width), jnp.bfloat16),
            pltpu.SemaphoreType.DMA((copies,)),
            pltpu.SemaphoreType.DMA((2,)),
        ],
    )


def half_products(sector, distances, place, basis, fermion, pieces):
    flavours, _, _, width = fermion.shape
    right = jnp.concatenate([fermion[flavour, sector] for flavour in range(flavours)], axis=1)
    for slot, distance in enumerate(distances):
        column = pl.multiple_of((place[0] ^ distance) * width, width)
        block = lax.dot_general(
            basis[sector, :, pl.ds(column, width)],
            right,
            (((0,), (0,)), ((), ())),
            preferred_element_type=jnp.float32,
        ).astype(jnp.bfloat16)
        for flavour in range(flavours):
            pieces[slot][sector, flavour] = block[:, flavour * width : (flavour + 1) * width]


def half_kernel(distances, place, basis, fermion, *refs):
    pieces = refs[len(distances) :]

    @pl.when(place[1] != 0)
    def _():
        half_products(0, distances, place, basis, fermion, pieces)

    for sector in range(1, basis.shape[0]):
        half_products(sector, distances, place, basis, fermion, pieces)


def half_blocks(place, basis, fermion, distances, earlier):
    return kernel_call(
        functools.partial(half_kernel, distances),
        "half",
        [place, in_vmem(basis), in_vmem(fermion), *map(in_vmem, earlier)],
        [SCALAR] + [WHOLE] * (2 + len(earlier)),
        [pltpu.VMEM(piece.shape, piece.dtype) for piece in earlier],
        [WHOLE] * len(distances),
        aliases={3 + at: at for at in range(len(earlier))},
    )


def cut_kernel(cuts, given, *refs):
    for cut, piece in zip(cuts, refs[-len(cuts) :]):
        piece[...] = given[cut]


def cut_out(array, cuts, after=()):
    shapes = [jax.eval_shape(lambda x, cut=cut: x[cut], array).shape for cut in cuts]
    return kernel_call(
        functools.partial(cut_kernel, cuts),
        "cut",
        [in_vmem(array), *map(in_vmem, after)],
        [WHOLE] * (1 + len(after)),
        [pltpu.VMEM(shape, array.dtype) for shape in shapes],
        [WHOLE] * len(cuts),
    )


def own_copies(units, unit, place, basis, right, sems, first):
    sectors, depth, _ = basis.shape
    slabs = lax.axis_size("slab")
    rows = depth // slabs
    copies, at = [], 0
    for start, count in units:
        for slab in range(slabs):
            to = ((slab % 2) * (slabs // 2) + slab // 2) * rows
            copies.append(
                pltpu.make_async_copy(
                    basis.at[:, pl.ds(slab * rows, rows), pl.ds(first_column(start, place, unit), count * unit)],
                    right.at[pl.ds(0, sectors), pl.ds(to, rows), pl.ds(at, count * unit)],
                    sems.at[first + len(copies)],
                )
            )
        at += count * unit
    return copies


def next_copies(nexts, place, pairs, right, sems, first):
    sectors, depth = right.shape[0] // 2, right.shape[1]
    copies = []
    for pair, holds in zip(pairs, nexts):
        for index, many, sector, column in holds:
            for side in range(2):
                to = pl.multiple_of(((place[0] + side) % 2) * (depth // 2), depth // 2)
                copies.append(
                    pltpu.make_async_copy(
                        pair[side].at[pl.ds(index, many)],
                        right.at[
                            pl.ds(sectors + sector, many), pl.ds(to, depth // 2), pl.ds(column, pair[side].shape[2])
                        ],
                        sems.at[first + len(copies)],
                    )
                )
    return copies


def half_copy(half, distance, place, left, sem):
    slabs = lax.axis_size("slab")
    width = half.shape[3]
    slab = place[0] ^ distance
    column = pl.multiple_of(((slab % 2) * (slabs // 2) + slab // 2) * width, width)
    return pltpu.make_async_copy(half, left.at[:, :, :, pl.ds(column, width)], sem)


def gather_kernel(early_units, late_units, nexts, unit, distances, cut, place, basis, *refs):
    halves, refs = refs[: len(distances)], refs[len(distances) :]
    pairs, refs = [refs[2 * i : 2 * i + 2] for i in range(len(nexts))], refs[2 * len(nexts) :]
    left, early_right, late_right, sent, sems = refs
    copies = own_copies(early_units, unit, place, basis, early_right, sems, 0)
    copies += next_copies(nexts, place, pairs, early_right, sems, len(copies))
    copies += own_copies(late_units, unit, place, basis, late_right, sems, len(copies))
    for half, distance in zip(halves, distances):
        copies.append(half_copy(half, distance, place, left, sems.at[len(copies)]))
    copies.append(pltpu.make_async_copy(pairs[-1][0].at[cut], sent, sems.at[len(copies)]))
    run(copies)


def gather(place, basis, early_units, late_units, nexts, unit, pairs, halves, distances, cut):
    sectors, depth, _ = basis.shape
    flavours, width = halves[0].shape[1:3]
    given = [in_vmem(array) for array in (basis, *halves, *(array for pair in pairs for array in pair))]
    early_columns, late_columns = (sum(count for _, count in units) * unit for units in (early_units, late_units))
    copies = (len(early_units) + len(late_units)) * (depth // width) + 2 * sum(len(holds) for holds in nexts)
    last = pairs[-1][0]
    return kernel_call(
        functools.partial(gather_kernel, early_units, late_units, nexts, unit, distances, cut),
        "gather",
        [place, *given],
        [SCALAR] + [WHOLE] * len(given),
        [
            pltpu.VMEM((sectors, flavours, width, depth), jnp.bfloat16),
            pltpu.VMEM((2 * sectors, depth, early_columns), jnp.bfloat16),
            pltpu.VMEM((2 * sectors, depth, late_columns), jnp.bfloat16),
            pltpu.VMEM((cut.size, *last.shape[1:]), jnp.bfloat16),
        ],
        [WHOLE] * 4,
        [pltpu.SemaphoreType.DMA((copies + len(halves) + 1,))],
    )


def product(place, partner, sector, flavour, left, right):
    index = (partner[sector, flavour] - place[1] + place[2]) % place[2]
    return jnp.dot(left[sector, flavour], right[index], preferred_element_type=jnp.float32).astype(jnp.bfloat16)


def early_kernel(distance, place, partner, half, right, _, left, stage, sem):
    run([half_copy(half, distance, place, left, sem)])
    sectors, flavours = left.shape[:2]
    for sector in range(sectors):
        for flavour in range(flavours):
            stage[flavour, sector] = product(place, partner, sector, flavour, left, right)


def early_products(place, partner, half, distance, left, right):
    sectors, flavours, width, _ = left.shape
    return kernel_call(
        functools.partial(early_kernel, distance),
        "early",
        [place, partner, in_vmem(half), in_vmem(right), in_vmem(left)],
        [SCALAR, SCALAR] + [WHOLE] * 3,
        [
            pltpu.VMEM(left.shape, left.dtype),
            pltpu.VMEM((flavours, sectors, width, right.shape[2]), jnp.bfloat16),
        ],
        [WHOLE] * 2,
        [pltpu.SemaphoreType.DMA],
        {4: 0},
    )


def late_kernel(early_units, units, nexts, unit, place, partner, left, early, *refs):
    pairs, refs = [refs[2 * i : 2 * i + 2] for i in range(len(nexts))], refs[2 * len(nexts) :]
    _, out, right, stage, sems, early_sems, out_sems = refs
    sectors, flavours = left.shape[:2]
    next_here = next_copies(nexts, place, pairs, right, sems, 0)
    for copy in next_here:
        copy.start()
    out_copies, at = [], 0
    for start, count in early_units:
        out_copies.append(
            pltpu.make_async_copy(
                early.at[:, :, :, pl.ds(at, count * unit)],
                out.at[:, :, :, pl.ds(first_column(start, place, unit), count * unit)],
                early_sems.at[len(out_copies)],
            )
        )
        out_copies[-1].start()
        at += count * unit
    for copy in next_here:
        copy.wait()
    for sector in range(sectors):
        for flavour in range(flavours):
            stage[flavour, sector] = product(place, partner, sector, flavour, left, right)
            at = 0
            for number, (start, count) in enumerate(units):
                copy = pltpu.make_async_copy(
                    stage.at[flavour, sector, :, pl.ds(at, count * unit)],
                    out.at[flavour, sector, :, pl.ds(first_column(start, place, unit), count * unit)],
                    out_sems.at[sector * flavours + flavour, number],
                )
                copy.start()
                out_copies.append(copy)
                at += count * unit
    for copy in out_copies:
        copy.wait()


def late_products(place, partner, early_units, units, nexts, unit, pairs, left, early, right):
    sectors, flavours, width, depth = left.shape
    given = [in_vmem(array) for array in (left, early, *(array for pair in pairs for array in pair), right)]
    return kernel_call(
        functools.partial(late_kernel, early_units, units, nexts, unit),
        "late",
        [place, partner, *given],
        [SCALAR, SCALAR] + [WHOLE] * len(given),
        [
            pltpu.HBM((flavours, sectors, width, depth), jnp.bfloat16),
            pltpu.VMEM(right.shape, right.dtype),
        ],
        [ANY, WHOLE],
        [
            pltpu.VMEM((flavours, sectors, width, right.shape[2]), jnp.bfloat16),
            pltpu.SemaphoreType.DMA((2 * sum(len(holds) for holds in nexts),)),
            pltpu.SemaphoreType.DMA((len(early_units),)),
            pltpu.SemaphoreType.DMA((sectors * flavours, len(units))),
        ],
        {1 + len(given): 1},
    )[0]


def local(basis, fermion, partner):
    sectors, depth, _ = basis.shape
    every = sectors * lax.axis_size("sec")
    unit = depth // 8
    place = jnp.stack([lax.axis_index("slab"), lax.axis_index("sec") * sectors, every, depth - 2 * unit])
    place = place.astype(jnp.int32)
    partner = partner.T
    distances = (3, 2, 1, 0)
    alone = sectors // 2
    count = 3
    early_units, late_units = ((0, count), (OWN, 1)), ((count, 6 - count), (OTHER, 1))
    first_blocks = [(sector, 1, start) for start in (*range(count), OWN) for sector in range(sectors)]
    last_blocks = [(sector, 1, start) for start in range(count, 6) for sector in range(sectors)]
    last_blocks += [(sector, 1, OTHER) for sector in range(alone)]
    first_part, last_part, *halves = basis_parts(
        place, basis, fermion, (first_blocks, last_blocks), unit, distances
    )
    first, last = previous(first_part), previous(last_part)
    far3, far2, mine, near = half_blocks(place, basis, fermion, distances, halves)
    got2, got3, beside = swapped(far2, 2), swapped(far3, 3), swapped(mine, 1)
    groups = ((0, 2), (2, 4))
    pieces = cut_out(first, [slice(begin * sectors, end * sectors) for begin, end in groups], (beside, got2))
    pairs = [(piece, swapped(piece, 1)) for piece in pieces]
    nexts = [
        [((at - begin) * sectors, sectors, 0, at * unit) for at in range(begin, end)] for begin, end in groups
    ]
    begin, end = groups[-1]
    cut = pl.ds((end - 1 - begin) * sectors + alone, sectors - alone)
    left, early_right, late_right, sent = gather(
        place, basis, early_units, late_units, nexts, unit, pairs, [got2, beside, near], distances[1:], cut
    )
    other = swapped(sent, 2)
    left, early = early_products(place, partner, got3, distances[0], left, early_right)
    nexts = [[(at * sectors, sectors, 0, at * unit) for at in range(6 - count)]]
    if alone:
        nexts[0].append(((6 - count) * sectors, alone, 0, (6 - count) * unit))
    nexts.append([(0, sectors - alone, alone, (6 - count) * unit)])
    last, other, early = lax.optimization_barrier((last, other, early))
    pairs = [(last, swapped(last, 1)), (other, swapped(other, 1))]
    return late_products(place, partner, early_units, late_units, nexts, unit, pairs, left, early, late_right)


def solution(mesh):
    placed = (P("sec", None, None), P(None, "sec", None, "slab"), P(None, "sec"))
    return jax.shard_map(
        local, mesh=mesh, in_specs=placed, out_specs=P(None, "sec", "slab", None), check_vma=False
    )
```

time: 123 us -> 57.6 us (0.47)
  waiting for transfers between devices: 59.2 us -> 28.8 us
  matrix products: 22.2 us -> 0 us
  local copies, waits for them, and re-layouts: 19.4 us -> 0.01 us
  Pallas kernels: 0 us -> 16.9 us
  loops' own time: 4.28 us -> 0 us
  between operations: 3.99 us -> 0.06 us
  other arithmetic: 2.94 us -> 0.08 us
  starting transfers between devices: 10 us -> 11.6 us
    all_to_all x1 -> x0, waiting for transfers between devices: 32.3 us -> none  [local(): lax.all_to_all(half_rotated, 'slab', split_axis=2, concat_axis=3, tiled=T...]
    dot_general x12 -> x0, matrix products: 22.2 us -> none  [the longest x5 13.5 us: from_next(): return jnp.dot(operand, chosen, preferred_element_type=jnp.float32)]
    pallas_call x0 -> x6, Pallas kernels: none -> 16.9 us  [kernel_call(): pl.pallas_call(body, out_shape=shapes, in_specs=specs, out_specs=out_spec...]
    all_to_all x2 -> x0, local copies, waits for them, and re-layouts: 8.77 us -> none  [local(): lax.all_to_all(half_rotated, 'slab', split_axis=2, concat_axis=3, tiled=T...]
    ppermute x1 -> x10, starting transfers between devices: 6 us -> 11.6 us  [the longest x2 5.98 us: previous(): lax.ppermute(block, 'sec', [((i + 1) % count, i) for i in range(count)])]
    another operation x1 -> x0, local copies, waits for them, and re-layouts: 4.9 us -> none  [local(): half_rotated = jnp.stack(half_blocks)]
    another operation x6 -> x0, loops' own time: 4.28 us -> none  [local(): lax.cond(where_index < sectors_here, from_own, from_next, rows_here)]
    all_to_all x1 -> x0, starting transfers between devices: 4.01 us -> none  [local(): lax.all_to_all(half_rotated, 'slab', split_axis=2, concat_axis=3, tiled=T...]
  transfers between devices with their start and end apart: 2 -> 10, of which waited for: 2 -> 7; matrix products, arithmetic and copies ran while one was open for 15% -> 0% of each run, Pallas kernels for 0% -> 13%
where the time goes in v2:
time: 57.6 us; the launch traced here: 57.4 us
  waiting for transfers between devices  28.8 us (50%)
  Pallas kernels  16.9 us (29%)
  starting transfers between devices  11.6 us (20%)
    ppermute x8, waiting for transfers between devices, swapped(): lax.ppermute(block, 'slab', [(i, i ^ distance) for i in range(lax.axis_si...  27.2 us
    pallas_call x6, Pallas kernels, kernel_call(): pl.pallas_call(body, out_shape=shapes, in_specs=specs, out_specs=out_spec...  16.9 us
    ppermute x2, starting transfers between devices, previous(): lax.ppermute(block, 'sec', [((i + 1) % count, i) for i in range(count)])  5.98 us
    ppermute x8, starting transfers between devices, swapped(): lax.ppermute(block, 'slab', [(i, i ^ distance) for i in range(lax.axis_si...  5.62 us
    ppermute x2, waiting for transfers between devices, previous(): lax.ppermute(block, 'sec', [((i + 1) % count, i) for i in range(count)])  1.65 us
  transfers between devices with their start and end apart: 10, of which 7 were waited for; matrix products, arithmetic and copies ran while one was open for 0% of the time, Pallas kernels for 13%

profile of v2, /device:TPU:0, one launch (start us, length us, event | category | flops | bytes accessed | tf_op | source)
XLA Modules:
  0.0 57.4 jit_solution(9153601980156190431)
XLA Ops:
  0.0 0.1 pad_add_fusion.place
  0.1 0.0 copy-start
  0.1 0.0 copy-start.1
  0.1 5.8 %part.1 = (bf16[8,512,128]{2,1,0:T(8,128)(2,1)S(1)}, bf16[7,512,128]{2,1,0:T(8,128)(2,1)S(1)}, bf16[2,3,256,256]{3,2,1,0:T(8,128)(2,1)S(1)}, bf16[2,3,256,256]{3...) custom-call(s32[4]{0:T(128)S(1)} %pad_add_fusion.place, ...), custom_call_target="tpu_custom_call" | custom-call | tf_op jit(solution)/shard_map/part/pallas_call | solution.py:27
  5.9 2.9 %collective-permute-start.3 = (bf16[8,512,128]{2,1,0:T(8,128)(2,1)S(1)}, bf16[8,512,128]{2,1,0:T(8,128)(2,1)S(1)}, u32[]{:S(2)}, u32[]{:S(2)}) collective-permute-start(bf16[8,512,128]{2,1,0:T(8,128)(2,1)S(1)} %get-tuple-element.35), channel_id=1, source_target_pairs={{4,0},{8,4},{12,8},{16,12},{20,16},{24,20},{28,24},{0,28},{5,1},{9... | collective-permute-start | bytes 3145736 | tf_op jit(solution)/shard_map/ppermute | solution.py:57
  8.8 0.0 copy-done
  8.8 0.0 copy-done.1
  8.8 2.4 %half.1 = (bf16[2,3,256,256]{3,2,1,0:T(8,128)(2,1)S(1)}, bf16[2,3,256,256]{3,2,1,0:T(8,128)(2,1)S(1)}, bf16[2,3,256,256]{3,2,1,0:T(8,128)(2,1)S(1)}, bf16[2,3,256,256]{3,2,1,0:T(8,128)(2,1)S(1)}) custom-call(s32[4]{0:T(128)S(1)} %pad_add_fusion.place, ...), custom_call_target="tpu_custom_call", output_to_operand_aliasing={{0}: (3, {}), {1}: (4, {}), {2}: (5, {}), {3}: (6, {})} | custom-call | tf_op jit(solution)/shard_map/half/pallas_call | solution.py:27
  11.2 1.6 %collective-permute-start.1 = (bf16[2,3,256,256]{3,2,1,0:T(8,128)(2,1)S(1)}, bf16[2,3,256,256]{3,2,1,0:T(8,128)(2,1)S(1)}, u32[]{:S(2)}, u32[]{:S(2)}) collective-permute-start(bf16[2,3,256,256]{3,2,1,0:T(8,128)(2,1)S(1)} %get-tuple-element.32), channel_id=1, source_target_pairs={{0,2},{1,3},{2,0},{3,1},{4,6},{5,7},{6,4},{7,5},{8,10},{9,11},{10,... | collective-permute-start | bytes 2359304 | tf_op jit(solution)/shard_map/ppermute | solution.py:61
  12.8 0.0 collective-permute-start.2
  12.8 3.1 %collective-permute-start.6 = (bf16[7,512,128]{2,1,0:T(8,128)(2,1)S(1)}, bf16[7,512,128]{2,1,0:T(8,128)(2,1)S(1)}, u32[]{:S(2)}, u32[]{:S(2)}) collective-permute-start(bf16[7,512,128]{2,1,0:T(8,128)(2,1)S(1)} %get-tuple-element.41), channel_id=1, source_target_pairs={{4,0},{8,4},{12,8},{16,12},{20,16},{24,20},{28,24},{0,28},{5,1},{9... | collective-permute-start | bytes 2752520 | tf_op jit(solution)/shard_map/ppermute | solution.py:57
  15.9 0.3 collective-permute-start
  16.2 15.6 %collective-permute-done.1.refs_1_.refs_0_ = bf16[2,3,256,256]{3,2,1,0:T(8,128)(2,1)S(1)} collective-permute-done((bf16[2,3,256,256]{3,2,1,0:T(8,128)(2,1)S(1)}, bf16[2,3,256,256]{3,2,1,0:T(8,128)(2,1)S(1)}, u32[]{:S(2)}, u32[]{:S(2)}) %collective-permute-start.1) | collective-permute-done | bytes 786464 | tf_op jit(solution)/shard_map/ppermute | solution.py:61
  31.8 0.0 collective-permute-done.2.refs_0_.refs_1_
  31.8 0.6 %collective-permute-done.3.given = bf16[8,512,128]{2,1,0:T(8,128)(2,1)S(1)} collective-permute-done((bf16[8,512,128]{2,1,0:T(8,128)(2,1)S(1)}, bf16[8,512,128]{2,1,0:T(8,128)(2,1)S(1)}, u32[]{:S(2)}, u32[]{:S(2)}) %collective-permute-start.3) | collective-permute-done | bytes 1048608 | tf_op jit(solution)/shard_map/ppermute | solution.py:57
  32.4 0.1 cut.1
  32.4 0.1 collective-permute-start.4
  32.5 0.5 collective-permute-start.5
  33.0 1.4 %collective-permute-done.4.refs_4_ = bf16[4,512,128]{2,1,0:T(8,128)(2,1)S(1)} collective-permute-done((bf16[4,512,128]{2,1,0:T(8,128)(2,1)S(1)}, bf16[4,512,128]{2,1,0:T(8,128)(2,1)S(1)}, u32[]{:S(2)}, u32[]{:S(2)}) %collective-permute-start.4) | collective-permute-done | bytes 524320 | tf_op jit(solution)/shard_map/ppermute | solution.py:61
  34.4 0.7 %collective-permute-done.5.refs_6_ = bf16[4,512,128]{2,1,0:T(8,128)(2,1)S(1)} collective-permute-done((bf16[4,512,128]{2,1,0:T(8,128)(2,1)S(1)}, bf16[4,512,128]{2,1,0:T(8,128)(2,1)S(1)}, u32[]{:S(2)}, u32[]{:S(2)}) %collective-permute-start.5) | collective-permute-done | bytes 524320 | tf_op jit(solution)/shard_map/ppermute | solution.py:61
  35.2 0.0 copy-start.2
  35.2 2.4 %gather.1 = (bf16[2,3,256,1024]{3,2,1,0:T(8,128)(2,1)S(1)}, bf16[4,1024,512]{2,1,0:T(8,128)(2,1)S(1)}, bf16[4,1024,512]{2,1,0:T(8,128)(2,1)S(1)}, bf16[1,512,128]{2,1,0:T(8,128)(2,1)S(1)}) custom-call(s32[4]{0:T(128)S(1)} %pad_add_fusion.place, bf16[2,1024,1024]{2,1,0:T(8,128)(2,1)S(1)} %copy-done, ...), custom_call_target="tpu_custom_call" | custom-call | tf_op jit(solution)/shard_map/gather/pallas_call | solution.py:27
  37.6 2.6 %collective-permute-start.7 = (bf16[1,512,128]{2,1,0:T(8,128)(2,1)S(1)}, bf16[1,512,128]{2,1,0:T(8,128)(2,1)S(1)}, u32[]{:S(2)}, u32[]{:S(2)}) collective-permute-start(bf16[1,512,128]{2,1,0:T(8,128)(2,1)S(1)} %get-tuple-element.42), channel_id=1, source_target_pairs={{0,2},{1,3},{2,0},{3,1},{4,6},{5,7},{6,4},{7,5},{8,10},{9,11},{10,... | collective-permute-start | bytes 393224 | tf_op jit(solution)/shard_map/ppermute | solution.py:61
  40.2 7.3 %collective-permute-done.half = bf16[2,3,256,256]{3,2,1,0:T(8,128)(2,1)S(1)} collective-permute-done((bf16[2,3,256,256]{3,2,1,0:T(8,128)(2,1)S(1)}, bf16[2,3,256,256]{3,2,1,0:T(8,128)(2,1)S(1)}, u32[]{:S(2)}, u32[]{:S(2)}) %collective-permute-start) | collective-permute-done | bytes 786464 | tf_op jit(solution)/shard_map/ppermute | solution.py:61
  47.6 0.0 copy-done.2
  47.6 2.5 %early.1 = (bf16[2,3,256,1024]{3,2,1,0:T(8,128)(2,1)S(1)}, bf16[3,2,256,512]{3,2,1,0:T(8,128)(2,1)S(1)}) custom-call(s32[4]{0:T(128)S(1)} %pad_add_fusion.place, s32[2,3]{1,0:T(2,128)S(1)} %bitcast.3, bf16[2,3,256,256]{3,2,1,0:T(8,128)(2,1)S(1)} %collective-permute-done.half, ...), custom_call_target="tpu_custom_call", output_to_operand_aliasing={{0}: (4, {})} | custom-call | tf_op jit(solution)/shard_map/early/pallas_call | solution.py:27
  50.1 1.0 %collective-permute-done.6.refs_0_ = bf16[7,512,128]{2,1,0:T(8,128)(2,1)S(1)} collective-permute-done((bf16[7,512,128]{2,1,0:T(8,128)(2,1)S(1)}, bf16[7,512,128]{2,1,0:T(8,128)(2,1)S(1)}, u32[]{:S(2)}, u32[]{:S(2)}) %collective-permute-start.6) | collective-permute-done | bytes 917536 | tf_op jit(solution)/shard_map/ppermute | solution.py:57
  51.1 0.0 collective-permute-done.7.refs_2_
  51.1 0.1 collective-permute-start.8
  51.3 0.4 collective-permute-start.9
  51.6 2.1 %collective-permute-done.9.refs_3_ = bf16[1,512,128]{2,1,0:T(8,128)(2,1)S(1)} collective-permute-done((bf16[1,512,128]{2,1,0:T(8,128)(2,1)S(1)}, bf16[1,512,128]{2,1,0:T(8,128)(2,1)S(1)}, u32[]{:S(2)}, u32[]{:S(2)}) %collective-permute-start.9) | collective-permute-done | bytes 131104 | tf_op jit(solution)/shard_map/ppermute | solution.py:61
  53.8 0.0 collective-permute-done.8.refs_1_
  53.8 3.7 %late.1 = (bf16[3,2,256,1024]{3,2,1,0:T(8,128)(2,1)}, bf16[4,1024,512]{2,1,0:T(8,128)(2,1)S(1)}) custom-call(s32[4]{0:T(128)S(1)} %pad_add_fusion.place, s32[2,3]{1,0:T(2,128)S(1)} %bitcast.4, bf16[2,3,256,1024]{3,2,1,0:T(8,128)(2,1)S(1)} %get-tuple-element.40.left, ...), custom_call_target="tpu_custom_call", output_to_operand_aliasing={{1}: (8, {})} | custom-call | tf_op jit(solution)/shard_map/late/pallas_call | solution.py:27
Async XLA Ops:
  0.1 8.7 %copy-start = (bf16[2,1024,1024]{2,1,0:T(8,128)(2,1)S(1)}, bf16[2,1024,1024]{2,1,0:T(8,128)(2,1)}, u32[]{:S(2)}) copy-start(bf16[2,1024,1024]{2,1,0:T(8,128)(2,1)} %basis.5) | copy-start | bytes 12582916
  0.1 8.7 %copy-start.1 = (bf16[3,2,1024,256]{3,2,1,0:T(8,128)(2,1)S(1)}, bf16[3,2,1024,256]{3,2,1,0:T(8,128)(2,1)}, u32[]{:S(2)}) copy-start(bf16[3,2,1024,256]{3,2,1,0:T(8,128)(2,1)} %fermion.3) | copy-start | bytes 9437188
  5.9 26.5 %collective-permute-start.3 = (bf16[8,512,128]{2,1,0:T(8,128)(2,1)S(1)}, bf16[8,512,128]{2,1,0:T(8,128)(2,1)S(1)}, u32[]{:S(2)}, u32[]{:S(2)}) collective-permute-start(bf16[8,512,128]{2,1,0:T(8,128)(2,1)S(1)} %get-tuple-element.35), channel_id=1, source_target_pairs={{4,0},{8,4},{12,8},{16,12},{20,16},{24,20},{28,24},{0,28},{5,1},{9... | collective-permute-start | bytes 3145736 | tf_op jit(solution)/shard_map/ppermute | solution.py:57
  11.2 20.5 %collective-permute-start.1 = (bf16[2,3,256,256]{3,2,1,0:T(8,128)(2,1)S(1)}, bf16[2,3,256,256]{3,2,1,0:T(8,128)(2,1)S(1)}, u32[]{:S(2)}, u32[]{:S(2)}) collective-permute-start(bf16[2,3,256,256]{3,2,1,0:T(8,128)(2,1)S(1)} %get-tuple-element.32), channel_id=1, source_target_pairs={{0,2},{1,3},{2,0},{3,1},{4,6},{5,7},{6,4},{7,5},{8,10},{9,11},{10,... | collective-permute-start | bytes 2359304 | tf_op jit(solution)/shard_map/ppermute | solution.py:61
  12.8 19.0 %collective-permute-start.2 = (bf16[2,3,256,256]{3,2,1,0:T(8,128)(2,1)S(1)}, bf16[2,3,256,256]{3,2,1,0:T(8,128)(2,1)S(1)}, u32[]{:S(2)}, u32[]{:S(2)}) collective-permute-start(bf16[2,3,256,256]{3,2,1,0:T(8,128)(2,1)S(1)} %get-tuple-element.33), channel_id=1, source_target_pairs={{0,1},{1,0},{2,3},{3,2},{4,5},{5,4},{6,7},{7,6},{8,9},{9,8},{10,11... | collective-permute-start | bytes 2359304 | tf_op jit(solution)/shard_map/ppermute | solution.py:61
  12.8 38.3 %collective-permute-start.6 = (bf16[7,512,128]{2,1,0:T(8,128)(2,1)S(1)}, bf16[7,512,128]{2,1,0:T(8,128)(2,1)S(1)}, u32[]{:S(2)}, u32[]{:S(2)}) collective-permute-start(bf16[7,512,128]{2,1,0:T(8,128)(2,1)S(1)} %get-tuple-element.41), channel_id=1, source_target_pairs={{4,0},{8,4},{12,8},{16,12},{20,16},{24,20},{28,24},{0,28},{5,1},{9... | collective-permute-start | bytes 2752520 | tf_op jit(solution)/shard_map/ppermute | solution.py:57
  15.9 31.7 %collective-permute-start = (bf16[2,3,256,256]{3,2,1,0:T(8,128)(2,1)S(1)}, bf16[2,3,256,256]{3,2,1,0:T(8,128)(2,1)S(1)}, u32[]{:S(2)}, u32[]{:S(2)}) collective-permute-start(bf16[2,3,256,256]{3,2,1,0:T(8,128)(2,1)S(1)} %get-tuple-element.31), channel_id=1, source_target_pairs={{0,3},{1,2},{2,1},{3,0},{4,7},{5,6},{6,5},{7,4},{8,11},{9,10},{10,... | collective-permute-start | bytes 2359304 | tf_op jit(solution)/shard_map/ppermute | solution.py:61
  32.4 2.0 %collective-permute-start.4 = (bf16[4,512,128]{2,1,0:T(8,128)(2,1)S(1)}, bf16[4,512,128]{2,1,0:T(8,128)(2,1)S(1)}, u32[]{:S(2)}, u32[]{:S(2)}) collective-permute-start(bf16[4,512,128]{2,1,0:T(8,128)(2,1)S(1)} %get-tuple-element.36.refs_3_), channel_id=1, source_target_pairs={{0,1},{1,0},{2,3},{3,2},{4,5},{5,4},{6,7},{7,6},{8,9},{9,8},{10,11... | collective-permute-start | bytes 1572872 | tf_op jit(solution)/shard_map/ppermute | solution.py:61
  32.5 2.6 %collective-permute-start.5 = (bf16[4,512,128]{2,1,0:T(8,128)(2,1)S(1)}, bf16[4,512,128]{2,1,0:T(8,128)(2,1)S(1)}, u32[]{:S(2)}, u32[]{:S(2)}) collective-permute-start(bf16[4,512,128]{2,1,0:T(8,128)(2,1)S(1)} %get-tuple-element.37.refs_5_), channel_id=1, source_target_pairs={{0,1},{1,0},{2,3},{3,2},{4,5},{5,4},{6,7},{7,6},{8,9},{9,8},{10,11... | collective-permute-start | bytes 1572872 | tf_op jit(solution)/shard_map/ppermute | solution.py:61
  35.2 12.4 %copy-start.2 = (s32[3,2]{0,1:T(2,128)S(1)}, s32[3,2]{0,1:T(2,128)}, u32[]{:S(2)}) copy-start(s32[3,2]{0,1:T(2,128)} %param.5) | copy-start | bytes 76
  37.6 13.5 %collective-permute-start.7 = (bf16[1,512,128]{2,1,0:T(8,128)(2,1)S(1)}, bf16[1,512,128]{2,1,0:T(8,128)(2,1)S(1)}, u32[]{:S(2)}, u32[]{:S(2)}) collective-permute-start(bf16[1,512,128]{2,1,0:T(8,128)(2,1)S(1)} %get-tuple-element.42), channel_id=1, source_target_pairs={{0,2},{1,3},{2,0},{3,1},{4,6},{5,7},{6,4},{7,5},{8,10},{9,11},{10,... | collective-permute-start | bytes 393224 | tf_op jit(solution)/shard_map/ppermute | solution.py:61
  51.1 2.7 %collective-permute-start.8 = (bf16[7,512,128]{2,1,0:T(8,128)(2,1)S(1)}, bf16[7,512,128]{2,1,0:T(8,128)(2,1)S(1)}, u32[]{:S(2)}, u32[]{:S(2)}) collective-permute-start(bf16[7,512,128]{2,1,0:T(8,128)(2,1)S(1)} %collective-permute-done.6.refs_0_), channel_id=1, source_target_pairs={{0,1},{1,0},{2,3},{3,2},{4,5},{5,4},{6,7},{7,6},{8,9},{9,8},{10,11... | collective-permute-start | bytes 2752520 | tf_op jit(solution)/shard_map/ppermute | solution.py:61
  51.3 2.5 %collective-permute-start.9 = (bf16[1,512,128]{2,1,0:T(8,128)(2,1)S(1)}, bf16[1,512,128]{2,1,0:T(8,128)(2,1)S(1)}, u32[]{:S(2)}, u32[]{:S(2)}) collective-permute-start(bf16[1,512,128]{2,1,0:T(8,128)(2,1)S(1)} %collective-permute-done.7.refs_2_), channel_id=1, source_target_pairs={{0,1},{1,0},{2,3},{3,2},{4,5},{5,4},{6,7},{7,6},{8,9},{9,8},{10,11... | collective-permute-start | bytes 393224 | tf_op jit(solution)/shard_map/ppermute | solution.py:61

commit v3 on v2

--- a/solution.py
+++ b/solution.py
@@ -8,7 +8,6 @@
 from jax.sharding import PartitionSpec as P
 
 ANY = pl.BlockSpec(memory_space=pl.ANY)
-SCALAR = pl.BlockSpec(memory_space=pltpu.SMEM)
 WHOLE = pl.BlockSpec(memory_space=pltpu.VMEM)
 OWN, OTHER = -1, -2
 KERNEL_BYTES = 16 * 1024 * 1024
@@ -23,9 +22,17 @@
     return pltpu.with_memory_space_constraint(array, pltpu.VMEM)
 
 
-def kernel_call(body, name, given, specs, shapes, out_specs, scratch=(), aliases={}, cost=BRIEF):
+def located(sectors, depth):
+    first = lax.axis_index("sec") * sectors
+    return lax.axis_index("slab"), first, lax.axis_size("sec") * sectors, depth - depth // 8 * 2
+
+
+def kernel_call(body, name, shape, given, specs, shapes, out_specs, scratch=(), aliases={}, cost=BRIEF):
+    def kernel(*refs):
+        body(*(() if shape is None else (located(*shape),)), *refs)
+
     return pl.pallas_call(
-        body,
+        kernel,
         out_shape=shapes,
         in_specs=specs,
         out_specs=out_specs,
@@ -61,96 +68,133 @@
     return lax.ppermute(block, "slab", [(i, i ^ distance) for i in range(lax.axis_size("slab"))])
 
 
-def part_kernel(lists, unit, distances, place, basis, fermion, *refs):
-    sent, refs = refs[: len(lists)], refs[len(lists) :]
-    *pieces, left, right, sems, half_sems = refs
+def part_copies(blocks, unit, place, basis, array, sems):
     slabs = lax.axis_size("slab")
     rows = basis.shape[1] // slabs
     copies = []
-    for array, blocks in zip(sent, lists):
-        for at, (sector, count, start) in enumerate(blocks):
-            for slab in range(slabs // 2):
-                row = pl.multiple_of((2 * slab + place[0] % 2) * rows, rows)
-                copies.append(
-                    pltpu.make_async_copy(
-                        basis.at[sector, pl.ds(row, rows), pl.ds(first_column(start, place, unit), count * unit)],
-                        array.at[at, pl.ds(slab * rows, rows)],
-                        sems.at[len(copies)],
-                    )
+    for at, (sector, start) in enumerate(blocks):
+        for slab in range(slabs // 2):
+            row = pl.multiple_of((2 * slab + place[0] % 2) * rows, rows)
+            copies.append(
+                pltpu.make_async_copy(
+                    basis.at[sector, pl.ds(row, rows), pl.ds(first_column(start, place, unit), unit)],
+                    array.at[at, pl.ds(slab * rows, rows)],
+                    sems.at[len(copies)],
                 )
+            )
+    return copies
+
+
+def half_products(sectors, distances, place, basis, fermion, pieces, ready=lambda sector: None):
+    flavours, _, _, width = fermion.shape
+    for sector in sectors:
+        ready(sector)
+        right = jnp.concatenate([fermion[flavour, sector] for flavour in range(flavours)], axis=1)
+        for slot, distance in enumerate(distances):
+            column = pl.multiple_of((place[0] ^ distance) * width, width)
+            block = lax.dot_general(
+                basis[sector, :, pl.ds(column, width)],
+                right,
+                (((0,), (0,)), ((), ())),
+                preferred_element_type=jnp.float32,
+            ).astype(jnp.bfloat16)
+            for flavour in range(flavours):
+                pieces[slot][sector, flavour] = block[:, flavour * width : (flavour + 1) * width]
+
+
+def part_kernel(blocks, unit, distances, place, basis, fermion, sent, *refs):
+    *pieces, left, right, sems, half_sems = refs
+    copies = part_copies(blocks, unit, place, basis, sent, sems)
     for copy in copies:
         copy.start()
 
     @pl.when(place[1] == 0)
     def _():
-        run(
+        held = [
             [
-                pltpu.make_async_copy(basis.at[pl.ds(0, 1)], left, half_sems.at[0]),
-                pltpu.make_async_copy(fermion.at[:, pl.ds(0, 1)], right, half_sems.at[1]),
+                pltpu.make_async_copy(basis.at[sector], left.at[sector], half_sems.at[sector, 0]),
+                pltpu.make_async_copy(fermion.at[:, sector], right.at[:, sector], half_sems.at[sector, 1]),
             ]
-        )
-        half_products(0, distances, place, left, right, pieces)
+            for sector in range(basis.shape[0])
+        ]
+        for pair in held:
+            for copy in pair:
+                copy.start()
+
+        def ready(sector):
+            for copy in held[sector]:
+                copy.wait()
+
+        half_products(range(basis.shape[0]), distances, place, left, right, pieces, ready)
 
     for copy in copies:
         copy.wait()
 
 
-def basis_parts(place, basis, fermion, lists, unit, distances):
+def basis_part(basis, fermion, blocks, unit, distances):
     flavours, sectors, depth, width = fermion.shape
-    copies = sum(len(blocks) for blocks in lists) * lax.axis_size("slab") // 2
-    shapes = [pltpu.VMEM((len(blocks), depth // 2, blocks[0][1] * unit), jnp.bfloat16) for blocks in lists]
+    shapes = [pltpu.VMEM((len(blocks), depth // 2, unit), jnp.bfloat16)]
     shapes += [pltpu.VMEM((sectors, flavours, width, width), jnp.bfloat16)] * len(distances)
     return kernel_call(
-        functools.partial(part_kernel, lists, unit, distances),
+        functools.partial(part_kernel, blocks, unit, distances),
         "part",
-        [place, in_hbm(basis), in_hbm(fermion)],
-        [SCALAR, ANY, ANY],
+        basis.shape[:2],
+        [in_hbm(basis), in_hbm(fermion)],
+        [ANY, ANY],
         shapes,
         [WHOLE] * len(shapes),
         [
-            pltpu.VMEM((1, depth, depth), jnp.bfloat16),
-            pltpu.VMEM((flavours, 1, depth, width), jnp.bfloat16),
-            pltpu.SemaphoreType.DMA((copies,)),
-            pltpu.SemaphoreType.DMA((2,)),
+            pltpu.VMEM((sectors, depth, depth), jnp.bfloat16),
+            pltpu.VMEM((flavours, sectors, depth, width), jnp.bfloat16),
+            pltpu.SemaphoreType.DMA((len(blocks) * lax.axis_size("slab") // 2,)),
+            pltpu.SemaphoreType.DMA((sectors, 2)),
         ],
     )
 
 
-def half_products(sector, distances, place, basis, fermion, pieces):
-    flavours, _, _, width = fermion.shape
-    right = jnp.concatenate([fermion[flavour, sector] for flavour in range(flavours)], axis=1)
-    for slot, distance in enumerate(distances):
-        column = pl.multiple_of((place[0] ^ distance) * width, width)
-        block = lax.dot_general(
-            basis[sector, :, pl.ds(column, width)],
-            right,
-            (((0,), (0,)), ((), ())),
-            preferred_element_type=jnp.float32,
-        ).astype(jnp.bfloat16)
-        for flavour in range(flavours):
-            pieces[slot][sector, flavour] = block[:, flavour * width : (flavour + 1) * width]
-
-
-def half_kernel(distances, place, basis, fermion, *refs):
+def far_kernel(distances, place, basis, fermion, *refs):
     pieces = refs[len(distances) :]
 
     @pl.when(place[1] != 0)
     def _():
-        half_products(0, distances, place, basis, fermion, pieces)
-
-    for sector in range(1, basis.shape[0]):
-        half_products(sector, distances, place, basis, fermion, pieces)
-
-
-def half_blocks(place, basis, fermion, distances, earlier):
-    return kernel_call(
-        functools.partial(half_kernel, distances),
-        "half",
-        [place, in_vmem(basis), in_vmem(fermion), *map(in_vmem, earlier)],
-        [SCALAR] + [WHOLE] * (2 + len(earlier)),
+        half_products(range(basis.shape[0]), distances, place, basis, fermion, pieces)
+
+
+def far_blocks(basis, fermion, distances, earlier):
+    return kernel_call(
+        functools.partial(far_kernel, distances),
+        "far",
+        basis.shape[:2],
+        [in_vmem(basis), in_vmem(fermion), *map(in_vmem, earlier)],
+        [WHOLE] * (2 + len(earlier)),
         [pltpu.VMEM(piece.shape, piece.dtype) for piece in earlier],
         [WHOLE] * len(distances),
-        aliases={3 + at: at for at in range(len(earlier))},
+        aliases={2 + at: at for at in range(len(earlier))},
+    )
+
+
+def near_kernel(blocks, unit, distances, place, basis, fermion, _, *refs):
+    *pieces, sent, sems = refs
+    copies = part_copies(blocks, unit, place, basis, sent, sems)
+    for copy in copies:
+        copy.start()
+    half_products(range(basis.shape[0]), distances, place, basis, fermion, pieces)
+    for copy in copies:
+        copy.wait()
+
+
+def near_blocks(basis, fermion, blocks, unit, distances, after):
+    flavours, sectors, depth, width = fermion.shape
+    return kernel_call(
+        functools.partial(near_kernel, blocks, unit, distances),
+        "near",
+        basis.shape[:2],
+        [in_vmem(basis), in_vmem(fermion), in_vmem(after)],
+        [WHOLE, WHOLE, WHOLE],
+        [pltpu.VMEM((sectors, flavours, width, width), jnp.bfloat16)] * len(distances)
+        + [pltpu.VMEM((len(blocks), depth // 2, unit), jnp.bfloat16)],
+        [WHOLE] * (len(distances) + 1),
+        [pltpu.SemaphoreType.DMA((len(blocks) * lax.axis_size("slab") // 2,))],
     )
 
 
@@ -164,6 +208,7 @@
     return kernel_call(
         functools.partial(cut_kernel, cuts),
         "cut",
+        None,
         [in_vmem(array), *map(in_vmem, after)],
         [WHOLE] * (1 + len(after)),
         [pltpu.VMEM(shape, array.dtype) for shape in shapes],
@@ -230,7 +275,7 @@
     run(copies)
 
 
-def gather(place, basis, early_units, late_units, nexts, unit, pairs, halves, distances, cut):
+def gather(basis, early_units, late_units, nexts, unit, pairs, halves, distances, cut):
     sectors, depth, _ = basis.shape
     flavours, width = halves[0].shape[1:3]
     given = [in_vmem(array) for array in (basis, *halves, *(array for pair in pairs for array in pair))]
@@ -240,8 +285,9 @@
     return kernel_call(
         functools.partial(gather_kernel, early_units, late_units, nexts, unit, distances, cut),
         "gather",
-        [place, *given],
-        [SCALAR] + [WHOLE] * len(given),
+        basis.shape[:2],
+        given,
+        [WHOLE] * len(given),
         [
             pltpu.VMEM((sectors, flavours, width, depth), jnp.bfloat16),
             pltpu.VMEM((2 * sectors, depth, early_columns), jnp.bfloat16),
@@ -254,7 +300,7 @@
 
 
 def product(place, partner, sector, flavour, left, right):
-    index = (partner[sector, flavour] - place[1] + place[2]) % place[2]
+    index = (partner[...][sector, flavour] - place[1] + place[2]) % place[2]
     return jnp.dot(left[sector, flavour], right[index], preferred_element_type=jnp.float32).astype(jnp.bfloat16)
 
 
@@ -266,20 +312,21 @@
             stage[flavour, sector] = product(place, partner, sector, flavour, left, right)
 
 
-def early_products(place, partner, half, distance, left, right):
+def early_products(partner, half, distance, left, right):
     sectors, flavours, width, _ = left.shape
     return kernel_call(
         functools.partial(early_kernel, distance),
         "early",
-        [place, partner, in_vmem(half), in_vmem(right), in_vmem(left)],
-        [SCALAR, SCALAR] + [WHOLE] * 3,
+        (left.shape[0], left.shape[3]),
+        [partner, in_vmem(half), in_vmem(right), in_vmem(left)],
+        [WHOLE] + [WHOLE] * 3,
         [
             pltpu.VMEM(left.shape, left.dtype),
             pltpu.VMEM((flavours, sectors, width, right.shape[2]), jnp.bfloat16),
         ],
         [WHOLE] * 2,
         [pltpu.SemaphoreType.DMA],
-        {4: 0},
+        {3: 0},
     )
 
 
@@ -320,14 +367,15 @@
         copy.wait()
 
 
-def late_products(place, partner, early_units, units, nexts, unit, pairs, left, early, right):
+def late_products(partner, early_units, units, nexts, unit, pairs, left, early, right):
     sectors, flavours, width, depth = left.shape
     given = [in_vmem(array) for array in (left, early, *(array for pair in pairs for array in pair), right)]
     return kernel_call(
         functools.partial(late_kernel, early_units, units, nexts, unit),
         "late",
-        [place, partner, *given],
-        [SCALAR, SCALAR] + [WHOLE] * len(given),
+        (sectors, depth),
+        [partner, *given],
+        [WHOLE] + [WHOLE] * len(given),
         [
             pltpu.HBM((flavours, sectors, width, depth), jnp.bfloat16),
             pltpu.VMEM(right.shape, right.dtype),
@@ -339,30 +387,27 @@
             pltpu.SemaphoreType.DMA((len(early_units),)),
             pltpu.SemaphoreType.DMA((sectors * flavours, len(units))),
         ],
-        {1 + len(given): 1},
+        {len(given): 1},
     )[0]
 
 
 def local(basis, fermion, partner):
     sectors, depth, _ = basis.shape
-    every = sectors * lax.axis_size("sec")
     unit = depth // 8
-    place = jnp.stack([lax.axis_index("slab"), lax.axis_index("sec") * sectors, every, depth - 2 * unit])
-    place = place.astype(jnp.int32)
     partner = partner.T
     distances = (3, 2, 1, 0)
     alone = sectors // 2
     count = 3
     early_units, late_units = ((0, count), (OWN, 1)), ((count, 6 - count), (OTHER, 1))
-    first_blocks = [(sector, 1, start) for start in (*range(count), OWN) for sector in range(sectors)]
-    last_blocks = [(sector, 1, start) for start in range(count, 6) for sector in range(sectors)]
-    last_blocks += [(sector, 1, OTHER) for sector in range(alone)]
-    first_part, last_part, *halves = basis_parts(
-        place, basis, fermion, (first_blocks, last_blocks), unit, distances
-    )
-    first, last = previous(first_part), previous(last_part)
-    far3, far2, mine, near = half_blocks(place, basis, fermion, distances, halves)
-    got2, got3, beside = swapped(far2, 2), swapped(far3, 3), swapped(mine, 1)
+    first_blocks = [(sector, start) for start in (*range(count), OWN) for sector in range(sectors)]
+    last_blocks = [(sector, start) for start in range(count, 6) for sector in range(sectors)]
+    last_blocks += [(sector, OTHER) for sector in range(alone)]
+    first_part, *far = basis_part(basis, fermion, first_blocks, unit, distances[:2])
+    first = previous(first_part)
+    far3, far2 = far_blocks(basis, fermion, distances[:2], far)
+    got2, got3 = swapped(far2, 2), swapped(far3, 3)
+    mine, near, last_part = near_blocks(basis, fermion, last_blocks, unit, distances[2:], far2)
+    beside, last = swapped(mine, 1), previous(last_part)
     groups = ((0, 2), (2, 4))
     pieces = cut_out(first, [slice(begin * sectors, end * sectors) for begin, end in groups], (beside, got2))
     pairs = [(piece, swapped(piece, 1)) for piece in pieces]
@@ -372,17 +417,17 @@
     begin, end = groups[-1]
     cut = pl.ds((end - 1 - begin) * sectors + alone, sectors - alone)
     left, early_right, late_right, sent = gather(
-        place, basis, early_units, late_units, nexts, unit, pairs, [got2, beside, near], distances[1:], cut
+        basis, early_units, late_units, nexts, unit, pairs, [got2, beside, near], distances[1:], cut
     )
     other = swapped(sent, 2)
-    left, early = early_products(place, partner, got3, distances[0], left, early_right)
+    left, early = early_products(partner, got3, distances[0], left, early_right)
     nexts = [[(at * sectors, sectors, 0, at * unit) for at in range(6 - count)]]
     if alone:
         nexts[0].append(((6 - count) * sectors, alone, 0, (6 - count) * unit))
     nexts.append([(0, sectors - alone, alone, (6 - count) * unit)])
     last, other, early = lax.optimization_barrier((last, other, early))
     pairs = [(last, swapped(last, 1)), (other, swapped(other, 1))]
-    return late_products(place, partner, early_units, late_units, nexts, unit, pairs, left, early, late_right)
+    return late_products(partner, early_units, late_units, nexts, unit, pairs, left, early, late_right)
 
 
 def solution(mesh):

time: 57.6 us -> 56.2 us (0.976)
  Pallas kernels: 16.9 us -> 14.4 us
  starting transfers between devices: 11.6 us -> 12.4 us
    ppermute x2, waiting for transfers between devices: 1.65 us -> 7.3 us  [previous(): lax.ppermute(block, 'sec', [((i + 1) % count, i) for i in range(count)])]
    ppermute x8, waiting for transfers between devices: 27.2 us -> 21.9 us  [swapped(): lax.ppermute(block, 'slab', [(i, i ^ distance) for i in range(lax.axis_si...]
    pallas_call x6 -> x7, Pallas kernels: 16.9 us -> 14.4 us  [kernel_call(): pl.pallas_call(kernel, out_shape=shapes, in_specs=specs, out_specs=out_sp...]
    ppermute x2, starting transfers between devices: 5.98 us -> 6.6 us  [previous(): lax.ppermute(block, 'sec', [((i + 1) % count, i) for i in range(count)])]
  transfers between devices with their start and end apart: 10 -> 10, of which waited for: 7 -> 7; matrix products, arithmetic and copies ran while one was open for 0% -> 0% of each run, Pallas kernels for 13% -> 11%
where the time goes in v3:
time: 56.2 us; the launch traced here: 56.1 us
  waiting for transfers between devices  29.2 us (52%)
  Pallas kernels  14.4 us (26%)
  starting transfers between devices  12.4 us (22%)
    ppermute x8, waiting for transfers between devices, swapped(): lax.ppermute(block, 'slab', [(i, i ^ distance) for i in range(lax.axis_si...  21.9 us
    pallas_call x7, Pallas kernels, kernel_call(): pl.pallas_call(kernel, out_shape=shapes, in_specs=specs, out_specs=out_sp...  14.4 us
    ppermute x2, waiting for transfers between devices, previous(): lax.ppermute(block, 'sec', [((i + 1) % count, i) for i in range(count)])  7.3 us
    ppermute x2, starting transfers between devices, previous(): lax.ppermute(block, 'sec', [((i + 1) % count, i) for i in range(count)])  6.6 us
    ppermute x8, starting transfers between devices, swapped(): lax.ppermute(block, 'slab', [(i, i ^ distance) for i in range(lax.axis_si...  5.84 us
  transfers between devices with their start and end apart: 10, of which 7 were waited for; matrix products, arithmetic and copies ran while one was open for 0% of the time, Pallas kernels for 11%

profile of v3, /device:TPU:0, one launch (start us, length us, event | category | flops | bytes accessed | tf_op | source)
XLA Modules:
  0.0 56.1 jit_solution(11315044033325494379)
XLA Ops:
  0.0 0.0 copy-start
  0.0 0.0 copy-start.1
  0.0 5.0 %part.1 = (bf16[8,512,128]{2,1,0:T(8,128)(2,1)S(1)}, bf16[2,3,256,256]{3,2,1,0:T(8,128)(2,1)S(1)}, bf16[2,3,256,256]{3,2,1,0:T(8,128)(2,1)S(1)}) custom-call(bf16[2,1024,1024]{2,1,0:T(8,128)(2,1)} %refs_0_.7, bf16[3,2,1024,256]{3,2,1,0:T(8,128)(2,1)} %refs_1_.5), custom_call_target="tpu_custom_call" | custom-call | tf_op jit(solution)/shard_map/part/pallas_call | solution.py:34
  5.0 2.7 %collective-permute-start.3 = (bf16[8,512,128]{2,1,0:T(8,128)(2,1)S(1)}, bf16[8,512,128]{2,1,0:T(8,128)(2,1)S(1)}, u32[]{:S(2)}, u32[]{:S(2)}) collective-permute-start(bf16[8,512,128]{2,1,0:T(8,128)(2,1)S(1)} %get-tuple-element.31), channel_id=1, source_target_pairs={{4,0},{8,4},{12,8},{16,12},{20,16},{24,20},{28,24},{0,28},{5,1},{9... | collective-permute-start | bytes 3145736 | tf_op jit(solution)/shard_map/ppermute | solution.py:64
  7.7 0.0 copy-done
  7.7 0.0 copy-done.1
  7.7 1.5 %collective-permute-start.1 = (bf16[2,3,256,256]{3,2,1,0:T(8,128)(2,1)S(1)}, bf16[2,3,256,256]{3,2,1,0:T(8,128)(2,1)S(1)}, u32[]{:S(2)}, u32[]{:S(2)}) collective-permute-start(bf16[2,3,256,256]{3,2,1,0:T(8,128)(2,1)S(1)} %get-tuple-element.28.refs_2_), channel_id=1, source_target_pairs={{0,2},{1,3},{2,0},{3,1},{4,6},{5,7},{6,4},{7,5},{8,10},{9,11},{10,... | collective-permute-start | bytes 2359304 | tf_op jit(solution)/shard_map/ppermute | solution.py:68
  9.2 2.2 %near.1 = (bf16[2,3,256,256]{3,2,1,0:T(8,128)(2,1)S(1)}, bf16[2,3,256,256]{3,2,1,0:T(8,128)(2,1)S(1)}, bf16[7,512,128]{2,1,0:T(8,128)(2,1)S(1)}) custom-call(bf16[2,1024,1024]{2,1,0:T(8,128)(2,1)S(1)} %copy-done, bf16[3,2,1024,256]{3,2,1,0:T(8,128)(2,1)S(1)} %copy-done.1, bf16[2,3,256,256]{3,2,1,0:T(8,128)(2,1)S(1)} %get-tuple-element.28.refs_2_), custom_call_target="tpu_custom_call" | custom-call | tf_op jit(solution)/shard_map/near/pallas_call | solution.py:34
  11.4 0.1 collective-permute-start.2
  11.5 3.9 %collective-permute-start.6 = (bf16[7,512,128]{2,1,0:T(8,128)(2,1)S(1)}, bf16[7,512,128]{2,1,0:T(8,128)(2,1)S(1)}, u32[]{:S(2)}, u32[]{:S(2)}) collective-permute-start(bf16[7,512,128]{2,1,0:T(8,128)(2,1)S(1)} %get-tuple-element.37), channel_id=1, source_target_pairs={{4,0},{8,4},{12,8},{16,12},{20,16},{24,20},{28,24},{0,28},{5,1},{9... | collective-permute-start | bytes 2752520 | tf_op jit(solution)/shard_map/ppermute | solution.py:64
  15.4 0.4 collective-permute-start
  15.8 12.4 %collective-permute-done.1.refs_2_.refs_1_ = bf16[2,3,256,256]{3,2,1,0:T(8,128)(2,1)S(1)} collective-permute-done((bf16[2,3,256,256]{3,2,1,0:T(8,128)(2,1)S(1)}, bf16[2,3,256,256]{3,2,1,0:T(8,128)(2,1)S(1)}, u32[]{:S(2)}, u32[]{:S(2)}) %collective-permute-start.1) | collective-permute-done | bytes 786464 | tf_op jit(solution)/shard_map/ppermute | solution.py:68
  28.1 0.0 collective-permute-done.2.refs_1_.refs_2_
  28.1 3.1 %collective-permute-done.3.refs_0_ = bf16[8,512,128]{2,1,0:T(8,128)(2,1)S(1)} collective-permute-done((bf16[8,512,128]{2,1,0:T(8,128)(2,1)S(1)}, bf16[8,512,128]{2,1,0:T(8,128)(2,1)S(1)}, u32[]{:S(2)}, u32[]{:S(2)}) %collective-permute-start.3) | collective-permute-done | bytes 1048608 | tf_op jit(solution)/shard_map/ppermute | solution.py:64
  31.2 0.1 cut.1
  31.3 0.1 collective-permute-start.4
  31.4 0.5 collective-permute-start.5
  31.9 1.4 %collective-permute-done.4.refs_5_ = bf16[4,512,128]{2,1,0:T(8,128)(2,1)S(1)} collective-permute-done((bf16[4,512,128]{2,1,0:T(8,128)(2,1)S(1)}, bf16[4,512,128]{2,1,0:T(8,128)(2,1)S(1)}, u32[]{:S(2)}, u32[]{:S(2)}) %collective-permute-start.4) | collective-permute-done | bytes 524320 | tf_op jit(solution)/shard_map/ppermute | solution.py:68
  33.3 0.7 %collective-permute-done.5.refs_7_ = bf16[4,512,128]{2,1,0:T(8,128)(2,1)S(1)} collective-permute-done((bf16[4,512,128]{2,1,0:T(8,128)(2,1)S(1)}, bf16[4,512,128]{2,1,0:T(8,128)(2,1)S(1)}, u32[]{:S(2)}, u32[]{:S(2)}) %collective-permute-start.5) | collective-permute-done | bytes 524320 | tf_op jit(solution)/shard_map/ppermute | solution.py:68
  34.0 0.0 copy-start.2
  34.0 1.9 %gather.1 = (bf16[2,3,256,1024]{3,2,1,0:T(8,128)(2,1)S(1)}, bf16[4,1024,512]{2,1,0:T(8,128)(2,1)S(1)}, bf16[4,1024,512]{2,1,0:T(8,128)(2,1)S(1)}, bf16[1,512,128]{2,1,0:T(8,128)(2,1)S(1)}) custom-call(bf16[2,1024,1024]{2,1,0:T(8,128)(2,1)S(1)} %copy-done, bf16[2,3,256,256]{3,2,1,0:T(8,128)(2,1)S(1)} %collective-permute-done.1.refs_2_.refs_1_, ...), custom_call_target="tpu_custom_call" | custom-call | tf_op jit(solution)/shard_map/gather/pallas_call | solution.py:34
  35.9 2.8 %collective-permute-start.7 = (bf16[1,512,128]{2,1,0:T(8,128)(2,1)S(1)}, bf16[1,512,128]{2,1,0:T(8,128)(2,1)S(1)}, u32[]{:S(2)}, u32[]{:S(2)}) collective-permute-start(bf16[1,512,128]{2,1,0:T(8,128)(2,1)S(1)} %get-tuple-element.38), channel_id=1, source_target_pairs={{0,2},{1,3},{2,0},{3,1},{4,6},{5,7},{6,4},{7,5},{8,10},{9,11},{10,... | collective-permute-start | bytes 393224 | tf_op jit(solution)/shard_map/ppermute | solution.py:68
  38.7 5.2 %collective-permute-done.refs_1_ = bf16[2,3,256,256]{3,2,1,0:T(8,128)(2,1)S(1)} collective-permute-done((bf16[2,3,256,256]{3,2,1,0:T(8,128)(2,1)S(1)}, bf16[2,3,256,256]{3,2,1,0:T(8,128)(2,1)S(1)}, u32[]{:S(2)}, u32[]{:S(2)}) %collective-permute-start) | collective-permute-done | bytes 786464 | tf_op jit(solution)/shard_map/ppermute | solution.py:68
  43.9 0.0 copy-done.2
  43.9 2.0 %early.1 = (bf16[2,3,256,1024]{3,2,1,0:T(8,128)(2,1)S(1)}, bf16[3,2,256,512]{3,2,1,0:T(8,128)(2,1)S(1)}) custom-call(s32[2,3]{1,0:T(2,128)S(1)} %bitcast.1, bf16[2,3,256,256]{3,2,1,0:T(8,128)(2,1)S(1)} %collective-permute-done.refs_1_, bf16[4,1024,512]{2,1,0:T(8,128)(2,1)S(1)} %get-tuple-element.34.refs_2_, ...), custom_call_target="tpu_custom_call", output_to_operand_aliasing={{0}: (3, {})} | custom-call | tf_op jit(solution)/shard_map/early/pallas_call | solution.py:34
  46.0 4.2 %collective-permute-done.6.refs_3_ = bf16[7,512,128]{2,1,0:T(8,128)(2,1)S(1)} collective-permute-done((bf16[7,512,128]{2,1,0:T(8,128)(2,1)S(1)}, bf16[7,512,128]{2,1,0:T(8,128)(2,1)S(1)}, u32[]{:S(2)}, u32[]{:S(2)}) %collective-permute-start.6) | collective-permute-done | bytes 917536 | tf_op jit(solution)/shard_map/ppermute | solution.py:64
  50.2 0.0 collective-permute-done.7.refs_5_
  50.2 0.0 collective-permute-start.8
  50.2 0.5 collective-permute-start.9
  50.7 2.1 %collective-permute-done.9.refs_6_ = bf16[1,512,128]{2,1,0:T(8,128)(2,1)S(1)} collective-permute-done((bf16[1,512,128]{2,1,0:T(8,128)(2,1)S(1)}, bf16[1,512,128]{2,1,0:T(8,128)(2,1)S(1)}, u32[]{:S(2)}, u32[]{:S(2)}) %collective-permute-start.9) | collective-permute-done | bytes 131104 | tf_op jit(solution)/shard_map/ppermute | solution.py:68
  52.9 0.0 collective-permute-done.8.refs_4_
  52.9 3.2 %late.1 = (bf16[3,2,256,1024]{3,2,1,0:T(8,128)(2,1)}, bf16[4,1024,512]{2,1,0:T(8,128)(2,1)S(1)}) custom-call(s32[2,3]{1,0:T(2,128)S(1)} %bitcast.2, bf16[2,3,256,1024]{3,2,1,0:T(8,128)(2,1)S(1)} %get-tuple-element.36.refs_1_, bf16[3,2,256,512]{3,2,1,0:T(8,128)(2,1)S(1)} %get-tuple-element.40.refs_2_, ...), custom_call_target="tpu_custom_call", output_to_operand_aliasing={{1}: (7, {})} | custom-call | tf_op jit(solution)/shard_map/late/pallas_call | solution.py:34
  (1 shorter events, 0.0 us)
Async XLA Ops:
  0.0 7.7 %copy-start = (bf16[2,1024,1024]{2,1,0:T(8,128)(2,1)S(1)}, bf16[2,1024,1024]{2,1,0:T(8,128)(2,1)}, u32[]{:S(2)}) copy-start(bf16[2,1024,1024]{2,1,0:T(8,128)(2,1)} %refs_0_.7) | copy-start | bytes 12582916
  0.0 7.7 %copy-start.1 = (bf16[3,2,1024,256]{3,2,1,0:T(8,128)(2,1)S(1)}, bf16[3,2,1024,256]{3,2,1,0:T(8,128)(2,1)}, u32[]{:S(2)}) copy-start(bf16[3,2,1024,256]{3,2,1,0:T(8,128)(2,1)} %refs_1_.5) | copy-start | bytes 9437188
  5.0 26.3 %collective-permute-start.3 = (bf16[8,512,128]{2,1,0:T(8,128)(2,1)S(1)}, bf16[8,512,128]{2,1,0:T(8,128)(2,1)S(1)}, u32[]{:S(2)}, u32[]{:S(2)}) collective-permute-start(bf16[8,512,128]{2,1,0:T(8,128)(2,1)S(1)} %get-tuple-element.31), channel_id=1, source_target_pairs={{4,0},{8,4},{12,8},{16,12},{20,16},{24,20},{28,24},{0,28},{5,1},{9... | collective-permute-start | bytes 3145736 | tf_op jit(solution)/shard_map/ppermute | solution.py:64
  7.7 20.5 %collective-permute-start.1 = (bf16[2,3,256,256]{3,2,1,0:T(8,128)(2,1)S(1)}, bf16[2,3,256,256]{3,2,1,0:T(8,128)(2,1)S(1)}, u32[]{:S(2)}, u32[]{:S(2)}) collective-permute-start(bf16[2,3,256,256]{3,2,1,0:T(8,128)(2,1)S(1)} %get-tuple-element.28.refs_2_), channel_id=1, source_target_pairs={{0,2},{1,3},{2,0},{3,1},{4,6},{5,7},{6,4},{7,5},{8,10},{9,11},{10,... | collective-permute-start | bytes 2359304 | tf_op jit(solution)/shard_map/ppermute | solution.py:68
  11.4 16.7 %collective-permute-start.2 = (bf16[2,3,256,256]{3,2,1,0:T(8,128)(2,1)S(1)}, bf16[2,3,256,256]{3,2,1,0:T(8,128)(2,1)S(1)}, u32[]{:S(2)}, u32[]{:S(2)}) collective-permute-start(bf16[2,3,256,256]{3,2,1,0:T(8,128)(2,1)S(1)} %get-tuple-element.29), channel_id=1, source_target_pairs={{0,1},{1,0},{2,3},{3,2},{4,5},{5,4},{6,7},{7,6},{8,9},{9,8},{10,11... | collective-permute-start | bytes 2359304 | tf_op jit(solution)/shard_map/ppermute | solution.py:68
  11.5 38.7 %collective-permute-start.6 = (bf16[7,512,128]{2,1,0:T(8,128)(2,1)S(1)}, bf16[7,512,128]{2,1,0:T(8,128)(2,1)S(1)}, u32[]{:S(2)}, u32[]{:S(2)}) collective-permute-start(bf16[7,512,128]{2,1,0:T(8,128)(2,1)S(1)} %get-tuple-element.37), channel_id=1, source_target_pairs={{4,0},{8,4},{12,8},{16,12},{20,16},{24,20},{28,24},{0,28},{5,1},{9... | collective-permute-start | bytes 2752520 | tf_op jit(solution)/shard_map/ppermute | solution.py:64
  15.4 28.6 %collective-permute-start = (bf16[2,3,256,256]{3,2,1,0:T(8,128)(2,1)S(1)}, bf16[2,3,256,256]{3,2,1,0:T(8,128)(2,1)S(1)}, u32[]{:S(2)}, u32[]{:S(2)}) collective-permute-start(bf16[2,3,256,256]{3,2,1,0:T(8,128)(2,1)S(1)} %get-tuple-element.27), channel_id=1, source_target_pairs={{0,3},{1,2},{2,1},{3,0},{4,7},{5,6},{6,5},{7,4},{8,11},{9,10},{10,... | collective-permute-start | bytes 2359304 | tf_op jit(solution)/shard_map/ppermute | solution.py:68
  31.3 2.0 %collective-permute-start.4 = (bf16[4,512,128]{2,1,0:T(8,128)(2,1)S(1)}, bf16[4,512,128]{2,1,0:T(8,128)(2,1)S(1)}, u32[]{:S(2)}, u32[]{:S(2)}) collective-permute-start(bf16[4,512,128]{2,1,0:T(8,128)(2,1)S(1)} %get-tuple-element.32.refs_4_), channel_id=1, source_target_pairs={{0,1},{1,0},{2,3},{3,2},{4,5},{5,4},{6,7},{7,6},{8,9},{9,8},{10,11... | collective-permute-start | bytes 1572872 | tf_op jit(solution)/shard_map/ppermute | solution.py:68
  31.4 2.6 %collective-permute-start.5 = (bf16[4,512,128]{2,1,0:T(8,128)(2,1)S(1)}, bf16[4,512,128]{2,1,0:T(8,128)(2,1)S(1)}, u32[]{:S(2)}, u32[]{:S(2)}) collective-permute-start(bf16[4,512,128]{2,1,0:T(8,128)(2,1)S(1)} %get-tuple-element.33.refs_6_), channel_id=1, source_target_pairs={{0,1},{1,0},{2,3},{3,2},{4,5},{5,4},{6,7},{7,6},{8,9},{9,8},{10,11... | collective-permute-start | bytes 1572872 | tf_op jit(solution)/shard_map/ppermute | solution.py:68
  34.0 9.9 %copy-start.2 = (s32[3,2]{0,1:T(2,128)S(1)}, s32[3,2]{0,1:T(2,128)}, u32[]{:S(2)}) copy-start(s32[3,2]{0,1:T(2,128)} %param.5) | copy-start | bytes 76
  35.9 14.3 %collective-permute-start.7 = (bf16[1,512,128]{2,1,0:T(8,128)(2,1)S(1)}, bf16[1,512,128]{2,1,0:T(8,128)(2,1)S(1)}, u32[]{:S(2)}, u32[]{:S(2)}) collective-permute-start(bf16[1,512,128]{2,1,0:T(8,128)(2,1)S(1)} %get-tuple-element.38), channel_id=1, source_target_pairs={{0,2},{1,3},{2,0},{3,1},{4,6},{5,7},{6,4},{7,5},{8,10},{9,11},{10,... | collective-permute-start | bytes 393224 | tf_op jit(solution)/shard_map/ppermute | solution.py:68
  50.2 2.7 %collective-permute-start.8 = (bf16[7,512,128]{2,1,0:T(8,128)(2,1)S(1)}, bf16[7,512,128]{2,1,0:T(8,128)(2,1)S(1)}, u32[]{:S(2)}, u32[]{:S(2)}) collective-permute-start(bf16[7,512,128]{2,1,0:T(8,128)(2,1)S(1)} %collective-permute-done.6.refs_3_), channel_id=1, source_target_pairs={{0,1},{1,0},{2,3},{3,2},{4,5},{5,4},{6,7},{7,6},{8,9},{9,8},{10,11... | collective-permute-start | bytes 2752520 | tf_op jit(solution)/shard_map/ppermute | solution.py:68
  50.2 2.7 %collective-permute-start.9 = (bf16[1,512,128]{2,1,0:T(8,128)(2,1)S(1)}, bf16[1,512,128]{2,1,0:T(8,128)(2,1)S(1)}, u32[]{:S(2)}, u32[]{:S(2)}) collective-permute-start(bf16[1,512,128]{2,1,0:T(8,128)(2,1)S(1)} %collective-permute-done.7.refs_5_), channel_id=1, source_target_pairs={{0,1},{1,0},{2,3},{3,2},{4,5},{5,4},{6,7},{7,6},{8,9},{9,8},{10,11... | collective-permute-start | bytes 393224 | tf_op jit(solution)/shard_map/ppermute | solution.py:68

commit v4 on v3

--- a/solution.py
+++ b/solution.py
@@ -69,19 +69,17 @@
 
 
 def part_copies(blocks, unit, place, basis, array, sems):
-    slabs = lax.axis_size("slab")
-    rows = basis.shape[1] // slabs
+    rows = basis.shape[1] // lax.axis_size("slab")
     copies = []
-    for at, (sector, start) in enumerate(blocks):
-        for slab in range(slabs // 2):
-            row = pl.multiple_of((2 * slab + place[0] % 2) * rows, rows)
-            copies.append(
-                pltpu.make_async_copy(
-                    basis.at[sector, pl.ds(row, rows), pl.ds(first_column(start, place, unit), unit)],
-                    array.at[at, pl.ds(slab * rows, rows)],
-                    sems.at[len(copies)],
-                )
+    for at, (sector, start, slab) in enumerate(blocks):
+        row = pl.multiple_of((2 * slab + place[0] % 2) * rows, rows)
+        copies.append(
+            pltpu.make_async_copy(
+                basis.at[sector, pl.ds(row, rows), pl.ds(first_column(start, place, unit), unit)],
+                array.at[at],
+                sems.at[len(copies)],
             )
+        )
     return copies
 
 
@@ -133,7 +131,7 @@
 
 def basis_part(basis, fermion, blocks, unit, distances):
     flavours, sectors, depth, width = fermion.shape
-    shapes = [pltpu.VMEM((len(blocks), depth // 2, unit), jnp.bfloat16)]
+    shapes = [pltpu.VMEM((len(blocks), width, unit), jnp.bfloat16)]
     shapes += [pltpu.VMEM((sectors, flavours, width, width), jnp.bfloat16)] * len(distances)
     return kernel_call(
         functools.partial(part_kernel, blocks, unit, distances),
@@ -146,7 +144,7 @@
         [
             pltpu.VMEM((sectors, depth, depth), jnp.bfloat16),
             pltpu.VMEM((flavours, sectors, depth, width), jnp.bfloat16),
-            pltpu.SemaphoreType.DMA((len(blocks) * lax.axis_size("slab") // 2,)),
+            pltpu.SemaphoreType.DMA((len(blocks),)),
             pltpu.SemaphoreType.DMA((sectors, 2)),
         ],
     )
@@ -192,9 +190,9 @@
         [in_vmem(basis), in_vmem(fermion), in_vmem(after)],
         [WHOLE, WHOLE, WHOLE],
         [pltpu.VMEM((sectors, flavours, width, width), jnp.bfloat16)] * len(distances)
-        + [pltpu.VMEM((len(blocks), depth // 2, unit), jnp.bfloat16)],
+        + [pltpu.VMEM((len(blocks), width, unit), jnp.bfloat16)],
         [WHOLE] * (len(distances) + 1),
-        [pltpu.SemaphoreType.DMA((len(blocks) * lax.axis_size("slab") // 2,))],
+        [pltpu.SemaphoreType.DMA((len(blocks),))],
     )
 
 
@@ -235,22 +233,20 @@
     return copies
 
 
-def next_copies(nexts, place, pairs, right, sems, first):
+def next_copies(nexts, place, arrays, side, right, sems, first):
     sectors, depth = right.shape[0] // 2, right.shape[1]
     copies = []
-    for pair, holds in zip(pairs, nexts):
-        for index, many, sector, column in holds:
-            for side in range(2):
-                to = pl.multiple_of(((place[0] + side) % 2) * (depth // 2), depth // 2)
-                copies.append(
-                    pltpu.make_async_copy(
-                        pair[side].at[pl.ds(index, many)],
-                        right.at[
-                            pl.ds(sectors + sector, many), pl.ds(to, depth // 2), pl.ds(column, pair[side].shape[2])
-                        ],
-                        sems.at[first + len(copies)],
-                    )
+    for array, blocks in zip(arrays, nexts):
+        _, rows, columns = array.shape
+        for index, (sector, slab, column) in enumerate(blocks):
+            to = pl.multiple_of(((place[0] + side) % 2) * (depth // 2) + slab * rows, rows)
+            copies.append(
+                pltpu.make_async_copy(
+                    array.at[index],
+                    right.at[sectors + sector, pl.ds(to, rows), pl.ds(column, columns)],
+                    sems.at[first + len(copies)],
                 )
+            )
     return copies
 
 
@@ -262,40 +258,40 @@
     return pltpu.make_async_copy(half, left.at[:, :, :, pl.ds(column, width)], sem)
 
 
-def gather_kernel(early_units, late_units, nexts, unit, distances, cut, place, basis, *refs):
+def gather_kernel(groups, nexts, unit, distances, cuts, place, basis, *refs):
     halves, refs = refs[: len(distances)], refs[len(distances) :]
     pairs, refs = [refs[2 * i : 2 * i + 2] for i in range(len(nexts))], refs[2 * len(nexts) :]
-    left, early_right, late_right, sent, sems = refs
-    copies = own_copies(early_units, unit, place, basis, early_right, sems, 0)
-    copies += next_copies(nexts, place, pairs, early_right, sems, len(copies))
-    copies += own_copies(late_units, unit, place, basis, late_right, sems, len(copies))
+    left, *rights, sent, sems = refs
+    copies = next_copies(nexts, place, [pair[0] for pair in pairs], 0, rights[0], sems, 0)
+    copies += next_copies(nexts, place, [pair[1] for pair in pairs], 1, rights[0], sems, len(copies))
+    for units, right in zip(groups, rights):
+        copies += own_copies(units, unit, place, basis, right, sems, len(copies))
     for half, distance in zip(halves, distances):
         copies.append(half_copy(half, distance, place, left, sems.at[len(copies)]))
-    copies.append(pltpu.make_async_copy(pairs[-1][0].at[cut], sent, sems.at[len(copies)]))
+    for at, cut in enumerate(cuts):
+        copies.append(pltpu.make_async_copy(pairs[-1][0].at[cut], sent.at[at], sems.at[len(copies)]))
     run(copies)
 
 
-def gather(basis, early_units, late_units, nexts, unit, pairs, halves, distances, cut):
+def gather(basis, groups, nexts, unit, pairs, halves, distances, cuts):
     sectors, depth, _ = basis.shape
     flavours, width = halves[0].shape[1:3]
     given = [in_vmem(array) for array in (basis, *halves, *(array for pair in pairs for array in pair))]
-    early_columns, late_columns = (sum(count for _, count in units) * unit for units in (early_units, late_units))
-    copies = (len(early_units) + len(late_units)) * (depth // width) + 2 * sum(len(holds) for holds in nexts)
+    copies = sum(map(len, groups)) * (depth // width) + 2 * sum(len(holds) for holds in nexts)
     last = pairs[-1][0]
-    return kernel_call(
-        functools.partial(gather_kernel, early_units, late_units, nexts, unit, distances, cut),
+    shapes = [pltpu.VMEM((sectors, flavours, width, depth), jnp.bfloat16)]
+    for units in groups:
+        shapes.append(pltpu.VMEM((2 * sectors, depth, sum(count for _, count in units) * unit), jnp.bfloat16))
+    shapes.append(pltpu.VMEM((len(cuts), *last.shape[1:]), jnp.bfloat16))
+    return kernel_call(
+        functools.partial(gather_kernel, groups, nexts, unit, distances, cuts),
         "gather",
         basis.shape[:2],
         given,
         [WHOLE] * len(given),
-        [
-            pltpu.VMEM((sectors, flavours, width, depth), jnp.bfloat16),
-            pltpu.VMEM((2 * sectors, depth, early_columns), jnp.bfloat16),
-            pltpu.VMEM((2 * sectors, depth, late_columns), jnp.bfloat16),
-            pltpu.VMEM((cut.size, *last.shape[1:]), jnp.bfloat16),
-        ],
-        [WHOLE] * 4,
-        [pltpu.SemaphoreType.DMA((copies + len(halves) + 1,))],
+        shapes,
+        [WHOLE] * len(shapes),
+        [pltpu.SemaphoreType.DMA((copies + len(halves) + len(cuts),))],
     )
 
 
@@ -330,29 +326,80 @@
     )
 
 
-def late_kernel(early_units, units, nexts, unit, place, partner, left, early, *refs):
-    pairs, refs = [refs[2 * i : 2 * i + 2] for i in range(len(nexts))], refs[2 * len(nexts) :]
-    _, out, right, stage, sems, early_sems, out_sems = refs
+def partial(place, partner, sector, flavour, side, left, right):
+    index = (partner[...][sector, flavour] - place[1] + place[2]) % place[2]
+    depth = right.shape[1]
+    half = pl.ds(pl.multiple_of(((place[0] + side) % 2) * (depth // 2), depth // 2), depth // 2)
+    return jnp.dot(left[sector, flavour, :, half], right[index, half, :], preferred_element_type=jnp.float32)
+
+
+def own_rows_kernel(groups, place, partner, left, *refs):
+    arrays = []
+    for nexts in groups:
+        arrays.append(refs[: len(nexts)])
+        refs = refs[len(nexts) :]
+    refs = refs[len(groups) :]
+    totals, rights, sems = refs[: len(groups)], refs[len(groups) : 2 * len(groups)], refs[2 * len(groups) :]
+    copies = [
+        next_copies(nexts, place, here, 0, right, sem, 0)
+        for nexts, here, right, sem in zip(groups, arrays, rights, sems)
+    ]
+    for group in copies:
+        for copy in group:
+            copy.start()
     sectors, flavours = left.shape[:2]
-    next_here = next_copies(nexts, place, pairs, right, sems, 0)
+    for group, total, right in zip(copies, totals, rights):
+        for copy in group:
+            copy.wait()
+        for sector in range(sectors):
+            for flavour in range(flavours):
+                total[flavour, sector] = partial(place, partner, sector, flavour, 0, left, right)
+
+
+def own_rows(partner, groups, arrays, left, rights):
+    sectors, flavours, width, depth = left.shape
+    given = [in_vmem(array) for array in (left, *(array for group in arrays for array in group), *rights)]
+    first = 1 + len(given) - len(rights)
+    return kernel_call(
+        functools.partial(own_rows_kernel, groups),
+        "own_rows",
+        (sectors, depth),
+        [partner, *given],
+        [WHOLE] * (1 + len(given)),
+        [pltpu.VMEM((flavours, sectors, width, right.shape[2]), jnp.float32) for right in rights]
+        + [pltpu.VMEM(right.shape, right.dtype) for right in rights],
+        [WHOLE] * (2 * len(rights)),
+        [pltpu.SemaphoreType.DMA((sum(map(len, nexts)),)) for nexts in groups],
+        {first + at: len(rights) + at for at in range(len(rights))},
+    )
+
+
+def late_kernel(earlier_units, units, nexts, unit, place, partner, left, total, *refs):
+    earlier, refs = refs[: len(earlier_units)], refs[len(earlier_units) :]
+    arrays, (_, out, right, stage, sems, early_sems, out_sems) = refs[: len(nexts)], refs[len(nexts) :]
+    sectors, flavours = left.shape[:2]
+    next_here = next_copies(nexts, place, arrays, 1, right, sems, 0)
     for copy in next_here:
         copy.start()
-    out_copies, at = [], 0
-    for start, count in early_units:
-        out_copies.append(
-            pltpu.make_async_copy(
-                early.at[:, :, :, pl.ds(at, count * unit)],
-                out.at[:, :, :, pl.ds(first_column(start, place, unit), count * unit)],
-                early_sems.at[len(out_copies)],
+    out_copies = []
+    for result, spans in zip(earlier, earlier_units):
+        at = 0
+        for start, count in spans:
+            out_copies.append(
+                pltpu.make_async_copy(
+                    result.at[:, :, :, pl.ds(at, count * unit)],
+                    out.at[:, :, :, pl.ds(first_column(start, place, unit), count * unit)],
+                    early_sems.at[len(out_copies)],
+                )
             )
-        )
-        out_copies[-1].start()
-        at += count * unit
+            out_copies[-1].start()
+            at += count * unit
     for copy in next_here:
         copy.wait()
     for sector in range(sectors):
         for flavour in range(flavours):
-            stage[flavour, sector] = product(place, partner, sector, flavour, left, right)
+            rest = partial(place, partner, sector, flavour, 1, left, right)
+            stage[flavour, sector] = (total[flavour, sector] + rest).astype(jnp.bfloat16)
             at = 0
             for number, (start, count) in enumerate(units):
                 copy = pltpu.make_async_copy(
@@ -367,15 +414,15 @@
         copy.wait()
 
 
-def late_products(partner, early_units, units, nexts, unit, pairs, left, early, right):
+def late_products(partner, groups, nexts, unit, arrays, left, total, earlier, right):
     sectors, flavours, width, depth = left.shape
-    given = [in_vmem(array) for array in (left, early, *(array for pair in pairs for array in pair), right)]
-    return kernel_call(
-        functools.partial(late_kernel, early_units, units, nexts, unit),
+    given = [in_vmem(array) for array in (left, total, *earlier, *arrays, right)]
+    return kernel_call(
+        functools.partial(late_kernel, groups[:-1], groups[-1], nexts, unit),
         "late",
         (sectors, depth),
         [partner, *given],
-        [WHOLE] + [WHOLE] * len(given),
+        [WHOLE] * (1 + len(given)),
         [
             pltpu.HBM((flavours, sectors, width, depth), jnp.bfloat16),
             pltpu.VMEM(right.shape, right.dtype),
@@ -383,9 +430,9 @@
         [ANY, WHOLE],
         [
             pltpu.VMEM((flavours, sectors, width, right.shape[2]), jnp.bfloat16),
-            pltpu.SemaphoreType.DMA((2 * sum(len(holds) for holds in nexts),)),
-            pltpu.SemaphoreType.DMA((len(early_units),)),
-            pltpu.SemaphoreType.DMA((sectors * flavours, len(units))),
+            pltpu.SemaphoreType.DMA((sum(map(len, nexts)),)),
+            pltpu.SemaphoreType.DMA((sum(map(len, groups[:-1])),)),
+            pltpu.SemaphoreType.DMA((sectors * flavours, len(groups[-1]))),
         ],
         {len(given): 1},
     )[0]
@@ -396,38 +443,43 @@
     unit = depth // 8
     partner = partner.T
     distances = (3, 2, 1, 0)
-    alone = sectors // 2
+    slabs = range(lax.axis_size("slab") // 2)
+    held = [(sector, slab) for sector in range(sectors) for slab in slabs]
+    alone = len(held) // 4
     count = 3
-    early_units, late_units = ((0, count), (OWN, 1)), ((count, 6 - count), (OTHER, 1))
-    first_blocks = [(sector, start) for start in (*range(count), OWN) for sector in range(sectors)]
-    last_blocks = [(sector, start) for start in range(count, 6) for sector in range(sectors)]
-    last_blocks += [(sector, OTHER) for sector in range(alone)]
+    units = ((0, count), (OWN, 1)), ((count, 6 - count), (OTHER, 1))
+    first_blocks = [(sector, start, slab) for start in (*range(count), OWN) for sector, slab in held]
+    last_blocks = [(sector, start, slab) for start in range(count, 6) for sector, slab in held]
+    last_blocks += [(sector, OTHER, slab) for sector, slab in held[:alone]]
     first_part, *far = basis_part(basis, fermion, first_blocks, unit, distances[:2])
     first = previous(first_part)
     far3, far2 = far_blocks(basis, fermion, distances[:2], far)
     got2, got3 = swapped(far2, 2), swapped(far3, 3)
     mine, near, last_part = near_blocks(basis, fermion, last_blocks, unit, distances[2:], far2)
     beside, last = swapped(mine, 1), previous(last_part)
+
+    def columns(begin, end):
+        return [(sector, slab, at * unit) for at in range(begin, end) for sector, slab in held]
+
     groups = ((0, 2), (2, 4))
-    pieces = cut_out(first, [slice(begin * sectors, end * sectors) for begin, end in groups], (beside, got2))
+    pieces = cut_out(first, [slice(begin * len(held), end * len(held)) for begin, end in groups], (beside, got2))
     pairs = [(piece, swapped(piece, 1)) for piece in pieces]
-    nexts = [
-        [((at - begin) * sectors, sectors, 0, at * unit) for at in range(begin, end)] for begin, end in groups
-    ]
-    begin, end = groups[-1]
-    cut = pl.ds((end - 1 - begin) * sectors + alone, sectors - alone)
+    nexts = [columns(*group) for group in groups]
+    cuts = range(len(nexts[-1]) - len(held) + alone, len(nexts[-1]))
     left, early_right, late_right, sent = gather(
-        basis, early_units, late_units, nexts, unit, pairs, [got2, beside, near], distances[1:], cut
+        basis, units, nexts, unit, pairs, [got2, beside, near], distances[1:], cuts
     )
     other = swapped(sent, 2)
     left, early = early_products(partner, got3, distances[0], left, early_right)
-    nexts = [[(at * sectors, sectors, 0, at * unit) for at in range(6 - count)]]
-    if alone:
-        nexts[0].append(((6 - count) * sectors, alone, 0, (6 - count) * unit))
-    nexts.append([(0, sectors - alone, alone, (6 - count) * unit)])
     last, other, early = lax.optimization_barrier((last, other, early))
-    pairs = [(last, swapped(last, 1)), (other, swapped(other, 1))]
-    return late_products(partner, early_units, late_units, nexts, unit, pairs, left, early, late_right)
+    last_other, other_other = swapped(last, 1), swapped(other, 1)
+    full = columns(0, 6 - count + 1)
+    split = len(full) - len(held) + alone
+    nexts = [full[:split], full[split:]]
+    total, late_right = own_rows(partner, [nexts], [[last, other]], left, [late_right])
+    return late_products(
+        partner, units, nexts, unit, [last_other, other_other], left, total, [early], late_right
+    )
 
 
 def solution(mesh):

time: 56.2 us -> 53.9 us (0.959)
  waiting for transfers between devices: 29.2 us -> 26 us
  Pallas kernels: 14.4 us -> 15.3 us
    ppermute x8, waiting for transfers between devices: 21.9 us -> 20.1 us  [swapped(): lax.ppermute(block, 'slab', [(i, i ^ distance) for i in range(lax.axis_si...]
    ppermute x2, waiting for transfers between devices: 7.3 us -> 5.85 us  [previous(): lax.ppermute(block, 'sec', [((i + 1) % count, i) for i in range(count)])]
    pallas_call x7 -> x8, Pallas kernels: 14.4 us -> 15.3 us  [kernel_call(): pl.pallas_call(kernel, out_shape=shapes, in_specs=specs, out_specs=out_sp...]
  transfers between devices with their start and end apart: 10 -> 10, of which waited for: 7 -> 7; matrix products, arithmetic and copies ran while one was open for 0% -> 0% of each run, Pallas kernels for 11% -> 15%
where the time goes in v4:
time: 53.9 us; the launch traced here: 53.8 us
  waiting for transfers between devices  26 us (48%)
  Pallas kernels  15.3 us (28%)
  starting transfers between devices  12.4 us (23%)
    ppermute x8, waiting for transfers between devices, swapped(): lax.ppermute(block, 'slab', [(i, i ^ distance) for i in range(lax.axis_si...  20.1 us
    pallas_call x8, Pallas kernels, kernel_call(): pl.pallas_call(kernel, out_shape=shapes, in_specs=specs, out_specs=out_sp...  15.3 us
    ppermute x2, starting transfers between devices, previous(): lax.ppermute(block, 'sec', [((i + 1) % count, i) for i in range(count)])  6.59 us
    ppermute x8, starting transfers between devices, swapped(): lax.ppermute(block, 'slab', [(i, i ^ distance) for i in range(lax.axis_si...  5.85 us
    ppermute x2, waiting for transfers between devices, previous(): lax.ppermute(block, 'sec', [((i + 1) % count, i) for i in range(count)])  5.85 us
  transfers between devices with their start and end apart: 10, of which 7 were waited for; matrix products, arithmetic and copies ran while one was open for 0% of the time, Pallas kernels for 15%

profile of v4, /device:TPU:0, one launch (start us, length us, event | category | flops | bytes accessed | tf_op | source)
XLA Modules:
  0.0 53.8 jit_solution(14608419946040772789)
XLA Ops:
  0.0 0.0 copy-start
  0.0 0.0 copy-start.1
  0.0 5.0 %part.1 = (bf16[16,256,128]{2,1,0:T(8,128)(2,1)S(1)}, bf16[2,3,256,256]{3,2,1,0:T(8,128)(2,1)S(1)}, bf16[2,3,256,256]{3,2,1,0:T(8,128)(2,1)S(1)}) custom-call(bf16[2,1024,1024]{2,1,0:T(8,128)(2,1)} %refs_0_.7, bf16[3,2,1024,256]{3,2,1,0:T(8,128)(2,1)} %refs_1_.5), custom_call_target="tpu_custom_call" | custom-call | tf_op jit(solution)/shard_map/part/pallas_call | solution.py:34
  5.0 2.7 %collective-permute-start.3 = (bf16[16,256,128]{2,1,0:T(8,128)(2,1)S(1)}, bf16[16,256,128]{2,1,0:T(8,128)(2,1)S(1)}, u32[]{:S(2)}, u32[]{:S(2)}) collective-permute-start(bf16[16,256,128]{2,1,0:T(8,128)(2,1)S(1)} %get-tuple-element.33), channel_id=1, source_target_pairs={{4,0},{8,4},{12,8},{16,12},{20,16},{24,20},{28,24},{0,28},{5,1},{9... | collective-permute-start | bytes 3145736 | tf_op jit(solution)/shard_map/ppermute | solution.py:64
  7.7 0.0 copy-done
  7.7 0.0 copy-done.1
  7.7 1.5 %collective-permute-start.1 = (bf16[2,3,256,256]{3,2,1,0:T(8,128)(2,1)S(1)}, bf16[2,3,256,256]{3,2,1,0:T(8,128)(2,1)S(1)}, u32[]{:S(2)}, u32[]{:S(2)}) collective-permute-start(bf16[2,3,256,256]{3,2,1,0:T(8,128)(2,1)S(1)} %get-tuple-element.30.refs_2_), channel_id=1, source_target_pairs={{0,2},{1,3},{2,0},{3,1},{4,6},{5,7},{6,4},{7,5},{8,10},{9,11},{10,... | collective-permute-start | bytes 2359304 | tf_op jit(solution)/shard_map/ppermute | solution.py:68
  9.2 2.2 %near.1 = (bf16[2,3,256,256]{3,2,1,0:T(8,128)(2,1)S(1)}, bf16[2,3,256,256]{3,2,1,0:T(8,128)(2,1)S(1)}, bf16[13,256,128]{2,1,0:T(8,128)(2,1)S(1)}) custom-call(bf16[2,1024,1024]{2,1,0:T(8,128)(2,1)S(1)} %copy-done, bf16[3,2,1024,256]{3,2,1,0:T(8,128)(2,1)S(1)} %copy-done.1, bf16[2,3,256,256]{3,2,1,0:T(8,128)(2,1)S(1)} %get-tuple-element.30.refs_2_), custom_call_target="tpu_custom_call" | custom-call | tf_op jit(solution)/shard_map/near/pallas_call | solution.py:34
  11.4 0.1 collective-permute-start.2
  11.4 3.9 %collective-permute-start.6 = (bf16[13,256,128]{2,1,0:T(8,128)(2,1)S(1)}, bf16[13,256,128]{2,1,0:T(8,128)(2,1)S(1)}, u32[]{:S(2)}, u32[]{:S(2)}) collective-permute-start(bf16[13,256,128]{2,1,0:T(8,128)(2,1)S(1)} %get-tuple-element.39), channel_id=1, source_target_pairs={{4,0},{8,4},{12,8},{16,12},{20,16},{24,20},{28,24},{0,28},{5,1},{9... | collective-permute-start | bytes 2555912 | tf_op jit(solution)/shard_map/ppermute | solution.py:64
  15.3 0.4 collective-permute-start
  15.7 12.4 %collective-permute-done.1.refs_2_.refs_1_ = bf16[2,3,256,256]{3,2,1,0:T(8,128)(2,1)S(1)} collective-permute-done((bf16[2,3,256,256]{3,2,1,0:T(8,128)(2,1)S(1)}, bf16[2,3,256,256]{3,2,1,0:T(8,128)(2,1)S(1)}, u32[]{:S(2)}, u32[]{:S(2)}) %collective-permute-start.1) | collective-permute-done | bytes 786464 | tf_op jit(solution)/shard_map/ppermute | solution.py:68
  28.1 0.0 collective-permute-done.2.refs_1_.refs_2_
  28.1 3.1 %collective-permute-done.3.refs_0_ = bf16[16,256,128]{2,1,0:T(8,128)(2,1)S(1)} collective-permute-done((bf16[16,256,128]{2,1,0:T(8,128)(2,1)S(1)}, bf16[16,256,128]{2,1,0:T(8,128)(2,1)S(1)}, u32[]{:S(2)}, u32[]{:S(2)}) %collective-permute-start.3) | collective-permute-done | bytes 1048608 | tf_op jit(solution)/shard_map/ppermute | solution.py:64
  31.2 0.1 cut.1
  31.3 0.1 collective-permute-start.4
  31.4 0.5 collective-permute-start.5
  31.9 1.4 %collective-permute-done.4.refs_5_ = bf16[8,256,128]{2,1,0:T(8,128)(2,1)S(1)} collective-permute-done((bf16[8,256,128]{2,1,0:T(8,128)(2,1)S(1)}, bf16[8,256,128]{2,1,0:T(8,128)(2,1)S(1)}, u32[]{:S(2)}, u32[]{:S(2)}) %collective-permute-start.4) | collective-permute-done | bytes 524320 | tf_op jit(solution)/shard_map/ppermute | solution.py:68
  33.3 0.7 %collective-permute-done.5.refs_7_ = bf16[8,256,128]{2,1,0:T(8,128)(2,1)S(1)} collective-permute-done((bf16[8,256,128]{2,1,0:T(8,128)(2,1)S(1)}, bf16[8,256,128]{2,1,0:T(8,128)(2,1)S(1)}, u32[]{:S(2)}, u32[]{:S(2)}) %collective-permute-start.5) | collective-permute-done | bytes 524320 | tf_op jit(solution)/shard_map/ppermute | solution.py:68
  34.0 0.0 copy-start.2
  34.0 2.3 %gather.1 = (bf16[2,3,256,1024]{3,2,1,0:T(8,128)(2,1)S(1)}, bf16[4,1024,512]{2,1,0:T(8,128)(2,1)S(1)}, bf16[4,1024,512]{2,1,0:T(8,128)(2,1)S(1)}, bf16[3,256,128]{2,1,0:T(8,128)(2,1)S(1)}) custom-call(bf16[2,1024,1024]{2,1,0:T(8,128)(2,1)S(1)} %copy-done, bf16[2,3,256,256]{3,2,1,0:T(8,128)(2,1)S(1)} %collective-permute-done.1.refs_2_.refs_1_, ...), custom_call_target="tpu_custom_call" | custom-call | tf_op jit(solution)/shard_map/gather/pallas_call | solution.py:34
  36.3 2.8 %collective-permute-start.7 = (bf16[3,256,128]{2,1,0:T(8,128)(2,1)S(1)}, bf16[3,256,128]{2,1,0:T(8,128)(2,1)S(1)}, u32[]{:S(2)}, u32[]{:S(2)}) collective-permute-start(bf16[3,256,128]{2,1,0:T(8,128)(2,1)S(1)} %get-tuple-element.40), channel_id=1, source_target_pairs={{0,2},{1,3},{2,0},{3,1},{4,6},{5,7},{6,4},{7,5},{8,10},{9,11},{10,... | collective-permute-start | bytes 589832 | tf_op jit(solution)/shard_map/ppermute | solution.py:68
  39.1 4.8 %collective-permute-done.refs_1_ = bf16[2,3,256,256]{3,2,1,0:T(8,128)(2,1)S(1)} collective-permute-done((bf16[2,3,256,256]{3,2,1,0:T(8,128)(2,1)S(1)}, bf16[2,3,256,256]{3,2,1,0:T(8,128)(2,1)S(1)}, u32[]{:S(2)}, u32[]{:S(2)}) %collective-permute-start) | collective-permute-done | bytes 786464 | tf_op jit(solution)/shard_map/ppermute | solution.py:68
  44.0 0.0 copy-done.2
  44.0 2.0 %early.1 = (bf16[2,3,256,1024]{3,2,1,0:T(8,128)(2,1)S(1)}, bf16[3,2,256,512]{3,2,1,0:T(8,128)(2,1)S(1)}) custom-call(s32[2,3]{1,0:T(2,128)S(1)} %bitcast.1, bf16[2,3,256,256]{3,2,1,0:T(8,128)(2,1)S(1)} %collective-permute-done.refs_1_, bf16[4,1024,512]{2,1,0:T(8,128)(2,1)S(1)} %get-tuple-element.36.refs_2_, ...), custom_call_target="tpu_custom_call", output_to_operand_aliasing={{0}: (3, {})} | custom-call | tf_op jit(solution)/shard_map/early/pallas_call | solution.py:34
  46.0 2.8 %collective-permute-done.6.refs_2_ = bf16[13,256,128]{2,1,0:T(8,128)(2,1)S(1)} collective-permute-done((bf16[13,256,128]{2,1,0:T(8,128)(2,1)S(1)}, bf16[13,256,128]{2,1,0:T(8,128)(2,1)S(1)}, u32[]{:S(2)}, u32[]{:S(2)}) %collective-permute-start.6) | collective-permute-done | bytes 852000 | tf_op jit(solution)/shard_map/ppermute | solution.py:64
  48.8 0.0 collective-permute-done.7.refs_3_
  48.8 0.0 collective-permute-start.8
  48.8 0.5 collective-permute-start.9
  49.3 1.4 %own_rows.1 = (f32[3,2,256,512]{3,2,1,0:T(8,128)S(1)}, bf16[4,1024,512]{2,1,0:T(8,128)(2,1)S(1)}) custom-call(s32[2,3]{1,0:T(2,128)S(1)} %bitcast.2, bf16[2,3,256,1024]{3,2,1,0:T(8,128)(2,1)S(1)} %get-tuple-element.38.refs_1_, bf16[13,256,128]{2,1,0:T(8,128)(2,1)S(1)} %collective-permute-done.6.refs_2_, ...), custom_call_target="tpu_custom_call", output_to_operand_aliasing={{1}: (4, {})} | custom-call | tf_op jit(solution)/shard_map/own_rows/pallas_call | solution.py:34
  50.7 0.7 %collective-permute-done.9.refs_5_ = bf16[3,256,128]{2,1,0:T(8,128)(2,1)S(1)} collective-permute-done((bf16[3,256,128]{2,1,0:T(8,128)(2,1)S(1)}, bf16[3,256,128]{2,1,0:T(8,128)(2,1)S(1)}, u32[]{:S(2)}, u32[]{:S(2)}) %collective-permute-start.9) | collective-permute-done | bytes 196640 | tf_op jit(solution)/shard_map/ppermute | solution.py:68
  51.5 0.0 collective-permute-done.8.refs_4_
  51.5 2.3 %late.1 = (bf16[3,2,256,1024]{3,2,1,0:T(8,128)(2,1)}, bf16[4,1024,512]{2,1,0:T(8,128)(2,1)S(1)}) custom-call(s32[2,3]{1,0:T(2,128)S(1)} %bitcast.3, bf16[2,3,256,1024]{3,2,1,0:T(8,128)(2,1)S(1)} %get-tuple-element.38.refs_1_, f32[3,2,256,512]{3,2,1,0:T(8,128)S(1)} %get-tuple-element.45.refs_2_, ...), custom_call_target="tpu_custom_call", output_to_operand_aliasing={{1}: (6, {})} | custom-call | tf_op jit(solution)/shard_map/late/pallas_call | solution.py:34
  (1 shorter events, 0.0 us)
Async XLA Ops:
  0.0 7.7 %copy-start = (bf16[2,1024,1024]{2,1,0:T(8,128)(2,1)S(1)}, bf16[2,1024,1024]{2,1,0:T(8,128)(2,1)}, u32[]{:S(2)}) copy-start(bf16[2,1024,1024]{2,1,0:T(8,128)(2,1)} %refs_0_.7) | copy-start | bytes 12582916
  0.0 7.7 %copy-start.1 = (bf16[3,2,1024,256]{3,2,1,0:T(8,128)(2,1)S(1)}, bf16[3,2,1024,256]{3,2,1,0:T(8,128)(2,1)}, u32[]{:S(2)}) copy-start(bf16[3,2,1024,256]{3,2,1,0:T(8,128)(2,1)} %refs_1_.5) | copy-start | bytes 9437188
  5.0 26.3 %collective-permute-start.3 = (bf16[16,256,128]{2,1,0:T(8,128)(2,1)S(1)}, bf16[16,256,128]{2,1,0:T(8,128)(2,1)S(1)}, u32[]{:S(2)}, u32[]{:S(2)}) collective-permute-start(bf16[16,256,128]{2,1,0:T(8,128)(2,1)S(1)} %get-tuple-element.33), channel_id=1, source_target_pairs={{4,0},{8,4},{12,8},{16,12},{20,16},{24,20},{28,24},{0,28},{5,1},{9... | collective-permute-start | bytes 3145736 | tf_op jit(solution)/shard_map/ppermute | solution.py:64
  7.7 20.5 %collective-permute-start.1 = (bf16[2,3,256,256]{3,2,1,0:T(8,128)(2,1)S(1)}, bf16[2,3,256,256]{3,2,1,0:T(8,128)(2,1)S(1)}, u32[]{:S(2)}, u32[]{:S(2)}) collective-permute-start(bf16[2,3,256,256]{3,2,1,0:T(8,128)(2,1)S(1)} %get-tuple-element.30.refs_2_), channel_id=1, source_target_pairs={{0,2},{1,3},{2,0},{3,1},{4,6},{5,7},{6,4},{7,5},{8,10},{9,11},{10,... | collective-permute-start | bytes 2359304 | tf_op jit(solution)/shard_map/ppermute | solution.py:68
  11.4 16.8 %collective-permute-start.2 = (bf16[2,3,256,256]{3,2,1,0:T(8,128)(2,1)S(1)}, bf16[2,3,256,256]{3,2,1,0:T(8,128)(2,1)S(1)}, u32[]{:S(2)}, u32[]{:S(2)}) collective-permute-start(bf16[2,3,256,256]{3,2,1,0:T(8,128)(2,1)S(1)} %get-tuple-element.31), channel_id=1, source_target_pairs={{0,1},{1,0},{2,3},{3,2},{4,5},{5,4},{6,7},{7,6},{8,9},{9,8},{10,11... | collective-permute-start | bytes 2359304 | tf_op jit(solution)/shard_map/ppermute | solution.py:68
  11.4 37.3 %collective-permute-start.6 = (bf16[13,256,128]{2,1,0:T(8,128)(2,1)S(1)}, bf16[13,256,128]{2,1,0:T(8,128)(2,1)S(1)}, u32[]{:S(2)}, u32[]{:S(2)}) collective-permute-start(bf16[13,256,128]{2,1,0:T(8,128)(2,1)S(1)} %get-tuple-element.39), channel_id=1, source_target_pairs={{4,0},{8,4},{12,8},{16,12},{20,16},{24,20},{28,24},{0,28},{5,1},{9... | collective-permute-start | bytes 2555912 | tf_op jit(solution)/shard_map/ppermute | solution.py:64
  15.3 28.6 %collective-permute-start = (bf16[2,3,256,256]{3,2,1,0:T(8,128)(2,1)S(1)}, bf16[2,3,256,256]{3,2,1,0:T(8,128)(2,1)S(1)}, u32[]{:S(2)}, u32[]{:S(2)}) collective-permute-start(bf16[2,3,256,256]{3,2,1,0:T(8,128)(2,1)S(1)} %get-tuple-element.29), channel_id=1, source_target_pairs={{0,3},{1,2},{2,1},{3,0},{4,7},{5,6},{6,5},{7,4},{8,11},{9,10},{10,... | collective-permute-start | bytes 2359304 | tf_op jit(solution)/shard_map/ppermute | solution.py:68
  31.3 2.0 %collective-permute-start.4 = (bf16[8,256,128]{2,1,0:T(8,128)(2,1)S(1)}, bf16[8,256,128]{2,1,0:T(8,128)(2,1)S(1)}, u32[]{:S(2)}, u32[]{:S(2)}) collective-permute-start(bf16[8,256,128]{2,1,0:T(8,128)(2,1)S(1)} %get-tuple-element.34.refs_4_), channel_id=1, source_target_pairs={{0,1},{1,0},{2,3},{3,2},{4,5},{5,4},{6,7},{7,6},{8,9},{9,8},{10,11... | collective-permute-start | bytes 1572872 | tf_op jit(solution)/shard_map/ppermute | solution.py:68
  31.4 2.6 %collective-permute-start.5 = (bf16[8,256,128]{2,1,0:T(8,128)(2,1)S(1)}, bf16[8,256,128]{2,1,0:T(8,128)(2,1)S(1)}, u32[]{:S(2)}, u32[]{:S(2)}) collective-permute-start(bf16[8,256,128]{2,1,0:T(8,128)(2,1)S(1)} %get-tuple-element.35.refs_6_), channel_id=1, source_target_pairs={{0,1},{1,0},{2,3},{3,2},{4,5},{5,4},{6,7},{7,6},{8,9},{9,8},{10,11... | collective-permute-start | bytes 1572872 | tf_op jit(solution)/shard_map/ppermute | solution.py:68
  34.0 10.0 %copy-start.2 = (s32[3,2]{0,1:T(2,128)S(1)}, s32[3,2]{0,1:T(2,128)}, u32[]{:S(2)}) copy-start(s32[3,2]{0,1:T(2,128)} %param.5) | copy-start | bytes 76
  36.3 12.5 %collective-permute-start.7 = (bf16[3,256,128]{2,1,0:T(8,128)(2,1)S(1)}, bf16[3,256,128]{2,1,0:T(8,128)(2,1)S(1)}, u32[]{:S(2)}, u32[]{:S(2)}) collective-permute-start(bf16[3,256,128]{2,1,0:T(8,128)(2,1)S(1)} %get-tuple-element.40), channel_id=1, source_target_pairs={{0,2},{1,3},{2,0},{3,1},{4,6},{5,7},{6,4},{7,5},{8,10},{9,11},{10,... | collective-permute-start | bytes 589832 | tf_op jit(solution)/shard_map/ppermute | solution.py:68
  48.8 2.7 %collective-permute-start.8 = (bf16[13,256,128]{2,1,0:T(8,128)(2,1)S(1)}, bf16[13,256,128]{2,1,0:T(8,128)(2,1)S(1)}, u32[]{:S(2)}, u32[]{:S(2)}) collective-permute-start(bf16[13,256,128]{2,1,0:T(8,128)(2,1)S(1)} %collective-permute-done.6.refs_2_), channel_id=1, source_target_pairs={{0,1},{1,0},{2,3},{3,2},{4,5},{5,4},{6,7},{7,6},{8,9},{9,8},{10,11... | collective-permute-start | bytes 2555912 | tf_op jit(solution)/shard_map/ppermute | solution.py:68
  48.8 2.7 %collective-permute-start.9 = (bf16[3,256,128]{2,1,0:T(8,128)(2,1)S(1)}, bf16[3,256,128]{2,1,0:T(8,128)(2,1)S(1)}, u32[]{:S(2)}, u32[]{:S(2)}) collective-permute-start(bf16[3,256,128]{2,1,0:T(8,128)(2,1)S(1)} %collective-permute-done.7.refs_3_), channel_id=1, source_target_pairs={{0,1},{1,0},{2,3},{3,2},{4,5},{5,4},{6,7},{7,6},{8,9},{9,8},{10,11... | collective-permute-start | bytes 589832 | tf_op jit(solution)/shard_map/ppermute | solution.py:68

commit v5 on v4

--- a/solution.py
+++ b/solution.py
@@ -71,16 +71,27 @@
 def part_copies(blocks, unit, place, basis, array, sems):
     rows = basis.shape[1] // lax.axis_size("slab")
     copies = []
-    for at, (sector, start, slab) in enumerate(blocks):
+    for at, (sector, spans, slab) in enumerate(blocks):
         row = pl.multiple_of((2 * slab + place[0] % 2) * rows, rows)
-        copies.append(
-            pltpu.make_async_copy(
-                basis.at[sector, pl.ds(row, rows), pl.ds(first_column(start, place, unit), unit)],
-                array.at[at],
-                sems.at[len(copies)],
+        column = 0
+        for start, count in spans:
+            copies.append(
+                pltpu.make_async_copy(
+                    basis.at[sector, pl.ds(row, rows), pl.ds(first_column(start, place, unit), count * unit)],
+                    array.at[at, :, pl.ds(column, count * unit)],
+                    sems.at[len(copies)],
+                )
             )
-        )
+            column += count * unit
     return copies
+
+
+def part_shape(blocks, rows, unit):
+    return pltpu.VMEM((len(blocks), rows, sum(count for _, count in blocks[0][1]) * unit), jnp.bfloat16)
+
+
+def part_sems(blocks):
+    return pltpu.SemaphoreType.DMA((sum(len(spans) for _, spans, _ in blocks),))
 
 
 def half_products(sectors, distances, place, basis, fermion, pieces, ready=lambda sector: None):
@@ -131,7 +142,7 @@
 
 def basis_part(basis, fermion, blocks, unit, distances):
     flavours, sectors, depth, width = fermion.shape
-    shapes = [pltpu.VMEM((len(blocks), width, unit), jnp.bfloat16)]
+    shapes = [part_shape(blocks, width, unit)]
     shapes += [pltpu.VMEM((sectors, flavours, width, width), jnp.bfloat16)] * len(distances)
     return kernel_call(
         functools.partial(part_kernel, blocks, unit, distances),
@@ -144,7 +155,7 @@
         [
             pltpu.VMEM((sectors, depth, depth), jnp.bfloat16),
             pltpu.VMEM((flavours, sectors, depth, width), jnp.bfloat16),
-            pltpu.SemaphoreType.DMA((len(blocks),)),
+            part_sems(blocks),
             pltpu.SemaphoreType.DMA((sectors, 2)),
         ],
     )
@@ -190,9 +201,9 @@
         [in_vmem(basis), in_vmem(fermion), in_vmem(after)],
         [WHOLE, WHOLE, WHOLE],
         [pltpu.VMEM((sectors, flavours, width, width), jnp.bfloat16)] * len(distances)
-        + [pltpu.VMEM((len(blocks), width, unit), jnp.bfloat16)],
+        + [part_shape(blocks, width, unit)],
         [WHOLE] * (len(distances) + 1),
-        [pltpu.SemaphoreType.DMA((len(blocks),))],
+        [part_sems(blocks)],
     )
 
 
@@ -221,11 +232,10 @@
     copies, at = [], 0
     for start, count in units:
         for slab in range(slabs):
-            to = ((slab % 2) * (slabs // 2) + slab // 2) * rows
             copies.append(
                 pltpu.make_async_copy(
                     basis.at[:, pl.ds(slab * rows, rows), pl.ds(first_column(start, place, unit), count * unit)],
-                    right.at[pl.ds(0, sectors), pl.ds(to, rows), pl.ds(at, count * unit)],
+                    right.at[pl.ds(0, sectors), slab % 2, slab // 2, :, pl.ds(at, count * unit)],
                     sems.at[first + len(copies)],
                 )
             )
@@ -234,19 +244,21 @@
 
 
 def next_copies(nexts, place, arrays, side, right, sems, first):
-    sectors, depth = right.shape[0] // 2, right.shape[1]
+    sectors = right.shape[0] // 2
     copies = []
-    for array, blocks in zip(arrays, nexts):
-        _, rows, columns = array.shape
-        for index, (sector, slab, column) in enumerate(blocks):
-            to = pl.multiple_of(((place[0] + side) % 2) * (depth // 2) + slab * rows, rows)
+    for array, runs in zip(arrays, nexts):
+        index = 0
+        for sector, slab, count, column in runs:
             copies.append(
                 pltpu.make_async_copy(
-                    array.at[index],
-                    right.at[sectors + sector, pl.ds(to, rows), pl.ds(column, columns)],
+                    array.at[pl.ds(index, count)],
+                    right.at[
+                        sectors + sector, (place[0] + side) % 2, pl.ds(slab, count), :, pl.ds(column, array.shape[2])
+                    ],
                     sems.at[first + len(copies)],
                 )
             )
+            index += count
     return copies
 
 
@@ -278,11 +290,11 @@
     flavours, width = halves[0].shape[1:3]
     given = [in_vmem(array) for array in (basis, *halves, *(array for pair in pairs for array in pair))]
     copies = sum(map(len, groups)) * (depth // width) + 2 * sum(len(holds) for holds in nexts)
-    last = pairs[-1][0]
     shapes = [pltpu.VMEM((sectors, flavours, width, depth), jnp.bfloat16)]
     for units in groups:
-        shapes.append(pltpu.VMEM((2 * sectors, depth, sum(count for _, count in units) * unit), jnp.bfloat16))
-    shapes.append(pltpu.VMEM((len(cuts), *last.shape[1:]), jnp.bfloat16))
+        columns = sum(count for _, count in units) * unit
+        shapes.append(pltpu.VMEM((2 * sectors, 2, depth // width // 2, width, columns), jnp.bfloat16))
+    shapes.append(pltpu.VMEM((len(cuts), width, unit), jnp.bfloat16))
     return kernel_call(
         functools.partial(gather_kernel, groups, nexts, unit, distances, cuts),
         "gather",
@@ -297,7 +309,8 @@
 
 def product(place, partner, sector, flavour, left, right):
     index = (partner[...][sector, flavour] - place[1] + place[2]) % place[2]
-    return jnp.dot(left[sector, flavour], right[index], preferred_element_type=jnp.float32).astype(jnp.bfloat16)
+    rows = right[index].reshape(left.shape[3], right.shape[4])
+    return jnp.dot(left[sector, flavour], rows, preferred_element_type=jnp.float32).astype(jnp.bfloat16)
 
 
 def early_kernel(distance, place, partner, half, right, _, left, stage, sem):
@@ -318,7 +331,7 @@
         [WHOLE] + [WHOLE] * 3,
         [
             pltpu.VMEM(left.shape, left.dtype),
-            pltpu.VMEM((flavours, sectors, width, right.shape[2]), jnp.bfloat16),
+            pltpu.VMEM((flavours, sectors, width, right.shape[4]), jnp.bfloat16),
         ],
         [WHOLE] * 2,
         [pltpu.SemaphoreType.DMA],
@@ -328,9 +341,11 @@
 
 def partial(place, partner, sector, flavour, side, left, right):
     index = (partner[...][sector, flavour] - place[1] + place[2]) % place[2]
-    depth = right.shape[1]
-    half = pl.ds(pl.multiple_of(((place[0] + side) % 2) * (depth // 2), depth // 2), depth // 2)
-    return jnp.dot(left[sector, flavour, :, half], right[index, half, :], preferred_element_type=jnp.float32)
+    core = (place[0] + side) % 2
+    half = left.shape[3] // 2
+    rows = right[index, core].reshape(half, right.shape[4])
+    columns = pl.ds(pl.multiple_of(core * half, half), half)
+    return jnp.dot(left[sector, flavour, :, columns], rows, preferred_element_type=jnp.float32)
 
 
 def own_rows_kernel(groups, place, partner, left, *refs):
@@ -366,7 +381,7 @@
         (sectors, depth),
         [partner, *given],
         [WHOLE] * (1 + len(given)),
-        [pltpu.VMEM((flavours, sectors, width, right.shape[2]), jnp.float32) for right in rights]
+        [pltpu.VMEM((flavours, sectors, width, right.shape[4]), jnp.float32) for right in rights]
         + [pltpu.VMEM(right.shape, right.dtype) for right in rights],
         [WHOLE] * (2 * len(rights)),
         [pltpu.SemaphoreType.DMA((sum(map(len, nexts)),)) for nexts in groups],
@@ -429,7 +444,7 @@
         ],
         [ANY, WHOLE],
         [
-            pltpu.VMEM((flavours, sectors, width, right.shape[2]), jnp.bfloat16),
+            pltpu.VMEM((flavours, sectors, width, right.shape[4]), jnp.bfloat16),
             pltpu.SemaphoreType.DMA((sum(map(len, nexts)),)),
             pltpu.SemaphoreType.DMA((sum(map(len, groups[:-1])),)),
             pltpu.SemaphoreType.DMA((sectors * flavours, len(groups[-1]))),
@@ -448,9 +463,9 @@
     alone = len(held) // 4
     count = 3
     units = ((0, count), (OWN, 1)), ((count, 6 - count), (OTHER, 1))
-    first_blocks = [(sector, start, slab) for start in (*range(count), OWN) for sector, slab in held]
-    last_blocks = [(sector, start, slab) for start in range(count, 6) for sector, slab in held]
-    last_blocks += [(sector, OTHER, slab) for sector, slab in held[:alone]]
+    first_blocks = [(sector, units[0], slab) for sector, slab in held]
+    last_blocks = [(sector, ((start, 1),), slab) for start in range(count, 6) for sector, slab in held]
+    last_blocks += [(sector, ((OTHER, 1),), slab) for sector, slab in held[:alone]]
     first_part, *far = basis_part(basis, fermion, first_blocks, unit, distances[:2])
     first = previous(first_part)
     far3, far2 = far_blocks(basis, fermion, distances[:2], far)
@@ -458,14 +473,21 @@
     mine, near, last_part = near_blocks(basis, fermion, last_blocks, unit, distances[2:], far2)
     beside, last = swapped(mine, 1), previous(last_part)
 
-    def columns(begin, end):
-        return [(sector, slab, at * unit) for at in range(begin, end) for sector, slab in held]
+    def runs(column, blocks):
+        found = []
+        for sector, slab in blocks:
+            if found and found[-1][0] == sector:
+                found[-1][2] += 1
+            else:
+                found.append([sector, slab, 1, column])
+        return found
 
     groups = ((0, 2), (2, 4))
-    pieces = cut_out(first, [slice(begin * len(held), end * len(held)) for begin, end in groups], (beside, got2))
+    every = slice(None)
+    pieces = cut_out(first, [(every, every, slice(begin * unit, end * unit)) for begin, end in groups], (beside, got2))
     pairs = [(piece, swapped(piece, 1)) for piece in pieces]
-    nexts = [columns(*group) for group in groups]
-    cuts = range(len(nexts[-1]) - len(held) + alone, len(nexts[-1]))
+    nexts = [runs(begin * unit, held) for begin, _ in groups]
+    cuts = [(at, every, pl.ds((groups[-1][1] - groups[-1][0] - 1) * unit, unit)) for at in range(alone, len(held))]
     left, early_right, late_right, sent = gather(
         basis, units, nexts, unit, pairs, [got2, beside, near], distances[1:], cuts
     )
@@ -473,9 +495,10 @@
     left, early = early_products(partner, got3, distances[0], left, early_right)
     last, other, early = lax.optimization_barrier((last, other, early))
     last_other, other_other = swapped(last, 1), swapped(other, 1)
-    full = columns(0, 6 - count + 1)
-    split = len(full) - len(held) + alone
-    nexts = [full[:split], full[split:]]
+    nexts = [[], runs((6 - count) * unit, held[alone:])]
+    for at in range(6 - count):
+        nexts[0] += runs(at * unit, held)
+    nexts[0] += runs((6 - count) * unit, held[:alone])
     total, late_right = own_rows(partner, [nexts], [[last, other]], left, [late_right])
     return late_products(
         partner, units, nexts, unit, [last_other, other_other], left, total, [early], late_right

time: 53.9 us -> 53.7 us (level)
  Pallas kernels: 15.3 us -> 14.3 us
  waiting for transfers between devices: 26 us -> 26.7 us
    pallas_call x8, Pallas kernels: 15.3 us -> 14.3 us  [kernel_call(): pl.pallas_call(kernel, out_shape=shapes, in_specs=specs, out_specs=out_sp...]
    ppermute x8, waiting for transfers between devices: 20.1 us -> 20.9 us  [swapped(): lax.ppermute(block, 'slab', [(i, i ^ distance) for i in range(lax.axis_si...]
  transfers between devices with their start and end apart: 10 -> 10, of which waited for: 7 -> 7; matrix products, arithmetic and copies ran while one was open for 0% -> 0% of each run, Pallas kernels for 15% -> 13%
where the time goes in v5:
time: 53.7 us; the launch traced here: 53.6 us
  waiting for transfers between devices  26.7 us (50%)
  Pallas kernels  14.3 us (27%)
  starting transfers between devices  12.5 us (23%)
    ppermute x8, waiting for transfers between devices, swapped(): lax.ppermute(block, 'slab', [(i, i ^ distance) for i in range(lax.axis_si...  20.9 us
    pallas_call x8, Pallas kernels, kernel_call(): pl.pallas_call(kernel, out_shape=shapes, in_specs=specs, out_specs=out_sp...  14.3 us
    ppermute x2, starting transfers between devices, previous(): lax.ppermute(block, 'sec', [((i + 1) % count, i) for i in range(count)])  6.69 us
    ppermute x8, starting transfers between devices, swapped(): lax.ppermute(block, 'slab', [(i, i ^ distance) for i in range(lax.axis_si...  5.82 us
    ppermute x2, waiting for transfers between devices, previous(): lax.ppermute(block, 'sec', [((i + 1) % count, i) for i in range(count)])  5.8 us
  transfers between devices with their start and end apart: 10, of which 7 were waited for; matrix products, arithmetic and copies ran while one was open for 0% of the time, Pallas kernels for 13%

profile of v5, /device:TPU:0, one launch (start us, length us, event | category | flops | bytes accessed | tf_op | source)
XLA Modules:
  0.0 53.6 jit_solution(639089605270142286)
XLA Ops:
  0.0 0.0 copy-start
  0.0 0.0 copy-start.1
  0.0 4.8 %part.1 = (bf16[4,256,512]{2,1,0:T(8,128)(2,1)S(1)}, bf16[2,3,256,256]{3,2,1,0:T(8,128)(2,1)S(1)}, bf16[2,3,256,256]{3,2,1,0:T(8,128)(2,1)S(1)}) custom-call(bf16[2,1024,1024]{2,1,0:T(8,128)(2,1)} %refs_0_.7, bf16[3,2,1024,256]{3,2,1,0:T(8,128)(2,1)} %refs_1_.5), custom_call_target="tpu_custom_call" | custom-call | tf_op jit(solution)/shard_map/part/pallas_call | solution.py:34
  4.9 2.7 %collective-permute-start.3 = (bf16[4,256,512]{2,1,0:T(8,128)(2,1)S(1)}, bf16[4,256,512]{2,1,0:T(8,128)(2,1)S(1)}, u32[]{:S(2)}, u32[]{:S(2)}) collective-permute-start(bf16[4,256,512]{2,1,0:T(8,128)(2,1)S(1)} %get-tuple-element.33), channel_id=1, source_target_pairs={{4,0},{8,4},{12,8},{16,12},{20,16},{24,20},{28,24},{0,28},{5,1},{9... | collective-permute-start | bytes 3145736 | tf_op jit(solution)/shard_map/ppermute | solution.py:64
  7.6 0.0 copy-done
  7.6 0.0 copy-done.1
  7.6 1.5 %collective-permute-start.1 = (bf16[2,3,256,256]{3,2,1,0:T(8,128)(2,1)S(1)}, bf16[2,3,256,256]{3,2,1,0:T(8,128)(2,1)S(1)}, u32[]{:S(2)}, u32[]{:S(2)}) collective-permute-start(bf16[2,3,256,256]{3,2,1,0:T(8,128)(2,1)S(1)} %get-tuple-element.30.refs_2_), channel_id=1, source_target_pairs={{0,2},{1,3},{2,0},{3,1},{4,6},{5,7},{6,4},{7,5},{8,10},{9,11},{10,... | collective-permute-start | bytes 2359304 | tf_op jit(solution)/shard_map/ppermute | solution.py:68
  9.1 2.2 %near.1 = (bf16[2,3,256,256]{3,2,1,0:T(8,128)(2,1)S(1)}, bf16[2,3,256,256]{3,2,1,0:T(8,128)(2,1)S(1)}, bf16[13,256,128]{2,1,0:T(8,128)(2,1)S(1)}) custom-call(bf16[2,1024,1024]{2,1,0:T(8,128)(2,1)S(1)} %copy-done, bf16[3,2,1024,256]{3,2,1,0:T(8,128)(2,1)S(1)} %copy-done.1, bf16[2,3,256,256]{3,2,1,0:T(8,128)(2,1)S(1)} %get-tuple-element.30.refs_2_), custom_call_target="tpu_custom_call" | custom-call | tf_op jit(solution)/shard_map/near/pallas_call | solution.py:34
  11.3 0.1 collective-permute-start.2
  11.4 4.0 %collective-permute-start.6 = (bf16[13,256,128]{2,1,0:T(8,128)(2,1)S(1)}, bf16[13,256,128]{2,1,0:T(8,128)(2,1)S(1)}, u32[]{:S(2)}, u32[]{:S(2)}) collective-permute-start(bf16[13,256,128]{2,1,0:T(8,128)(2,1)S(1)} %get-tuple-element.39), channel_id=1, source_target_pairs={{4,0},{8,4},{12,8},{16,12},{20,16},{24,20},{28,24},{0,28},{5,1},{9... | collective-permute-start | bytes 2555912 | tf_op jit(solution)/shard_map/ppermute | solution.py:64
  15.3 0.4 collective-permute-start
  15.7 12.3 %collective-permute-done.1.refs_2_.refs_1_ = bf16[2,3,256,256]{3,2,1,0:T(8,128)(2,1)S(1)} collective-permute-done((bf16[2,3,256,256]{3,2,1,0:T(8,128)(2,1)S(1)}, bf16[2,3,256,256]{3,2,1,0:T(8,128)(2,1)S(1)}, u32[]{:S(2)}, u32[]{:S(2)}) %collective-permute-start.1) | collective-permute-done | bytes 786464 | tf_op jit(solution)/shard_map/ppermute | solution.py:68
  28.1 0.0 collective-permute-done.2.refs_1_.refs_2_
  28.1 3.1 %collective-permute-done.3.refs_0_ = bf16[4,256,512]{2,1,0:T(8,128)(2,1)S(1)} collective-permute-done((bf16[4,256,512]{2,1,0:T(8,128)(2,1)S(1)}, bf16[4,256,512]{2,1,0:T(8,128)(2,1)S(1)}, u32[]{:S(2)}, u32[]{:S(2)}) %collective-permute-start.3) | collective-permute-done | bytes 1048608 | tf_op jit(solution)/shard_map/ppermute | solution.py:64
  31.2 0.1 cut.1
  31.2 0.1 collective-permute-start.4
  31.3 0.5 collective-permute-start.5
  31.8 1.4 %collective-permute-done.4.refs_5_ = bf16[4,256,256]{2,1,0:T(8,128)(2,1)S(1)} collective-permute-done((bf16[4,256,256]{2,1,0:T(8,128)(2,1)S(1)}, bf16[4,256,256]{2,1,0:T(8,128)(2,1)S(1)}, u32[]{:S(2)}, u32[]{:S(2)}) %collective-permute-start.4) | collective-permute-done | bytes 524320 | tf_op jit(solution)/shard_map/ppermute | solution.py:68
  33.2 0.7 %collective-permute-done.5.refs_7_ = bf16[4,256,256]{2,1,0:T(8,128)(2,1)S(1)} collective-permute-done((bf16[4,256,256]{2,1,0:T(8,128)(2,1)S(1)}, bf16[4,256,256]{2,1,0:T(8,128)(2,1)S(1)}, u32[]{:S(2)}, u32[]{:S(2)}) %collective-permute-start.5) | collective-permute-done | bytes 524320 | tf_op jit(solution)/shard_map/ppermute | solution.py:68
  34.0 0.0 copy-start.2
  34.0 1.5 %gather.1 = (bf16[2,3,256,1024]{3,2,1,0:T(8,128)(2,1)S(1)}, bf16[4,2,2,256,512]{4,3,2,1,0:T(8,128)(2,1)S(1)}, bf16[4,2,2,256,512]{4,3,2,1,0:T(8,128)(2,1)S(1)}, bf16[3,256,128]{2,1,0:T(8,128)(2,1)S(1)}) custom-call(bf16[2,1024,1024]{2,1,0:T(8,128)(2,1)S(1)} %copy-done, bf16[2,3,256,256]{3,2,1,0:T(8,128)(2,1)S(1)} %collective-permute-done.1.refs_2_.refs_1_, ...), custom_call_target="tpu_custom_call" | custom-call | tf_op jit(solution)/shard_map/gather/pallas_call | solution.py:34
  35.5 2.8 %collective-permute-start.7 = (bf16[3,256,128]{2,1,0:T(8,128)(2,1)S(1)}, bf16[3,256,128]{2,1,0:T(8,128)(2,1)S(1)}, u32[]{:S(2)}, u32[]{:S(2)}) collective-permute-start(bf16[3,256,128]{2,1,0:T(8,128)(2,1)S(1)} %get-tuple-element.40), channel_id=1, source_target_pairs={{0,2},{1,3},{2,0},{3,1},{4,6},{5,7},{6,4},{7,5},{8,10},{9,11},{10,... | collective-permute-start | bytes 589832 | tf_op jit(solution)/shard_map/ppermute | solution.py:68
  38.3 5.6 %collective-permute-done.refs_1_ = bf16[2,3,256,256]{3,2,1,0:T(8,128)(2,1)S(1)} collective-permute-done((bf16[2,3,256,256]{3,2,1,0:T(8,128)(2,1)S(1)}, bf16[2,3,256,256]{3,2,1,0:T(8,128)(2,1)S(1)}, u32[]{:S(2)}, u32[]{:S(2)}) %collective-permute-start) | collective-permute-done | bytes 786464 | tf_op jit(solution)/shard_map/ppermute | solution.py:68
  43.9 0.0 copy-done.2
  43.9 2.0 %early.1 = (bf16[2,3,256,1024]{3,2,1,0:T(8,128)(2,1)S(1)}, bf16[3,2,256,512]{3,2,1,0:T(8,128)(2,1)S(1)}) custom-call(s32[2,3]{1,0:T(2,128)S(1)} %bitcast.1, bf16[2,3,256,256]{3,2,1,0:T(8,128)(2,1)S(1)} %collective-permute-done.refs_1_, bf16[4,2,2,256,512]{4,3,2,1,0:T(8,128)(2,1)S(1)} %get-tuple-element.36.refs_2_, ...), custom_call_target="tpu_custom_call", output_to_operand_aliasing={{0}: (3, {})} | custom-call | tf_op jit(solution)/shard_map/early/pallas_call | solution.py:34
  46.0 2.7 %collective-permute-done.6.refs_2_ = bf16[13,256,128]{2,1,0:T(8,128)(2,1)S(1)} collective-permute-done((bf16[13,256,128]{2,1,0:T(8,128)(2,1)S(1)}, bf16[13,256,128]{2,1,0:T(8,128)(2,1)S(1)}, u32[]{:S(2)}, u32[]{:S(2)}) %collective-permute-start.6) | collective-permute-done | bytes 852000 | tf_op jit(solution)/shard_map/ppermute | solution.py:64
  48.7 0.0 collective-permute-done.7.refs_3_
  48.7 0.0 collective-permute-start.8
  48.7 0.5 collective-permute-start.9
  49.2 1.4 %own_rows.1 = (f32[3,2,256,512]{3,2,1,0:T(8,128)S(1)}, bf16[4,2,2,256,512]{4,3,2,1,0:T(8,128)(2,1)S(1)}) custom-call(s32[2,3]{1,0:T(2,128)S(1)} %bitcast.2, bf16[2,3,256,1024]{3,2,1,0:T(8,128)(2,1)S(1)} %get-tuple-element.38.refs_1_, bf16[13,256,128]{2,1,0:T(8,128)(2,1)S(1)} %collective-permute-done.6.refs_2_, ...), custom_call_target="tpu_custom_call", output_to_operand_aliasing={{1}: (4, {})} | custom-call | tf_op jit(solution)/shard_map/own_rows/pallas_call | solution.py:34
  50.6 0.8 %collective-permute-done.9.refs_5_ = bf16[3,256,128]{2,1,0:T(8,128)(2,1)S(1)} collective-permute-done((bf16[3,256,128]{2,1,0:T(8,128)(2,1)S(1)}, bf16[3,256,128]{2,1,0:T(8,128)(2,1)S(1)}, u32[]{:S(2)}, u32[]{:S(2)}) %collective-permute-start.9) | collective-permute-done | bytes 196640 | tf_op jit(solution)/shard_map/ppermute | solution.py:68
  51.3 0.0 collective-permute-done.8.refs_4_
  51.4 2.2 %late.1 = (bf16[3,2,256,1024]{3,2,1,0:T(8,128)(2,1)}, bf16[4,2,2,256,512]{4,3,2,1,0:T(8,128)(2,1)S(1)}) custom-call(s32[2,3]{1,0:T(2,128)S(1)} %bitcast.3, bf16[2,3,256,1024]{3,2,1,0:T(8,128)(2,1)S(1)} %get-tuple-element.38.refs_1_, f32[3,2,256,512]{3,2,1,0:T(8,128)S(1)} %get-tuple-element.45.refs_2_, ...), custom_call_target="tpu_custom_call", output_to_operand_aliasing={{1}: (6, {})} | custom-call | tf_op jit(solution)/shard_map/late/pallas_call | solution.py:34
  (1 shorter events, 0.0 us)
Async XLA Ops:
  0.0 7.6 %copy-start = (bf16[2,1024,1024]{2,1,0:T(8,128)(2,1)S(1)}, bf16[2,1024,1024]{2,1,0:T(8,128)(2,1)}, u32[]{:S(2)}) copy-start(bf16[2,1024,1024]{2,1,0:T(8,128)(2,1)} %refs_0_.7) | copy-start | bytes 12582916
  0.0 7.6 %copy-start.1 = (bf16[3,2,1024,256]{3,2,1,0:T(8,128)(2,1)S(1)}, bf16[3,2,1024,256]{3,2,1,0:T(8,128)(2,1)}, u32[]{:S(2)}) copy-start(bf16[3,2,1024,256]{3,2,1,0:T(8,128)(2,1)} %refs_1_.5) | copy-start | bytes 9437188
  4.9 26.3 %collective-permute-start.3 = (bf16[4,256,512]{2,1,0:T(8,128)(2,1)S(1)}, bf16[4,256,512]{2,1,0:T(8,128)(2,1)S(1)}, u32[]{:S(2)}, u32[]{:S(2)}) collective-permute-start(bf16[4,256,512]{2,1,0:T(8,128)(2,1)S(1)} %get-tuple-element.33), channel_id=1, source_target_pairs={{4,0},{8,4},{12,8},{16,12},{20,16},{24,20},{28,24},{0,28},{5,1},{9... | collective-permute-start | bytes 3145736 | tf_op jit(solution)/shard_map/ppermute | solution.py:64
  7.6 20.5 %collective-permute-start.1 = (bf16[2,3,256,256]{3,2,1,0:T(8,128)(2,1)S(1)}, bf16[2,3,256,256]{3,2,1,0:T(8,128)(2,1)S(1)}, u32[]{:S(2)}, u32[]{:S(2)}) collective-permute-start(bf16[2,3,256,256]{3,2,1,0:T(8,128)(2,1)S(1)} %get-tuple-element.30.refs_2_), channel_id=1, source_target_pairs={{0,2},{1,3},{2,0},{3,1},{4,6},{5,7},{6,4},{7,5},{8,10},{9,11},{10,... | collective-permute-start | bytes 2359304 | tf_op jit(solution)/shard_map/ppermute | solution.py:68
  11.3 16.8 %collective-permute-start.2 = (bf16[2,3,256,256]{3,2,1,0:T(8,128)(2,1)S(1)}, bf16[2,3,256,256]{3,2,1,0:T(8,128)(2,1)S(1)}, u32[]{:S(2)}, u32[]{:S(2)}) collective-permute-start(bf16[2,3,256,256]{3,2,1,0:T(8,128)(2,1)S(1)} %get-tuple-element.31), channel_id=1, source_target_pairs={{0,1},{1,0},{2,3},{3,2},{4,5},{5,4},{6,7},{7,6},{8,9},{9,8},{10,11... | collective-permute-start | bytes 2359304 | tf_op jit(solution)/shard_map/ppermute | solution.py:68
  11.4 37.3 %collective-permute-start.6 = (bf16[13,256,128]{2,1,0:T(8,128)(2,1)S(1)}, bf16[13,256,128]{2,1,0:T(8,128)(2,1)S(1)}, u32[]{:S(2)}, u32[]{:S(2)}) collective-permute-start(bf16[13,256,128]{2,1,0:T(8,128)(2,1)S(1)} %get-tuple-element.39), channel_id=1, source_target_pairs={{4,0},{8,4},{12,8},{16,12},{20,16},{24,20},{28,24},{0,28},{5,1},{9... | collective-permute-start | bytes 2555912 | tf_op jit(solution)/shard_map/ppermute | solution.py:64
  15.3 28.6 %collective-permute-start = (bf16[2,3,256,256]{3,2,1,0:T(8,128)(2,1)S(1)}, bf16[2,3,256,256]{3,2,1,0:T(8,128)(2,1)S(1)}, u32[]{:S(2)}, u32[]{:S(2)}) collective-permute-start(bf16[2,3,256,256]{3,2,1,0:T(8,128)(2,1)S(1)} %get-tuple-element.29), channel_id=1, source_target_pairs={{0,3},{1,2},{2,1},{3,0},{4,7},{5,6},{6,5},{7,4},{8,11},{9,10},{10,... | collective-permute-start | bytes 2359304 | tf_op jit(solution)/shard_map/ppermute | solution.py:68
  31.2 2.0 %collective-permute-start.4 = (bf16[4,256,256]{2,1,0:T(8,128)(2,1)S(1)}, bf16[4,256,256]{2,1,0:T(8,128)(2,1)S(1)}, u32[]{:S(2)}, u32[]{:S(2)}) collective-permute-start(bf16[4,256,256]{2,1,0:T(8,128)(2,1)S(1)} %get-tuple-element.34.refs_4_), channel_id=1, source_target_pairs={{0,1},{1,0},{2,3},{3,2},{4,5},{5,4},{6,7},{7,6},{8,9},{9,8},{10,11... | collective-permute-start | bytes 1572872 | tf_op jit(solution)/shard_map/ppermute | solution.py:68
  31.3 2.6 %collective-permute-start.5 = (bf16[4,256,256]{2,1,0:T(8,128)(2,1)S(1)}, bf16[4,256,256]{2,1,0:T(8,128)(2,1)S(1)}, u32[]{:S(2)}, u32[]{:S(2)}) collective-permute-start(bf16[4,256,256]{2,1,0:T(8,128)(2,1)S(1)} %get-tuple-element.35.refs_6_), channel_id=1, source_target_pairs={{0,1},{1,0},{2,3},{3,2},{4,5},{5,4},{6,7},{7,6},{8,9},{9,8},{10,11... | collective-permute-start | bytes 1572872 | tf_op jit(solution)/shard_map/ppermute | solution.py:68
  34.0 10.0 %copy-start.2 = (s32[3,2]{0,1:T(2,128)S(1)}, s32[3,2]{0,1:T(2,128)}, u32[]{:S(2)}) copy-start(s32[3,2]{0,1:T(2,128)} %param.5) | copy-start | bytes 76
  35.5 13.2 %collective-permute-start.7 = (bf16[3,256,128]{2,1,0:T(8,128)(2,1)S(1)}, bf16[3,256,128]{2,1,0:T(8,128)(2,1)S(1)}, u32[]{:S(2)}, u32[]{:S(2)}) collective-permute-start(bf16[3,256,128]{2,1,0:T(8,128)(2,1)S(1)} %get-tuple-element.40), channel_id=1, source_target_pairs={{0,2},{1,3},{2,0},{3,1},{4,6},{5,7},{6,4},{7,5},{8,10},{9,11},{10,... | collective-permute-start | bytes 589832 | tf_op jit(solution)/shard_map/ppermute | solution.py:68
  48.7 2.7 %collective-permute-start.8 = (bf16[13,256,128]{2,1,0:T(8,128)(2,1)S(1)}, bf16[13,256,128]{2,1,0:T(8,128)(2,1)S(1)}, u32[]{:S(2)}, u32[]{:S(2)}) collective-permute-start(bf16[13,256,128]{2,1,0:T(8,128)(2,1)S(1)} %collective-permute-done.6.refs_2_), channel_id=1, source_target_pairs={{0,1},{1,0},{2,3},{3,2},{4,5},{5,4},{6,7},{7,6},{8,9},{9,8},{10,11... | collective-permute-start | bytes 2555912 | tf_op jit(solution)/shard_map/ppermute | solution.py:68
  48.7 2.7 %collective-permute-start.9 = (bf16[3,256,128]{2,1,0:T(8,128)(2,1)S(1)}, bf16[3,256,128]{2,1,0:T(8,128)(2,1)S(1)}, u32[]{:S(2)}, u32[]{:S(2)}) collective-permute-start(bf16[3,256,128]{2,1,0:T(8,128)(2,1)S(1)} %collective-permute-done.7.refs_3_), channel_id=1, source_target_pairs={{0,1},{1,0},{2,3},{3,2},{4,5},{5,4},{6,7},{7,6},{8,9},{9,8},{10,11... | collective-permute-start | bytes 589832 | tf_op jit(solution)/shard_map/ppermute | solution.py:68

commit v6 on v5

--- a/solution.py
+++ b/solution.py
@@ -457,7 +457,7 @@
     sectors, depth, _ = basis.shape
     unit = depth // 8
     partner = partner.T
-    distances = (3, 2, 1, 0)
+    distances = tuple(reversed(range(lax.axis_size("slab"))))
     slabs = range(lax.axis_size("slab") // 2)
     held = [(sector, slab) for sector in range(sectors) for slab in slabs]
     alone = len(held) // 4
@@ -469,9 +469,9 @@
     first_part, *far = basis_part(basis, fermion, first_blocks, unit, distances[:2])
     first = previous(first_part)
     far3, far2 = far_blocks(basis, fermion, distances[:2], far)
-    got2, got3 = swapped(far2, 2), swapped(far3, 3)
+    got3, got2 = swapped(far3, distances[0]), swapped(far2, distances[1])
     mine, near, last_part = near_blocks(basis, fermion, last_blocks, unit, distances[2:], far2)
-    beside, last = swapped(mine, 1), previous(last_part)
+    beside, last = swapped(mine, distances[2]), previous(last_part)
 
     def runs(column, blocks):
         found = []
@@ -491,7 +491,7 @@
     left, early_right, late_right, sent = gather(
         basis, units, nexts, unit, pairs, [got2, beside, near], distances[1:], cuts
     )
-    other = swapped(sent, 2)
+    other = swapped(sent, distances[1])
     left, early = early_products(partner, got3, distances[0], left, early_right)
     last, other, early = lax.optimization_barrier((last, other, early))
     last_other, other_other = swapped(last, 1), swapped(other, 1)

time: 53.7 us -> 53.7 us (level)
  no operation moved by 1% of the time
where the time goes in v6:
time: 53.7 us; the launch traced here: 53.6 us
  waiting for transfers between devices  26.7 us (50%)
  Pallas kernels  14.3 us (27%)
  starting transfers between devices  12.5 us (23%)
    ppermute x8, waiting for transfers between devices, swapped(): lax.ppermute(block, 'slab', [(i, i ^ distance) for i in range(lax.axis_si...  20.9 us
    pallas_call x8, Pallas kernels, kernel_call(): pl.pallas_call(kernel, out_shape=shapes, in_specs=specs, out_specs=out_sp...  14.3 us
    ppermute x2, starting transfers between devices, previous(): lax.ppermute(block, 'sec', [((i + 1) % count, i) for i in range(count)])  6.69 us
    ppermute x8, starting transfers between devices, swapped(): lax.ppermute(block, 'slab', [(i, i ^ distance) for i in range(lax.axis_si...  5.82 us
    ppermute x2, waiting for transfers between devices, previous(): lax.ppermute(block, 'sec', [((i + 1) % count, i) for i in range(count)])  5.8 us
  transfers between devices with their start and end apart: 10, of which 7 were waited for; matrix products, arithmetic and copies ran while one was open for 0% of the time, Pallas kernels for 13%

profile of v6, /device:TPU:0, one launch (start us, length us, event | category | flops | bytes accessed | tf_op | source)
XLA Modules:
  0.0 53.6 jit_solution(639089605270142286)
XLA Ops:
  0.0 0.0 copy-start
  0.0 0.0 copy-start.1
  0.0 4.8 %part.1 = (bf16[4,256,512]{2,1,0:T(8,128)(2,1)S(1)}, bf16[2,3,256,256]{3,2,1,0:T(8,128)(2,1)S(1)}, bf16[2,3,256,256]{3,2,1,0:T(8,128)(2,1)S(1)}) custom-call(bf16[2,1024,1024]{2,1,0:T(8,128)(2,1)} %refs_0_.7, bf16[3,2,1024,256]{3,2,1,0:T(8,128)(2,1)} %refs_1_.5), custom_call_target="tpu_custom_call" | custom-call | tf_op jit(solution)/shard_map/part/pallas_call | solution.py:34
  4.9 2.7 %collective-permute-start.3 = (bf16[4,256,512]{2,1,0:T(8,128)(2,1)S(1)}, bf16[4,256,512]{2,1,0:T(8,128)(2,1)S(1)}, u32[]{:S(2)}, u32[]{:S(2)}) collective-permute-start(bf16[4,256,512]{2,1,0:T(8,128)(2,1)S(1)} %get-tuple-element.33), channel_id=1, source_target_pairs={{4,0},{8,4},{12,8},{16,12},{20,16},{24,20},{28,24},{0,28},{5,1},{9... | collective-permute-start | bytes 3145736 | tf_op jit(solution)/shard_map/ppermute | solution.py:64
  7.6 0.0 copy-done
  7.6 0.0 copy-done.1
  7.6 1.5 %collective-permute-start.1 = (bf16[2,3,256,256]{3,2,1,0:T(8,128)(2,1)S(1)}, bf16[2,3,256,256]{3,2,1,0:T(8,128)(2,1)S(1)}, u32[]{:S(2)}, u32[]{:S(2)}) collective-permute-start(bf16[2,3,256,256]{3,2,1,0:T(8,128)(2,1)S(1)} %get-tuple-element.30.refs_2_), channel_id=1, source_target_pairs={{0,2},{1,3},{2,0},{3,1},{4,6},{5,7},{6,4},{7,5},{8,10},{9,11},{10,... | collective-permute-start | bytes 2359304 | tf_op jit(solution)/shard_map/ppermute | solution.py:68
  9.1 2.2 %near.1 = (bf16[2,3,256,256]{3,2,1,0:T(8,128)(2,1)S(1)}, bf16[2,3,256,256]{3,2,1,0:T(8,128)(2,1)S(1)}, bf16[13,256,128]{2,1,0:T(8,128)(2,1)S(1)}) custom-call(bf16[2,1024,1024]{2,1,0:T(8,128)(2,1)S(1)} %copy-done, bf16[3,2,1024,256]{3,2,1,0:T(8,128)(2,1)S(1)} %copy-done.1, bf16[2,3,256,256]{3,2,1,0:T(8,128)(2,1)S(1)} %get-tuple-element.30.refs_2_), custom_call_target="tpu_custom_call" | custom-call | tf_op jit(solution)/shard_map/near/pallas_call | solution.py:34
  11.3 0.1 collective-permute-start.2
  11.4 4.0 %collective-permute-start.6 = (bf16[13,256,128]{2,1,0:T(8,128)(2,1)S(1)}, bf16[13,256,128]{2,1,0:T(8,128)(2,1)S(1)}, u32[]{:S(2)}, u32[]{:S(2)}) collective-permute-start(bf16[13,256,128]{2,1,0:T(8,128)(2,1)S(1)} %get-tuple-element.39), channel_id=1, source_target_pairs={{4,0},{8,4},{12,8},{16,12},{20,16},{24,20},{28,24},{0,28},{5,1},{9... | collective-permute-start | bytes 2555912 | tf_op jit(solution)/shard_map/ppermute | solution.py:64
  15.3 0.4 collective-permute-start
  15.7 12.3 %collective-permute-done.1.refs_2_.refs_1_ = bf16[2,3,256,256]{3,2,1,0:T(8,128)(2,1)S(1)} collective-permute-done((bf16[2,3,256,256]{3,2,1,0:T(8,128)(2,1)S(1)}, bf16[2,3,256,256]{3,2,1,0:T(8,128)(2,1)S(1)}, u32[]{:S(2)}, u32[]{:S(2)}) %collective-permute-start.1) | collective-permute-done | bytes 786464 | tf_op jit(solution)/shard_map/ppermute | solution.py:68
  28.1 0.0 collective-permute-done.2.refs_1_.refs_2_
  28.1 3.1 %collective-permute-done.3.refs_0_ = bf16[4,256,512]{2,1,0:T(8,128)(2,1)S(1)} collective-permute-done((bf16[4,256,512]{2,1,0:T(8,128)(2,1)S(1)}, bf16[4,256,512]{2,1,0:T(8,128)(2,1)S(1)}, u32[]{:S(2)}, u32[]{:S(2)}) %collective-permute-start.3) | collective-permute-done | bytes 1048608 | tf_op jit(solution)/shard_map/ppermute | solution.py:64
  31.2 0.1 cut.1
  31.2 0.1 collective-permute-start.4
  31.3 0.5 collective-permute-start.5
  31.8 1.4 %collective-permute-done.4.refs_5_ = bf16[4,256,256]{2,1,0:T(8,128)(2,1)S(1)} collective-permute-done((bf16[4,256,256]{2,1,0:T(8,128)(2,1)S(1)}, bf16[4,256,256]{2,1,0:T(8,128)(2,1)S(1)}, u32[]{:S(2)}, u32[]{:S(2)}) %collective-permute-start.4) | collective-permute-done | bytes 524320 | tf_op jit(solution)/shard_map/ppermute | solution.py:68
  33.2 0.7 %collective-permute-done.5.refs_7_ = bf16[4,256,256]{2,1,0:T(8,128)(2,1)S(1)} collective-permute-done((bf16[4,256,256]{2,1,0:T(8,128)(2,1)S(1)}, bf16[4,256,256]{2,1,0:T(8,128)(2,1)S(1)}, u32[]{:S(2)}, u32[]{:S(2)}) %collective-permute-start.5) | collective-permute-done | bytes 524320 | tf_op jit(solution)/shard_map/ppermute | solution.py:68
  34.0 0.0 copy-start.2
  34.0 1.5 %gather.1 = (bf16[2,3,256,1024]{3,2,1,0:T(8,128)(2,1)S(1)}, bf16[4,2,2,256,512]{4,3,2,1,0:T(8,128)(2,1)S(1)}, bf16[4,2,2,256,512]{4,3,2,1,0:T(8,128)(2,1)S(1)}, bf16[3,256,128]{2,1,0:T(8,128)(2,1)S(1)}) custom-call(bf16[2,1024,1024]{2,1,0:T(8,128)(2,1)S(1)} %copy-done, bf16[2,3,256,256]{3,2,1,0:T(8,128)(2,1)S(1)} %collective-permute-done.1.refs_2_.refs_1_, ...), custom_call_target="tpu_custom_call" | custom-call | tf_op jit(solution)/shard_map/gather/pallas_call | solution.py:34
  35.5 2.8 %collective-permute-start.7 = (bf16[3,256,128]{2,1,0:T(8,128)(2,1)S(1)}, bf16[3,256,128]{2,1,0:T(8,128)(2,1)S(1)}, u32[]{:S(2)}, u32[]{:S(2)}) collective-permute-start(bf16[3,256,128]{2,1,0:T(8,128)(2,1)S(1)} %get-tuple-element.40), channel_id=1, source_target_pairs={{0,2},{1,3},{2,0},{3,1},{4,6},{5,7},{6,4},{7,5},{8,10},{9,11},{10,... | collective-permute-start | bytes 589832 | tf_op jit(solution)/shard_map/ppermute | solution.py:68
  38.3 5.6 %collective-permute-done.refs_1_ = bf16[2,3,256,256]{3,2,1,0:T(8,128)(2,1)S(1)} collective-permute-done((bf16[2,3,256,256]{3,2,1,0:T(8,128)(2,1)S(1)}, bf16[2,3,256,256]{3,2,1,0:T(8,128)(2,1)S(1)}, u32[]{:S(2)}, u32[]{:S(2)}) %collective-permute-start) | collective-permute-done | bytes 786464 | tf_op jit(solution)/shard_map/ppermute | solution.py:68
  43.9 0.0 copy-done.2
  43.9 2.0 %early.1 = (bf16[2,3,256,1024]{3,2,1,0:T(8,128)(2,1)S(1)}, bf16[3,2,256,512]{3,2,1,0:T(8,128)(2,1)S(1)}) custom-call(s32[2,3]{1,0:T(2,128)S(1)} %bitcast.1, bf16[2,3,256,256]{3,2,1,0:T(8,128)(2,1)S(1)} %collective-permute-done.refs_1_, bf16[4,2,2,256,512]{4,3,2,1,0:T(8,128)(2,1)S(1)} %get-tuple-element.36.refs_2_, ...), custom_call_target="tpu_custom_call", output_to_operand_aliasing={{0}: (3, {})} | custom-call | tf_op jit(solution)/shard_map/early/pallas_call | solution.py:34
  46.0 2.7 %collective-permute-done.6.refs_2_ = bf16[13,256,128]{2,1,0:T(8,128)(2,1)S(1)} collective-permute-done((bf16[13,256,128]{2,1,0:T(8,128)(2,1)S(1)}, bf16[13,256,128]{2,1,0:T(8,128)(2,1)S(1)}, u32[]{:S(2)}, u32[]{:S(2)}) %collective-permute-start.6) | collective-permute-done | bytes 852000 | tf_op jit(solution)/shard_map/ppermute | solution.py:64
  48.7 0.0 collective-permute-done.7.refs_3_
  48.7 0.0 collective-permute-start.8
  48.7 0.5 collective-permute-start.9
  49.2 1.4 %own_rows.1 = (f32[3,2,256,512]{3,2,1,0:T(8,128)S(1)}, bf16[4,2,2,256,512]{4,3,2,1,0:T(8,128)(2,1)S(1)}) custom-call(s32[2,3]{1,0:T(2,128)S(1)} %bitcast.2, bf16[2,3,256,1024]{3,2,1,0:T(8,128)(2,1)S(1)} %get-tuple-element.38.refs_1_, bf16[13,256,128]{2,1,0:T(8,128)(2,1)S(1)} %collective-permute-done.6.refs_2_, ...), custom_call_target="tpu_custom_call", output_to_operand_aliasing={{1}: (4, {})} | custom-call | tf_op jit(solution)/shard_map/own_rows/pallas_call | solution.py:34
  50.6 0.8 %collective-permute-done.9.refs_5_ = bf16[3,256,128]{2,1,0:T(8,128)(2,1)S(1)} collective-permute-done((bf16[3,256,128]{2,1,0:T(8,128)(2,1)S(1)}, bf16[3,256,128]{2,1,0:T(8,128)(2,1)S(1)}, u32[]{:S(2)}, u32[]{:S(2)}) %collective-permute-start.9) | collective-permute-done | bytes 196640 | tf_op jit(solution)/shard_map/ppermute | solution.py:68
  51.3 0.0 collective-permute-done.8.refs_4_
  51.4 2.2 %late.1 = (bf16[3,2,256,1024]{3,2,1,0:T(8,128)(2,1)}, bf16[4,2,2,256,512]{4,3,2,1,0:T(8,128)(2,1)S(1)}) custom-call(s32[2,3]{1,0:T(2,128)S(1)} %bitcast.3, bf16[2,3,256,1024]{3,2,1,0:T(8,128)(2,1)S(1)} %get-tuple-element.38.refs_1_, f32[3,2,256,512]{3,2,1,0:T(8,128)S(1)} %get-tuple-element.45.refs_2_, ...), custom_call_target="tpu_custom_call", output_to_operand_aliasing={{1}: (6, {})} | custom-call | tf_op jit(solution)/shard_map/late/pallas_call | solution.py:34
  (1 shorter events, 0.0 us)
Async XLA Ops:
  0.0 7.6 %copy-start = (bf16[2,1024,1024]{2,1,0:T(8,128)(2,1)S(1)}, bf16[2,1024,1024]{2,1,0:T(8,128)(2,1)}, u32[]{:S(2)}) copy-start(bf16[2,1024,1024]{2,1,0:T(8,128)(2,1)} %refs_0_.7) | copy-start | bytes 12582916
  0.0 7.6 %copy-start.1 = (bf16[3,2,1024,256]{3,2,1,0:T(8,128)(2,1)S(1)}, bf16[3,2,1024,256]{3,2,1,0:T(8,128)(2,1)}, u32[]{:S(2)}) copy-start(bf16[3,2,1024,256]{3,2,1,0:T(8,128)(2,1)} %refs_1_.5) | copy-start | bytes 9437188
  4.9 26.3 %collective-permute-start.3 = (bf16[4,256,512]{2,1,0:T(8,128)(2,1)S(1)}, bf16[4,256,512]{2,1,0:T(8,128)(2,1)S(1)}, u32[]{:S(2)}, u32[]{:S(2)}) collective-permute-start(bf16[4,256,512]{2,1,0:T(8,128)(2,1)S(1)} %get-tuple-element.33), channel_id=1, source_target_pairs={{4,0},{8,4},{12,8},{16,12},{20,16},{24,20},{28,24},{0,28},{5,1},{9... | collective-permute-start | bytes 3145736 | tf_op jit(solution)/shard_map/ppermute | solution.py:64
  7.6 20.5 %collective-permute-start.1 = (bf16[2,3,256,256]{3,2,1,0:T(8,128)(2,1)S(1)}, bf16[2,3,256,256]{3,2,1,0:T(8,128)(2,1)S(1)}, u32[]{:S(2)}, u32[]{:S(2)}) collective-permute-start(bf16[2,3,256,256]{3,2,1,0:T(8,128)(2,1)S(1)} %get-tuple-element.30.refs_2_), channel_id=1, source_target_pairs={{0,2},{1,3},{2,0},{3,1},{4,6},{5,7},{6,4},{7,5},{8,10},{9,11},{10,... | collective-permute-start | bytes 2359304 | tf_op jit(solution)/shard_map/ppermute | solution.py:68
  11.3 16.8 %collective-permute-start.2 = (bf16[2,3,256,256]{3,2,1,0:T(8,128)(2,1)S(1)}, bf16[2,3,256,256]{3,2,1,0:T(8,128)(2,1)S(1)}, u32[]{:S(2)}, u32[]{:S(2)}) collective-permute-start(bf16[2,3,256,256]{3,2,1,0:T(8,128)(2,1)S(1)} %get-tuple-element.31), channel_id=1, source_target_pairs={{0,1},{1,0},{2,3},{3,2},{4,5},{5,4},{6,7},{7,6},{8,9},{9,8},{10,11... | collective-permute-start | bytes 2359304 | tf_op jit(solution)/shard_map/ppermute | solution.py:68
  11.4 37.3 %collective-permute-start.6 = (bf16[13,256,128]{2,1,0:T(8,128)(2,1)S(1)}, bf16[13,256,128]{2,1,0:T(8,128)(2,1)S(1)}, u32[]{:S(2)}, u32[]{:S(2)}) collective-permute-start(bf16[13,256,128]{2,1,0:T(8,128)(2,1)S(1)} %get-tuple-element.39), channel_id=1, source_target_pairs={{4,0},{8,4},{12,8},{16,12},{20,16},{24,20},{28,24},{0,28},{5,1},{9... | collective-permute-start | bytes 2555912 | tf_op jit(solution)/shard_map/ppermute | solution.py:64
  15.3 28.6 %collective-permute-start = (bf16[2,3,256,256]{3,2,1,0:T(8,128)(2,1)S(1)}, bf16[2,3,256,256]{3,2,1,0:T(8,128)(2,1)S(1)}, u32[]{:S(2)}, u32[]{:S(2)}) collective-permute-start(bf16[2,3,256,256]{3,2,1,0:T(8,128)(2,1)S(1)} %get-tuple-element.29), channel_id=1, source_target_pairs={{0,3},{1,2},{2,1},{3,0},{4,7},{5,6},{6,5},{7,4},{8,11},{9,10},{10,... | collective-permute-start | bytes 2359304 | tf_op jit(solution)/shard_map/ppermute | solution.py:68
  31.2 2.0 %collective-permute-start.4 = (bf16[4,256,256]{2,1,0:T(8,128)(2,1)S(1)}, bf16[4,256,256]{2,1,0:T(8,128)(2,1)S(1)}, u32[]{:S(2)}, u32[]{:S(2)}) collective-permute-start(bf16[4,256,256]{2,1,0:T(8,128)(2,1)S(1)} %get-tuple-element.34.refs_4_), channel_id=1, source_target_pairs={{0,1},{1,0},{2,3},{3,2},{4,5},{5,4},{6,7},{7,6},{8,9},{9,8},{10,11... | collective-permute-start | bytes 1572872 | tf_op jit(solution)/shard_map/ppermute | solution.py:68
  31.3 2.6 %collective-permute-start.5 = (bf16[4,256,256]{2,1,0:T(8,128)(2,1)S(1)}, bf16[4,256,256]{2,1,0:T(8,128)(2,1)S(1)}, u32[]{:S(2)}, u32[]{:S(2)}) collective-permute-start(bf16[4,256,256]{2,1,0:T(8,128)(2,1)S(1)} %get-tuple-element.35.refs_6_), channel_id=1, source_target_pairs={{0,1},{1,0},{2,3},{3,2},{4,5},{5,4},{6,7},{7,6},{8,9},{9,8},{10,11... | collective-permute-start | bytes 1572872 | tf_op jit(solution)/shard_map/ppermute | solution.py:68
  34.0 10.0 %copy-start.2 = (s32[3,2]{0,1:T(2,128)S(1)}, s32[3,2]{0,1:T(2,128)}, u32[]{:S(2)}) copy-start(s32[3,2]{0,1:T(2,128)} %param.5) | copy-start | bytes 76
  35.5 13.2 %collective-permute-start.7 = (bf16[3,256,128]{2,1,0:T(8,128)(2,1)S(1)}, bf16[3,256,128]{2,1,0:T(8,128)(2,1)S(1)}, u32[]{:S(2)}, u32[]{:S(2)}) collective-permute-start(bf16[3,256,128]{2,1,0:T(8,128)(2,1)S(1)} %get-tuple-element.40), channel_id=1, source_target_pairs={{0,2},{1,3},{2,0},{3,1},{4,6},{5,7},{6,4},{7,5},{8,10},{9,11},{10,... | collective-permute-start | bytes 589832 | tf_op jit(solution)/shard_map/ppermute | solution.py:68
  48.7 2.7 %collective-permute-start.8 = (bf16[13,256,128]{2,1,0:T(8,128)(2,1)S(1)}, bf16[13,256,128]{2,1,0:T(8,128)(2,1)S(1)}, u32[]{:S(2)}, u32[]{:S(2)}) collective-permute-start(bf16[13,256,128]{2,1,0:T(8,128)(2,1)S(1)} %collective-permute-done.6.refs_2_), channel_id=1, source_target_pairs={{0,1},{1,0},{2,3},{3,2},{4,5},{5,4},{6,7},{7,6},{8,9},{9,8},{10,11... | collective-permute-start | bytes 2555912 | tf_op jit(solution)/shard_map/ppermute | solution.py:68
  48.7 2.7 %collective-permute-start.9 = (bf16[3,256,128]{2,1,0:T(8,128)(2,1)S(1)}, bf16[3,256,128]{2,1,0:T(8,128)(2,1)S(1)}, u32[]{:S(2)}, u32[]{:S(2)}) collective-permute-start(bf16[3,256,128]{2,1,0:T(8,128)(2,1)S(1)} %collective-permute-done.7.refs_3_), channel_id=1, source_target_pairs={{0,1},{1,0},{2,3},{3,2},{4,5},{5,4},{6,7},{7,6},{8,9},{9,8},{10,11... | collective-permute-start | bytes 589832 | tf_op jit(solution)/shard_map/ppermute | solution.py:68

commit v7 on v6

--- a/solution.py
+++ b/solution.py
@@ -94,13 +94,13 @@
     return pltpu.SemaphoreType.DMA((sum(len(spans) for _, spans, _ in blocks),))
 
 
-def half_products(sectors, distances, place, basis, fermion, pieces, ready=lambda sector: None):
+def half_products(sectors, distances, place, basis, fermion, pieces, ready=lambda sector: None, slots=None):
     flavours, _, _, width = fermion.shape
     for sector in sectors:
         ready(sector)
         right = jnp.concatenate([fermion[flavour, sector] for flavour in range(flavours)], axis=1)
         for slot, distance in enumerate(distances):
-            column = pl.multiple_of((place[0] ^ distance) * width, width)
+            column = slots[slot] if slots else pl.multiple_of((place[0] ^ distance) * width, width)
             block = lax.dot_general(
                 basis[sector, :, pl.ds(column, width)],
                 right,
@@ -113,6 +113,7 @@
 
 def part_kernel(blocks, unit, distances, place, basis, fermion, sent, *refs):
     *pieces, left, right, sems, half_sems = refs
+    width = fermion.shape[3]
     copies = part_copies(blocks, unit, place, basis, sent, sems)
     for copy in copies:
         copy.start()
@@ -121,8 +122,15 @@
     def _():
         held = [
             [
-                pltpu.make_async_copy(basis.at[sector], left.at[sector], half_sems.at[sector, 0]),
-                pltpu.make_async_copy(fermion.at[:, sector], right.at[:, sector], half_sems.at[sector, 1]),
+                pltpu.make_async_copy(fermion.at[:, sector], right.at[:, sector], half_sems.at[sector, 0]),
+                *(
+                    pltpu.make_async_copy(
+                        basis.at[sector, :, pl.ds(pl.multiple_of((place[0] ^ distance) * width, width), width)],
+                        left.at[sector, :, pl.ds(slot * width, width)],
+                        half_sems.at[sector, 1 + slot],
+                    )
+                    for slot, distance in enumerate(distances)
+                ),
             ]
             for sector in range(basis.shape[0])
         ]
@@ -134,7 +142,8 @@
             for copy in held[sector]:
                 copy.wait()
 
-        half_products(range(basis.shape[0]), distances, place, left, right, pieces, ready)
+        slots = [slot * width for slot in range(len(distances))]
+        half_products(range(basis.shape[0]), distances, place, left, right, pieces, ready, slots)
 
     for copy in copies:
         copy.wait()
@@ -153,10 +162,10 @@
         shapes,
         [WHOLE] * len(shapes),
         [
-            pltpu.VMEM((sectors, depth, depth), jnp.bfloat16),
+            pltpu.VMEM((sectors, depth, len(distances) * width), jnp.bfloat16),
             pltpu.VMEM((flavours, sectors, depth, width), jnp.bfloat16),
             part_sems(blocks),
-            pltpu.SemaphoreType.DMA((sectors, 2)),
+            pltpu.SemaphoreType.DMA((sectors, 1 + len(distances))),
         ],
     )
 

time: 53.7 us -> 53.3 us (level)
  transfers between devices with their start and end apart: 10 -> 10, of which waited for: 7 -> 7; matrix products, arithmetic and copies ran while one was open for 0% -> 0% of each run, Pallas kernels for 13% -> 14%
where the time goes in v7:
time: 53.3 us; the launch traced here: 53.2 us
  waiting for transfers between devices  26.7 us (50%)
  Pallas kernels  13.8 us (26%)
  starting transfers between devices  12.5 us (23%)
    ppermute x8, waiting for transfers between devices, swapped(): lax.ppermute(block, 'slab', [(i, i ^ distance) for i in range(lax.axis_si...  21.4 us
    pallas_call x8, Pallas kernels, kernel_call(): pl.pallas_call(kernel, out_shape=shapes, in_specs=specs, out_specs=out_sp...  13.8 us
    ppermute x2, starting transfers between devices, previous(): lax.ppermute(block, 'sec', [((i + 1) % count, i) for i in range(count)])  7.12 us
    ppermute x8, starting transfers between devices, swapped(): lax.ppermute(block, 'slab', [(i, i ^ distance) for i in range(lax.axis_si...  5.4 us
    ppermute x2, waiting for transfers between devices, previous(): lax.ppermute(block, 'sec', [((i + 1) % count, i) for i in range(count)])  5.39 us
  transfers between devices with their start and end apart: 10, of which 7 were waited for; matrix products, arithmetic and copies ran while one was open for 0% of the time, Pallas kernels for 14%

profile of v7, /device:TPU:0, one launch (start us, length us, event | category | flops | bytes accessed | tf_op | source)
XLA Modules:
  0.0 53.2 jit_solution(3597281536023598063)
XLA Ops:
  0.0 0.0 copy-start
  0.0 0.0 copy-start.1
  0.0 4.4 %part.1 = (bf16[4,256,512]{2,1,0:T(8,128)(2,1)S(1)}, bf16[2,3,256,256]{3,2,1,0:T(8,128)(2,1)S(1)}, bf16[2,3,256,256]{3,2,1,0:T(8,128)(2,1)S(1)}) custom-call(bf16[2,1024,1024]{2,1,0:T(8,128)(2,1)} %refs_0_.7, bf16[3,2,1024,256]{3,2,1,0:T(8,128)(2,1)} %refs_1_.5), custom_call_target="tpu_custom_call" | custom-call | tf_op jit(solution)/shard_map/part/pallas_call | solution.py:34
  4.4 3.2 %collective-permute-start.3 = (bf16[4,256,512]{2,1,0:T(8,128)(2,1)S(1)}, bf16[4,256,512]{2,1,0:T(8,128)(2,1)S(1)}, u32[]{:S(2)}, u32[]{:S(2)}) collective-permute-start(bf16[4,256,512]{2,1,0:T(8,128)(2,1)S(1)} %get-tuple-element.33), channel_id=1, source_target_pairs={{4,0},{8,4},{12,8},{16,12},{20,16},{24,20},{28,24},{0,28},{5,1},{9... | collective-permute-start | bytes 3145736 | tf_op jit(solution)/shard_map/ppermute | solution.py:64
  7.6 0.0 copy-done
  7.6 0.0 copy-done.1
  7.6 1.5 %collective-permute-start.1 = (bf16[2,3,256,256]{3,2,1,0:T(8,128)(2,1)S(1)}, bf16[2,3,256,256]{3,2,1,0:T(8,128)(2,1)S(1)}, u32[]{:S(2)}, u32[]{:S(2)}) collective-permute-start(bf16[2,3,256,256]{3,2,1,0:T(8,128)(2,1)S(1)} %get-tuple-element.30.refs_2_), channel_id=1, source_target_pairs={{0,2},{1,3},{2,0},{3,1},{4,6},{5,7},{6,4},{7,5},{8,10},{9,11},{10,... | collective-permute-start | bytes 2359304 | tf_op jit(solution)/shard_map/ppermute | solution.py:68
  9.1 2.2 %near.1 = (bf16[2,3,256,256]{3,2,1,0:T(8,128)(2,1)S(1)}, bf16[2,3,256,256]{3,2,1,0:T(8,128)(2,1)S(1)}, bf16[13,256,128]{2,1,0:T(8,128)(2,1)S(1)}) custom-call(bf16[2,1024,1024]{2,1,0:T(8,128)(2,1)S(1)} %copy-done, bf16[3,2,1024,256]{3,2,1,0:T(8,128)(2,1)S(1)} %copy-done.1, bf16[2,3,256,256]{3,2,1,0:T(8,128)(2,1)S(1)} %get-tuple-element.30.refs_2_), custom_call_target="tpu_custom_call" | custom-call | tf_op jit(solution)/shard_map/near/pallas_call | solution.py:34
  11.3 0.1 collective-permute-start.2
  11.4 3.9 %collective-permute-start.6 = (bf16[13,256,128]{2,1,0:T(8,128)(2,1)S(1)}, bf16[13,256,128]{2,1,0:T(8,128)(2,1)S(1)}, u32[]{:S(2)}, u32[]{:S(2)}) collective-permute-start(bf16[13,256,128]{2,1,0:T(8,128)(2,1)S(1)} %get-tuple-element.39), channel_id=1, source_target_pairs={{4,0},{8,4},{12,8},{16,12},{20,16},{24,20},{28,24},{0,28},{5,1},{9... | collective-permute-start | bytes 2555912 | tf_op jit(solution)/shard_map/ppermute | solution.py:64
  15.3 0.4 collective-permute-start
  15.7 12.4 %collective-permute-done.1.refs_2_.refs_1_ = bf16[2,3,256,256]{3,2,1,0:T(8,128)(2,1)S(1)} collective-permute-done((bf16[2,3,256,256]{3,2,1,0:T(8,128)(2,1)S(1)}, bf16[2,3,256,256]{3,2,1,0:T(8,128)(2,1)S(1)}, u32[]{:S(2)}, u32[]{:S(2)}) %collective-permute-start.1) | collective-permute-done | bytes 786464 | tf_op jit(solution)/shard_map/ppermute | solution.py:68
  28.1 0.0 collective-permute-done.2.refs_1_.refs_2_
  28.1 3.1 %collective-permute-done.3.refs_0_ = bf16[4,256,512]{2,1,0:T(8,128)(2,1)S(1)} collective-permute-done((bf16[4,256,512]{2,1,0:T(8,128)(2,1)S(1)}, bf16[4,256,512]{2,1,0:T(8,128)(2,1)S(1)}, u32[]{:S(2)}, u32[]{:S(2)}) %collective-permute-start.3) | collective-permute-done | bytes 1048608 | tf_op jit(solution)/shard_map/ppermute | solution.py:64
  31.2 0.1 cut.1
  31.2 0.1 collective-permute-start.4
  31.3 0.5 collective-permute-start.5
  31.8 1.4 %collective-permute-done.4.refs_5_ = bf16[4,256,256]{2,1,0:T(8,128)(2,1)S(1)} collective-permute-done((bf16[4,256,256]{2,1,0:T(8,128)(2,1)S(1)}, bf16[4,256,256]{2,1,0:T(8,128)(2,1)S(1)}, u32[]{:S(2)}, u32[]{:S(2)}) %collective-permute-start.4) | collective-permute-done | bytes 524320 | tf_op jit(solution)/shard_map/ppermute | solution.py:68
  33.2 0.7 %collective-permute-done.5.refs_7_ = bf16[4,256,256]{2,1,0:T(8,128)(2,1)S(1)} collective-permute-done((bf16[4,256,256]{2,1,0:T(8,128)(2,1)S(1)}, bf16[4,256,256]{2,1,0:T(8,128)(2,1)S(1)}, u32[]{:S(2)}, u32[]{:S(2)}) %collective-permute-start.5) | collective-permute-done | bytes 524320 | tf_op jit(solution)/shard_map/ppermute | solution.py:68
  34.0 0.0 copy-start.2
  34.0 1.5 %gather.1 = (bf16[2,3,256,1024]{3,2,1,0:T(8,128)(2,1)S(1)}, bf16[4,2,2,256,512]{4,3,2,1,0:T(8,128)(2,1)S(1)}, bf16[4,2,2,256,512]{4,3,2,1,0:T(8,128)(2,1)S(1)}, bf16[3,256,128]{2,1,0:T(8,128)(2,1)S(1)}) custom-call(bf16[2,1024,1024]{2,1,0:T(8,128)(2,1)S(1)} %copy-done, bf16[2,3,256,256]{3,2,1,0:T(8,128)(2,1)S(1)} %collective-permute-done.1.refs_2_.refs_1_, ...), custom_call_target="tpu_custom_call" | custom-call | tf_op jit(solution)/shard_map/gather/pallas_call | solution.py:34
  35.5 2.4 %collective-permute-start.7 = (bf16[3,256,128]{2,1,0:T(8,128)(2,1)S(1)}, bf16[3,256,128]{2,1,0:T(8,128)(2,1)S(1)}, u32[]{:S(2)}, u32[]{:S(2)}) collective-permute-start(bf16[3,256,128]{2,1,0:T(8,128)(2,1)S(1)} %get-tuple-element.40), channel_id=1, source_target_pairs={{0,2},{1,3},{2,0},{3,1},{4,6},{5,7},{6,4},{7,5},{8,10},{9,11},{10,... | collective-permute-start | bytes 589832 | tf_op jit(solution)/shard_map/ppermute | solution.py:68
  37.9 6.1 %collective-permute-done.refs_1_ = bf16[2,3,256,256]{3,2,1,0:T(8,128)(2,1)S(1)} collective-permute-done((bf16[2,3,256,256]{3,2,1,0:T(8,128)(2,1)S(1)}, bf16[2,3,256,256]{3,2,1,0:T(8,128)(2,1)S(1)}, u32[]{:S(2)}, u32[]{:S(2)}) %collective-permute-start) | collective-permute-done | bytes 786464 | tf_op jit(solution)/shard_map/ppermute | solution.py:68
  43.9 0.0 copy-done.2
  44.0 2.0 %early.1 = (bf16[2,3,256,1024]{3,2,1,0:T(8,128)(2,1)S(1)}, bf16[3,2,256,512]{3,2,1,0:T(8,128)(2,1)S(1)}) custom-call(s32[2,3]{1,0:T(2,128)S(1)} %bitcast.1, bf16[2,3,256,256]{3,2,1,0:T(8,128)(2,1)S(1)} %collective-permute-done.refs_1_, bf16[4,2,2,256,512]{4,3,2,1,0:T(8,128)(2,1)S(1)} %get-tuple-element.36.refs_2_, ...), custom_call_target="tpu_custom_call", output_to_operand_aliasing={{0}: (3, {})} | custom-call | tf_op jit(solution)/shard_map/early/pallas_call | solution.py:34
  46.0 2.3 %collective-permute-done.6.refs_2_ = bf16[13,256,128]{2,1,0:T(8,128)(2,1)S(1)} collective-permute-done((bf16[13,256,128]{2,1,0:T(8,128)(2,1)S(1)}, bf16[13,256,128]{2,1,0:T(8,128)(2,1)S(1)}, u32[]{:S(2)}, u32[]{:S(2)}) %collective-permute-start.6) | collective-permute-done | bytes 852000 | tf_op jit(solution)/shard_map/ppermute | solution.py:64
  48.3 0.0 collective-permute-done.7.refs_3_
  48.3 0.0 collective-permute-start.8
  48.3 0.5 collective-permute-start.9
  48.8 1.4 %own_rows.1 = (f32[3,2,256,512]{3,2,1,0:T(8,128)S(1)}, bf16[4,2,2,256,512]{4,3,2,1,0:T(8,128)(2,1)S(1)}) custom-call(s32[2,3]{1,0:T(2,128)S(1)} %bitcast.2, bf16[2,3,256,1024]{3,2,1,0:T(8,128)(2,1)S(1)} %get-tuple-element.38.refs_1_, bf16[13,256,128]{2,1,0:T(8,128)(2,1)S(1)} %collective-permute-done.6.refs_2_, ...), custom_call_target="tpu_custom_call", output_to_operand_aliasing={{1}: (4, {})} | custom-call | tf_op jit(solution)/shard_map/own_rows/pallas_call | solution.py:34
  50.2 0.8 %collective-permute-done.9.refs_5_ = bf16[3,256,128]{2,1,0:T(8,128)(2,1)S(1)} collective-permute-done((bf16[3,256,128]{2,1,0:T(8,128)(2,1)S(1)}, bf16[3,256,128]{2,1,0:T(8,128)(2,1)S(1)}, u32[]{:S(2)}, u32[]{:S(2)}) %collective-permute-start.9) | collective-permute-done | bytes 196640 | tf_op jit(solution)/shard_map/ppermute | solution.py:68
  51.0 0.0 collective-permute-done.8.refs_4_
  51.0 2.2 %late.1 = (bf16[3,2,256,1024]{3,2,1,0:T(8,128)(2,1)}, bf16[4,2,2,256,512]{4,3,2,1,0:T(8,128)(2,1)S(1)}) custom-call(s32[2,3]{1,0:T(2,128)S(1)} %bitcast.3, bf16[2,3,256,1024]{3,2,1,0:T(8,128)(2,1)S(1)} %get-tuple-element.38.refs_1_, f32[3,2,256,512]{3,2,1,0:T(8,128)S(1)} %get-tuple-element.45.refs_2_, ...), custom_call_target="tpu_custom_call", output_to_operand_aliasing={{1}: (6, {})} | custom-call | tf_op jit(solution)/shard_map/late/pallas_call | solution.py:34
  (1 shorter events, 0.0 us)
Async XLA Ops:
  0.0 7.6 %copy-start = (bf16[2,1024,1024]{2,1,0:T(8,128)(2,1)S(1)}, bf16[2,1024,1024]{2,1,0:T(8,128)(2,1)}, u32[]{:S(2)}) copy-start(bf16[2,1024,1024]{2,1,0:T(8,128)(2,1)} %refs_0_.7) | copy-start | bytes 12582916
  0.0 7.6 %copy-start.1 = (bf16[3,2,1024,256]{3,2,1,0:T(8,128)(2,1)S(1)}, bf16[3,2,1024,256]{3,2,1,0:T(8,128)(2,1)}, u32[]{:S(2)}) copy-start(bf16[3,2,1024,256]{3,2,1,0:T(8,128)(2,1)} %refs_1_.5) | copy-start | bytes 9437188
  4.4 26.8 %collective-permute-start.3 = (bf16[4,256,512]{2,1,0:T(8,128)(2,1)S(1)}, bf16[4,256,512]{2,1,0:T(8,128)(2,1)S(1)}, u32[]{:S(2)}, u32[]{:S(2)}) collective-permute-start(bf16[4,256,512]{2,1,0:T(8,128)(2,1)S(1)} %get-tuple-element.33), channel_id=1, source_target_pairs={{4,0},{8,4},{12,8},{16,12},{20,16},{24,20},{28,24},{0,28},{5,1},{9... | collective-permute-start | bytes 3145736 | tf_op jit(solution)/shard_map/ppermute | solution.py:64
  7.6 20.5 %collective-permute-start.1 = (bf16[2,3,256,256]{3,2,1,0:T(8,128)(2,1)S(1)}, bf16[2,3,256,256]{3,2,1,0:T(8,128)(2,1)S(1)}, u32[]{:S(2)}, u32[]{:S(2)}) collective-permute-start(bf16[2,3,256,256]{3,2,1,0:T(8,128)(2,1)S(1)} %get-tuple-element.30.refs_2_), channel_id=1, source_target_pairs={{0,2},{1,3},{2,0},{3,1},{4,6},{5,7},{6,4},{7,5},{8,10},{9,11},{10,... | collective-permute-start | bytes 2359304 | tf_op jit(solution)/shard_map/ppermute | solution.py:68
  11.3 16.8 %collective-permute-start.2 = (bf16[2,3,256,256]{3,2,1,0:T(8,128)(2,1)S(1)}, bf16[2,3,256,256]{3,2,1,0:T(8,128)(2,1)S(1)}, u32[]{:S(2)}, u32[]{:S(2)}) collective-permute-start(bf16[2,3,256,256]{3,2,1,0:T(8,128)(2,1)S(1)} %get-tuple-element.31), channel_id=1, source_target_pairs={{0,1},{1,0},{2,3},{3,2},{4,5},{5,4},{6,7},{7,6},{8,9},{9,8},{10,11... | collective-permute-start | bytes 2359304 | tf_op jit(solution)/shard_map/ppermute | solution.py:68
  11.4 36.9 %collective-permute-start.6 = (bf16[13,256,128]{2,1,0:T(8,128)(2,1)S(1)}, bf16[13,256,128]{2,1,0:T(8,128)(2,1)S(1)}, u32[]{:S(2)}, u32[]{:S(2)}) collective-permute-start(bf16[13,256,128]{2,1,0:T(8,128)(2,1)S(1)} %get-tuple-element.39), channel_id=1, source_target_pairs={{4,0},{8,4},{12,8},{16,12},{20,16},{24,20},{28,24},{0,28},{5,1},{9... | collective-permute-start | bytes 2555912 | tf_op jit(solution)/shard_map/ppermute | solution.py:64
  15.3 28.6 %collective-permute-start = (bf16[2,3,256,256]{3,2,1,0:T(8,128)(2,1)S(1)}, bf16[2,3,256,256]{3,2,1,0:T(8,128)(2,1)S(1)}, u32[]{:S(2)}, u32[]{:S(2)}) collective-permute-start(bf16[2,3,256,256]{3,2,1,0:T(8,128)(2,1)S(1)} %get-tuple-element.29), channel_id=1, source_target_pairs={{0,3},{1,2},{2,1},{3,0},{4,7},{5,6},{6,5},{7,4},{8,11},{9,10},{10,... | collective-permute-start | bytes 2359304 | tf_op jit(solution)/shard_map/ppermute | solution.py:68
  31.2 2.0 %collective-permute-start.4 = (bf16[4,256,256]{2,1,0:T(8,128)(2,1)S(1)}, bf16[4,256,256]{2,1,0:T(8,128)(2,1)S(1)}, u32[]{:S(2)}, u32[]{:S(2)}) collective-permute-start(bf16[4,256,256]{2,1,0:T(8,128)(2,1)S(1)} %get-tuple-element.34.refs_4_), channel_id=1, source_target_pairs={{0,1},{1,0},{2,3},{3,2},{4,5},{5,4},{6,7},{7,6},{8,9},{9,8},{10,11... | collective-permute-start | bytes 1572872 | tf_op jit(solution)/shard_map/ppermute | solution.py:68
  31.3 2.6 %collective-permute-start.5 = (bf16[4,256,256]{2,1,0:T(8,128)(2,1)S(1)}, bf16[4,256,256]{2,1,0:T(8,128)(2,1)S(1)}, u32[]{:S(2)}, u32[]{:S(2)}) collective-permute-start(bf16[4,256,256]{2,1,0:T(8,128)(2,1)S(1)} %get-tuple-element.35.refs_6_), channel_id=1, source_target_pairs={{0,1},{1,0},{2,3},{3,2},{4,5},{5,4},{6,7},{7,6},{8,9},{9,8},{10,11... | collective-permute-start | bytes 1572872 | tf_op jit(solution)/shard_map/ppermute | solution.py:68
  34.0 10.0 %copy-start.2 = (s32[3,2]{0,1:T(2,128)S(1)}, s32[3,2]{0,1:T(2,128)}, u32[]{:S(2)}) copy-start(s32[3,2]{0,1:T(2,128)} %param.5) | copy-start | bytes 76
  35.5 12.8 %collective-permute-start.7 = (bf16[3,256,128]{2,1,0:T(8,128)(2,1)S(1)}, bf16[3,256,128]{2,1,0:T(8,128)(2,1)S(1)}, u32[]{:S(2)}, u32[]{:S(2)}) collective-permute-start(bf16[3,256,128]{2,1,0:T(8,128)(2,1)S(1)} %get-tuple-element.40), channel_id=1, source_target_pairs={{0,2},{1,3},{2,0},{3,1},{4,6},{5,7},{6,4},{7,5},{8,10},{9,11},{10,... | collective-permute-start | bytes 589832 | tf_op jit(solution)/shard_map/ppermute | solution.py:68
  48.3 2.7 %collective-permute-start.8 = (bf16[13,256,128]{2,1,0:T(8,128)(2,1)S(1)}, bf16[13,256,128]{2,1,0:T(8,128)(2,1)S(1)}, u32[]{:S(2)}, u32[]{:S(2)}) collective-permute-start(bf16[13,256,128]{2,1,0:T(8,128)(2,1)S(1)} %collective-permute-done.6.refs_2_), channel_id=1, source_target_pairs={{0,1},{1,0},{2,3},{3,2},{4,5},{5,4},{6,7},{7,6},{8,9},{9,8},{10,11... | collective-permute-start | bytes 2555912 | tf_op jit(solution)/shard_map/ppermute | solution.py:68
  48.3 2.7 %collective-permute-start.9 = (bf16[3,256,128]{2,1,0:T(8,128)(2,1)S(1)}, bf16[3,256,128]{2,1,0:T(8,128)(2,1)S(1)}, u32[]{:S(2)}, u32[]{:S(2)}) collective-permute-start(bf16[3,256,128]{2,1,0:T(8,128)(2,1)S(1)} %collective-permute-done.7.refs_3_), channel_id=1, source_target_pairs={{0,1},{1,0},{2,3},{3,2},{4,5},{5,4},{6,7},{7,6},{8,9},{9,8},{10,11... | collective-permute-start | bytes 589832 | tf_op jit(solution)/shard_map/ppermute | solution.py:68

commit v8 on v7

--- a/solution.py
+++ b/solution.py
@@ -322,28 +322,51 @@
     return jnp.dot(left[sector, flavour], rows, preferred_element_type=jnp.float32).astype(jnp.bfloat16)
 
 
-def early_kernel(distance, place, partner, half, right, _, left, stage, sem):
+def write_out(units, unit, place, sector, flavour, stage, out, sems):
+    copies, at = [], 0
+    for number, (start, count) in enumerate(units):
+        copies.append(
+            pltpu.make_async_copy(
+                stage.at[flavour, sector, :, pl.ds(at, count * unit)],
+                out.at[flavour, sector, :, pl.ds(first_column(start, place, unit), count * unit)],
+                sems.at[sector * stage.shape[0] + flavour, number],
+            )
+        )
+        copies[-1].start()
+        at += count * unit
+    return copies
+
+
+def early_kernel(units, unit, distance, place, partner, half, right, _, left, out, stage, sem, out_sems):
     run([half_copy(half, distance, place, left, sem)])
     sectors, flavours = left.shape[:2]
+    copies = []
     for sector in range(sectors):
         for flavour in range(flavours):
             stage[flavour, sector] = product(place, partner, sector, flavour, left, right)
-
-
-def early_products(partner, half, distance, left, right):
-    sectors, flavours, width, _ = left.shape
-    return kernel_call(
-        functools.partial(early_kernel, distance),
+            copies += write_out(units, unit, place, sector, flavour, stage, out, out_sems)
+    for copy in copies:
+        copy.wait()
+
+
+def early_products(partner, half, distance, units, unit, left, right):
+    sectors, flavours, width, depth = left.shape
+    return kernel_call(
+        functools.partial(early_kernel, units, unit, distance),
         "early",
-        (left.shape[0], left.shape[3]),
+        (sectors, depth),
         [partner, in_vmem(half), in_vmem(right), in_vmem(left)],
-        [WHOLE] + [WHOLE] * 3,
+        [WHOLE] * 4,
         [
             pltpu.VMEM(left.shape, left.dtype),
+            pltpu.HBM((flavours, sectors, width, depth), jnp.bfloat16),
+        ],
+        [WHOLE, ANY],
+        [
             pltpu.VMEM((flavours, sectors, width, right.shape[4]), jnp.bfloat16),
+            pltpu.SemaphoreType.DMA,
+            pltpu.SemaphoreType.DMA((sectors * flavours, len(units))),
         ],
-        [WHOLE] * 2,
-        [pltpu.SemaphoreType.DMA],
         {3: 0},
     )
 
@@ -398,67 +421,37 @@
     )
 
 
-def late_kernel(earlier_units, units, nexts, unit, place, partner, left, total, *refs):
-    earlier, refs = refs[: len(earlier_units)], refs[len(earlier_units) :]
-    arrays, (_, out, right, stage, sems, early_sems, out_sems) = refs[: len(nexts)], refs[len(nexts) :]
+def late_kernel(units, nexts, unit, place, partner, left, total, *refs):
+    arrays, (_, _, out, right, stage, sems, out_sems) = refs[: len(nexts)], refs[len(nexts) :]
     sectors, flavours = left.shape[:2]
-    next_here = next_copies(nexts, place, arrays, 1, right, sems, 0)
-    for copy in next_here:
-        copy.start()
-    out_copies = []
-    for result, spans in zip(earlier, earlier_units):
-        at = 0
-        for start, count in spans:
-            out_copies.append(
-                pltpu.make_async_copy(
-                    result.at[:, :, :, pl.ds(at, count * unit)],
-                    out.at[:, :, :, pl.ds(first_column(start, place, unit), count * unit)],
-                    early_sems.at[len(out_copies)],
-                )
-            )
-            out_copies[-1].start()
-            at += count * unit
-    for copy in next_here:
-        copy.wait()
+    run(next_copies(nexts, place, arrays, 1, right, sems, 0))
+    copies = []
     for sector in range(sectors):
         for flavour in range(flavours):
             rest = partial(place, partner, sector, flavour, 1, left, right)
             stage[flavour, sector] = (total[flavour, sector] + rest).astype(jnp.bfloat16)
-            at = 0
-            for number, (start, count) in enumerate(units):
-                copy = pltpu.make_async_copy(
-                    stage.at[flavour, sector, :, pl.ds(at, count * unit)],
-                    out.at[flavour, sector, :, pl.ds(first_column(start, place, unit), count * unit)],
-                    out_sems.at[sector * flavours + flavour, number],
-                )
-                copy.start()
-                out_copies.append(copy)
-                at += count * unit
-    for copy in out_copies:
+            copies += write_out(units, unit, place, sector, flavour, stage, out, out_sems)
+    for copy in copies:
         copy.wait()
 
 
-def late_products(partner, groups, nexts, unit, arrays, left, total, earlier, right):
+def late_products(partner, units, nexts, unit, arrays, left, total, right, out):
     sectors, flavours, width, depth = left.shape
-    given = [in_vmem(array) for array in (left, total, *earlier, *arrays, right)]
-    return kernel_call(
-        functools.partial(late_kernel, groups[:-1], groups[-1], nexts, unit),
+    given = [in_vmem(array) for array in (left, total, *arrays, right)]
+    return kernel_call(
+        functools.partial(late_kernel, units, nexts, unit),
         "late",
         (sectors, depth),
-        [partner, *given],
-        [WHOLE] * (1 + len(given)),
-        [
-            pltpu.HBM((flavours, sectors, width, depth), jnp.bfloat16),
-            pltpu.VMEM(right.shape, right.dtype),
-        ],
+        [partner, *given, out],
+        [WHOLE] * (1 + len(given)) + [ANY],
+        [pltpu.HBM(out.shape, out.dtype), pltpu.VMEM(right.shape, right.dtype)],
         [ANY, WHOLE],
         [
             pltpu.VMEM((flavours, sectors, width, right.shape[4]), jnp.bfloat16),
             pltpu.SemaphoreType.DMA((sum(map(len, nexts)),)),
-            pltpu.SemaphoreType.DMA((sum(map(len, groups[:-1])),)),
-            pltpu.SemaphoreType.DMA((sectors * flavours, len(groups[-1]))),
+            pltpu.SemaphoreType.DMA((sectors * flavours, len(units))),
         ],
-        {len(given): 1},
+        {len(given): 1, 1 + len(given): 0},
     )[0]
 
 
@@ -501,17 +494,15 @@
         basis, units, nexts, unit, pairs, [got2, beside, near], distances[1:], cuts
     )
     other = swapped(sent, distances[1])
-    left, early = early_products(partner, got3, distances[0], left, early_right)
-    last, other, early = lax.optimization_barrier((last, other, early))
+    left, out = early_products(partner, got3, distances[0], units[0], unit, left, early_right)
+    last, other, out = lax.optimization_barrier((last, other, out))
     last_other, other_other = swapped(last, 1), swapped(other, 1)
     nexts = [[], runs((6 - count) * unit, held[alone:])]
     for at in range(6 - count):
         nexts[0] += runs(at * unit, held)
     nexts[0] += runs((6 - count) * unit, held[:alone])
     total, late_right = own_rows(partner, [nexts], [[last, other]], left, [late_right])
-    return late_products(
-        partner, units, nexts, unit, [last_other, other_other], left, total, [early], late_right
-    )
+    return late_products(partner, units[1], nexts, unit, [last_other, other_other], left, total, late_right, out)
 
 
 def solution(mesh):

time: 53.3 us -> 53.3 us (level)
  waiting for transfers between devices: 26.7 us -> 25.9 us
  Pallas kernels: 13.8 us -> 14.6 us
    ppermute x2, waiting for transfers between devices: 5.39 us -> 4.59 us  [previous(): lax.ppermute(block, 'sec', [((i + 1) % count, i) for i in range(count)])]
    pallas_call x8, Pallas kernels: 13.8 us -> 14.6 us  [kernel_call(): pl.pallas_call(kernel, out_shape=shapes, in_specs=specs, out_specs=out_sp...]
  transfers between devices with their start and end apart: 10 -> 10, of which waited for: 7 -> 7; matrix products, arithmetic and copies ran while one was open for 0% -> 0% of each run, Pallas kernels for 14% -> 15%
where the time goes in v8:
time: 53.3 us; the launch traced here: 53.1 us
  waiting for transfers between devices  25.9 us (49%)
  Pallas kernels  14.6 us (27%)
  starting transfers between devices  12.5 us (23%)
    ppermute x8, waiting for transfers between devices, swapped(): lax.ppermute(block, 'slab', [(i, i ^ distance) for i in range(lax.axis_si...  21.4 us
    pallas_call x8, Pallas kernels, kernel_call(): pl.pallas_call(kernel, out_shape=shapes, in_specs=specs, out_specs=out_sp...  14.6 us
    ppermute x2, starting transfers between devices, previous(): lax.ppermute(block, 'sec', [((i + 1) % count, i) for i in range(count)])  7.12 us
    ppermute x8, starting transfers between devices, swapped(): lax.ppermute(block, 'slab', [(i, i ^ distance) for i in range(lax.axis_si...  5.4 us
    ppermute x2, waiting for transfers between devices, previous(): lax.ppermute(block, 'sec', [((i + 1) % count, i) for i in range(count)])  4.59 us
  transfers between devices with their start and end apart: 10, of which 7 were waited for; matrix products, arithmetic and copies ran while one was open for 0% of the time, Pallas kernels for 15%

profile of v8, /device:TPU:0, one launch (start us, length us, event | category | flops | bytes accessed | tf_op | source)
XLA Modules:
  0.0 53.1 jit_solution(16365930997678232236)
XLA Ops:
  0.0 0.0 copy-start
  0.0 0.0 copy-start.1
  0.0 4.4 %part.1 = (bf16[4,256,512]{2,1,0:T(8,128)(2,1)S(1)}, bf16[2,3,256,256]{3,2,1,0:T(8,128)(2,1)S(1)}, bf16[2,3,256,256]{3,2,1,0:T(8,128)(2,1)S(1)}) custom-call(bf16[2,1024,1024]{2,1,0:T(8,128)(2,1)} %refs_0_.7, bf16[3,2,1024,256]{3,2,1,0:T(8,128)(2,1)} %refs_1_.5), custom_call_target="tpu_custom_call" | custom-call | tf_op jit(solution)/shard_map/part/pallas_call | solution.py:34
  4.4 3.2 %collective-permute-start.3 = (bf16[4,256,512]{2,1,0:T(8,128)(2,1)S(1)}, bf16[4,256,512]{2,1,0:T(8,128)(2,1)S(1)}, u32[]{:S(2)}, u32[]{:S(2)}) collective-permute-start(bf16[4,256,512]{2,1,0:T(8,128)(2,1)S(1)} %get-tuple-element.33), channel_id=1, source_target_pairs={{4,0},{8,4},{12,8},{16,12},{20,16},{24,20},{28,24},{0,28},{5,1},{9... | collective-permute-start | bytes 3145736 | tf_op jit(solution)/shard_map/ppermute | solution.py:64
  7.6 0.0 copy-done
  7.6 0.0 copy-done.1
  7.6 1.5 %collective-permute-start.1 = (bf16[2,3,256,256]{3,2,1,0:T(8,128)(2,1)S(1)}, bf16[2,3,256,256]{3,2,1,0:T(8,128)(2,1)S(1)}, u32[]{:S(2)}, u32[]{:S(2)}) collective-permute-start(bf16[2,3,256,256]{3,2,1,0:T(8,128)(2,1)S(1)} %get-tuple-element.30.refs_2_), channel_id=1, source_target_pairs={{0,2},{1,3},{2,0},{3,1},{4,6},{5,7},{6,4},{7,5},{8,10},{9,11},{10,... | collective-permute-start | bytes 2359304 | tf_op jit(solution)/shard_map/ppermute | solution.py:68
  9.1 2.2 %near.1 = (bf16[2,3,256,256]{3,2,1,0:T(8,128)(2,1)S(1)}, bf16[2,3,256,256]{3,2,1,0:T(8,128)(2,1)S(1)}, bf16[13,256,128]{2,1,0:T(8,128)(2,1)S(1)}) custom-call(bf16[2,1024,1024]{2,1,0:T(8,128)(2,1)S(1)} %copy-done, bf16[3,2,1024,256]{3,2,1,0:T(8,128)(2,1)S(1)} %copy-done.1, bf16[2,3,256,256]{3,2,1,0:T(8,128)(2,1)S(1)} %get-tuple-element.30.refs_2_), custom_call_target="tpu_custom_call" | custom-call | tf_op jit(solution)/shard_map/near/pallas_call | solution.py:34
  11.3 0.1 collective-permute-start.2
  11.4 3.9 %collective-permute-start.6 = (bf16[13,256,128]{2,1,0:T(8,128)(2,1)S(1)}, bf16[13,256,128]{2,1,0:T(8,128)(2,1)S(1)}, u32[]{:S(2)}, u32[]{:S(2)}) collective-permute-start(bf16[13,256,128]{2,1,0:T(8,128)(2,1)S(1)} %get-tuple-element.39), channel_id=1, source_target_pairs={{4,0},{8,4},{12,8},{16,12},{20,16},{24,20},{28,24},{0,28},{5,1},{9... | collective-permute-start | bytes 2555912 | tf_op jit(solution)/shard_map/ppermute | solution.py:64
  15.3 0.4 collective-permute-start
  15.7 12.4 %collective-permute-done.1.refs_2_.refs_1_ = bf16[2,3,256,256]{3,2,1,0:T(8,128)(2,1)S(1)} collective-permute-done((bf16[2,3,256,256]{3,2,1,0:T(8,128)(2,1)S(1)}, bf16[2,3,256,256]{3,2,1,0:T(8,128)(2,1)S(1)}, u32[]{:S(2)}, u32[]{:S(2)}) %collective-permute-start.1) | collective-permute-done | bytes 786464 | tf_op jit(solution)/shard_map/ppermute | solution.py:68
  28.1 0.0 collective-permute-done.2.refs_1_.refs_2_
  28.1 3.1 %collective-permute-done.3.refs_0_ = bf16[4,256,512]{2,1,0:T(8,128)(2,1)S(1)} collective-permute-done((bf16[4,256,512]{2,1,0:T(8,128)(2,1)S(1)}, bf16[4,256,512]{2,1,0:T(8,128)(2,1)S(1)}, u32[]{:S(2)}, u32[]{:S(2)}) %collective-permute-start.3) | collective-permute-done | bytes 1048608 | tf_op jit(solution)/shard_map/ppermute | solution.py:64
  31.2 0.1 cut.1
  31.2 0.1 collective-permute-start.4
  31.3 0.5 collective-permute-start.5
  31.8 1.4 %collective-permute-done.4.refs_5_ = bf16[4,256,256]{2,1,0:T(8,128)(2,1)S(1)} collective-permute-done((bf16[4,256,256]{2,1,0:T(8,128)(2,1)S(1)}, bf16[4,256,256]{2,1,0:T(8,128)(2,1)S(1)}, u32[]{:S(2)}, u32[]{:S(2)}) %collective-permute-start.4) | collective-permute-done | bytes 524320 | tf_op jit(solution)/shard_map/ppermute | solution.py:68
  33.2 0.7 %collective-permute-done.5.refs_7_ = bf16[4,256,256]{2,1,0:T(8,128)(2,1)S(1)} collective-permute-done((bf16[4,256,256]{2,1,0:T(8,128)(2,1)S(1)}, bf16[4,256,256]{2,1,0:T(8,128)(2,1)S(1)}, u32[]{:S(2)}, u32[]{:S(2)}) %collective-permute-start.5) | collective-permute-done | bytes 524320 | tf_op jit(solution)/shard_map/ppermute | solution.py:68
  34.0 0.0 copy-start.2
  34.0 1.5 %gather.1 = (bf16[2,3,256,1024]{3,2,1,0:T(8,128)(2,1)S(1)}, bf16[4,2,2,256,512]{4,3,2,1,0:T(8,128)(2,1)S(1)}, bf16[4,2,2,256,512]{4,3,2,1,0:T(8,128)(2,1)S(1)}, bf16[3,256,128]{2,1,0:T(8,128)(2,1)S(1)}) custom-call(bf16[2,1024,1024]{2,1,0:T(8,128)(2,1)S(1)} %copy-done, bf16[2,3,256,256]{3,2,1,0:T(8,128)(2,1)S(1)} %collective-permute-done.1.refs_2_.refs_1_, ...), custom_call_target="tpu_custom_call" | custom-call | tf_op jit(solution)/shard_map/gather/pallas_call | solution.py:34
  35.5 2.4 %collective-permute-start.7 = (bf16[3,256,128]{2,1,0:T(8,128)(2,1)S(1)}, bf16[3,256,128]{2,1,0:T(8,128)(2,1)S(1)}, u32[]{:S(2)}, u32[]{:S(2)}) collective-permute-start(bf16[3,256,128]{2,1,0:T(8,128)(2,1)S(1)} %get-tuple-element.40), channel_id=1, source_target_pairs={{0,2},{1,3},{2,0},{3,1},{4,6},{5,7},{6,4},{7,5},{8,10},{9,11},{10,... | collective-permute-start | bytes 589832 | tf_op jit(solution)/shard_map/ppermute | solution.py:68
  37.9 6.1 %collective-permute-done.refs_1_ = bf16[2,3,256,256]{3,2,1,0:T(8,128)(2,1)S(1)} collective-permute-done((bf16[2,3,256,256]{3,2,1,0:T(8,128)(2,1)S(1)}, bf16[2,3,256,256]{3,2,1,0:T(8,128)(2,1)S(1)}, u32[]{:S(2)}, u32[]{:S(2)}) %collective-permute-start) | collective-permute-done | bytes 786464 | tf_op jit(solution)/shard_map/ppermute | solution.py:68
  43.9 0.0 copy-done.2
  44.0 2.8 %early.1 = (bf16[2,3,256,1024]{3,2,1,0:T(8,128)(2,1)S(1)}, bf16[3,2,256,1024]{3,2,1,0:T(8,128)(2,1)}) custom-call(s32[2,3]{1,0:T(2,128)S(1)} %bitcast.1, bf16[2,3,256,256]{3,2,1,0:T(8,128)(2,1)S(1)} %collective-permute-done.refs_1_, bf16[4,2,2,256,512]{4,3,2,1,0:T(8,128)(2,1)S(1)} %get-tuple-element.36.refs_2_, ...), custom_call_target="tpu_custom_call", output_to_operand_aliasing={{0}: (3, {})} | custom-call | tf_op jit(solution)/shard_map/early/pallas_call | solution.py:34
  46.8 1.5 %collective-permute-done.6.refs_2_ = bf16[13,256,128]{2,1,0:T(8,128)(2,1)S(1)} collective-permute-done((bf16[13,256,128]{2,1,0:T(8,128)(2,1)S(1)}, bf16[13,256,128]{2,1,0:T(8,128)(2,1)S(1)}, u32[]{:S(2)}, u32[]{:S(2)}) %collective-permute-start.6) | collective-permute-done | bytes 852000 | tf_op jit(solution)/shard_map/ppermute | solution.py:64
  48.3 0.0 collective-permute-done.7.refs_3_
  48.3 0.0 collective-permute-start.8
  48.3 0.5 collective-permute-start.9
  48.8 1.4 %own_rows.1 = (f32[3,2,256,512]{3,2,1,0:T(8,128)S(1)}, bf16[4,2,2,256,512]{4,3,2,1,0:T(8,128)(2,1)S(1)}) custom-call(s32[2,3]{1,0:T(2,128)S(1)} %bitcast.2, bf16[2,3,256,1024]{3,2,1,0:T(8,128)(2,1)S(1)} %get-tuple-element.38.refs_1_, bf16[13,256,128]{2,1,0:T(8,128)(2,1)S(1)} %collective-permute-done.6.refs_2_, ...), custom_call_target="tpu_custom_call", output_to_operand_aliasing={{1}: (4, {})} | custom-call | tf_op jit(solution)/shard_map/own_rows/pallas_call | solution.py:34
  50.2 0.8 %collective-permute-done.9.refs_4_ = bf16[3,256,128]{2,1,0:T(8,128)(2,1)S(1)} collective-permute-done((bf16[3,256,128]{2,1,0:T(8,128)(2,1)S(1)}, bf16[3,256,128]{2,1,0:T(8,128)(2,1)S(1)}, u32[]{:S(2)}, u32[]{:S(2)}) %collective-permute-start.9) | collective-permute-done | bytes 196640 | tf_op jit(solution)/shard_map/ppermute | solution.py:68
  51.0 0.0 collective-permute-done.8.refs_3_
  51.0 2.2 %late.1 = (bf16[3,2,256,1024]{3,2,1,0:T(8,128)(2,1)}, bf16[4,2,2,256,512]{4,3,2,1,0:T(8,128)(2,1)S(1)}) custom-call(s32[2,3]{1,0:T(2,128)S(1)} %bitcast.3, bf16[2,3,256,1024]{3,2,1,0:T(8,128)(2,1)S(1)} %get-tuple-element.38.refs_1_, f32[3,2,256,512]{3,2,1,0:T(8,128)S(1)} %get-tuple-element.45.refs_2_, ...), custom_call_target="tpu_custom_call", output_to_operand_aliasing={{1}: (5, {}), {0}: (6, {})} | custom-call | tf_op jit(solution)/shard_map/late/pallas_call | solution.py:34
  (1 shorter events, 0.0 us)
Async XLA Ops:
  0.0 7.6 %copy-start = (bf16[2,1024,1024]{2,1,0:T(8,128)(2,1)S(1)}, bf16[2,1024,1024]{2,1,0:T(8,128)(2,1)}, u32[]{:S(2)}) copy-start(bf16[2,1024,1024]{2,1,0:T(8,128)(2,1)} %refs_0_.7) | copy-start | bytes 12582916
  0.0 7.6 %copy-start.1 = (bf16[3,2,1024,256]{3,2,1,0:T(8,128)(2,1)S(1)}, bf16[3,2,1024,256]{3,2,1,0:T(8,128)(2,1)}, u32[]{:S(2)}) copy-start(bf16[3,2,1024,256]{3,2,1,0:T(8,128)(2,1)} %refs_1_.5) | copy-start | bytes 9437188
  4.4 26.8 %collective-permute-start.3 = (bf16[4,256,512]{2,1,0:T(8,128)(2,1)S(1)}, bf16[4,256,512]{2,1,0:T(8,128)(2,1)S(1)}, u32[]{:S(2)}, u32[]{:S(2)}) collective-permute-start(bf16[4,256,512]{2,1,0:T(8,128)(2,1)S(1)} %get-tuple-element.33), channel_id=1, source_target_pairs={{4,0},{8,4},{12,8},{16,12},{20,16},{24,20},{28,24},{0,28},{5,1},{9... | collective-permute-start | bytes 3145736 | tf_op jit(solution)/shard_map/ppermute | solution.py:64
  7.6 20.5 %collective-permute-start.1 = (bf16[2,3,256,256]{3,2,1,0:T(8,128)(2,1)S(1)}, bf16[2,3,256,256]{3,2,1,0:T(8,128)(2,1)S(1)}, u32[]{:S(2)}, u32[]{:S(2)}) collective-permute-start(bf16[2,3,256,256]{3,2,1,0:T(8,128)(2,1)S(1)} %get-tuple-element.30.refs_2_), channel_id=1, source_target_pairs={{0,2},{1,3},{2,0},{3,1},{4,6},{5,7},{6,4},{7,5},{8,10},{9,11},{10,... | collective-permute-start | bytes 2359304 | tf_op jit(solution)/shard_map/ppermute | solution.py:68
  11.3 16.8 %collective-permute-start.2 = (bf16[2,3,256,256]{3,2,1,0:T(8,128)(2,1)S(1)}, bf16[2,3,256,256]{3,2,1,0:T(8,128)(2,1)S(1)}, u32[]{:S(2)}, u32[]{:S(2)}) collective-permute-start(bf16[2,3,256,256]{3,2,1,0:T(8,128)(2,1)S(1)} %get-tuple-element.31), channel_id=1, source_target_pairs={{0,1},{1,0},{2,3},{3,2},{4,5},{5,4},{6,7},{7,6},{8,9},{9,8},{10,11... | collective-permute-start | bytes 2359304 | tf_op jit(solution)/shard_map/ppermute | solution.py:68
  11.4 36.9 %collective-permute-start.6 = (bf16[13,256,128]{2,1,0:T(8,128)(2,1)S(1)}, bf16[13,256,128]{2,1,0:T(8,128)(2,1)S(1)}, u32[]{:S(2)}, u32[]{:S(2)}) collective-permute-start(bf16[13,256,128]{2,1,0:T(8,128)(2,1)S(1)} %get-tuple-element.39), channel_id=1, source_target_pairs={{4,0},{8,4},{12,8},{16,12},{20,16},{24,20},{28,24},{0,28},{5,1},{9... | collective-permute-start | bytes 2555912 | tf_op jit(solution)/shard_map/ppermute | solution.py:64
  15.3 28.6 %collective-permute-start = (bf16[2,3,256,256]{3,2,1,0:T(8,128)(2,1)S(1)}, bf16[2,3,256,256]{3,2,1,0:T(8,128)(2,1)S(1)}, u32[]{:S(2)}, u32[]{:S(2)}) collective-permute-start(bf16[2,3,256,256]{3,2,1,0:T(8,128)(2,1)S(1)} %get-tuple-element.29), channel_id=1, source_target_pairs={{0,3},{1,2},{2,1},{3,0},{4,7},{5,6},{6,5},{7,4},{8,11},{9,10},{10,... | collective-permute-start | bytes 2359304 | tf_op jit(solution)/shard_map/ppermute | solution.py:68
  31.2 2.0 %collective-permute-start.4 = (bf16[4,256,256]{2,1,0:T(8,128)(2,1)S(1)}, bf16[4,256,256]{2,1,0:T(8,128)(2,1)S(1)}, u32[]{:S(2)}, u32[]{:S(2)}) collective-permute-start(bf16[4,256,256]{2,1,0:T(8,128)(2,1)S(1)} %get-tuple-element.34.refs_4_), channel_id=1, source_target_pairs={{0,1},{1,0},{2,3},{3,2},{4,5},{5,4},{6,7},{7,6},{8,9},{9,8},{10,11... | collective-permute-start | bytes 1572872 | tf_op jit(solution)/shard_map/ppermute | solution.py:68
  31.3 2.6 %collective-permute-start.5 = (bf16[4,256,256]{2,1,0:T(8,128)(2,1)S(1)}, bf16[4,256,256]{2,1,0:T(8,128)(2,1)S(1)}, u32[]{:S(2)}, u32[]{:S(2)}) collective-permute-start(bf16[4,256,256]{2,1,0:T(8,128)(2,1)S(1)} %get-tuple-element.35.refs_6_), channel_id=1, source_target_pairs={{0,1},{1,0},{2,3},{3,2},{4,5},{5,4},{6,7},{7,6},{8,9},{9,8},{10,11... | collective-permute-start | bytes 1572872 | tf_op jit(solution)/shard_map/ppermute | solution.py:68
  34.0 10.0 %copy-start.2 = (s32[3,2]{0,1:T(2,128)S(1)}, s32[3,2]{0,1:T(2,128)}, u32[]{:S(2)}) copy-start(s32[3,2]{0,1:T(2,128)} %param.5) | copy-start | bytes 76
  35.5 12.8 %collective-permute-start.7 = (bf16[3,256,128]{2,1,0:T(8,128)(2,1)S(1)}, bf16[3,256,128]{2,1,0:T(8,128)(2,1)S(1)}, u32[]{:S(2)}, u32[]{:S(2)}) collective-permute-start(bf16[3,256,128]{2,1,0:T(8,128)(2,1)S(1)} %get-tuple-element.40), channel_id=1, source_target_pairs={{0,2},{1,3},{2,0},{3,1},{4,6},{5,7},{6,4},{7,5},{8,10},{9,11},{10,... | collective-permute-start | bytes 589832 | tf_op jit(solution)/shard_map/ppermute | solution.py:68
  48.3 2.7 %collective-permute-start.8 = (bf16[13,256,128]{2,1,0:T(8,128)(2,1)S(1)}, bf16[13,256,128]{2,1,0:T(8,128)(2,1)S(1)}, u32[]{:S(2)}, u32[]{:S(2)}) collective-permute-start(bf16[13,256,128]{2,1,0:T(8,128)(2,1)S(1)} %collective-permute-done.6.refs_2_), channel_id=1, source_target_pairs={{0,1},{1,0},{2,3},{3,2},{4,5},{5,4},{6,7},{7,6},{8,9},{9,8},{10,11... | collective-permute-start | bytes 2555912 | tf_op jit(solution)/shard_map/ppermute | solution.py:68
  48.3 2.7 %collective-permute-start.9 = (bf16[3,256,128]{2,1,0:T(8,128)(2,1)S(1)}, bf16[3,256,128]{2,1,0:T(8,128)(2,1)S(1)}, u32[]{:S(2)}, u32[]{:S(2)}) collective-permute-start(bf16[3,256,128]{2,1,0:T(8,128)(2,1)S(1)} %collective-permute-done.7.refs_3_), channel_id=1, source_target_pairs={{0,1},{1,0},{2,3},{3,2},{4,5},{5,4},{6,7},{7,6},{8,9},{9,8},{10,11... | collective-permute-start | bytes 589832 | tf_op jit(solution)/shard_map/ppermute | solution.py:68

commit v9 on v7

--- a/solution.py
+++ b/solution.py
@@ -475,11 +475,12 @@
     first_blocks = [(sector, units[0], slab) for sector, slab in held]
     last_blocks = [(sector, ((start, 1),), slab) for start in range(count, 6) for sector, slab in held]
     last_blocks += [(sector, ((OTHER, 1),), slab) for sector, slab in held[:alone]]
-    first_part, *far = basis_part(basis, fermion, first_blocks, unit, distances[:2])
+    first_part, *far = basis_part(basis, fermion, first_blocks, unit, distances[1:2])
     first = previous(first_part)
-    far3, far2 = far_blocks(basis, fermion, distances[:2], far)
+    far2 = far_blocks(basis, fermion, distances[1:2], far)[0]
+    rest = distances[:1] + distances[2:]
+    far3, mine, near, last_part = near_blocks(basis, fermion, last_blocks, unit, rest, far2)
     got3, got2 = swapped(far3, distances[0]), swapped(far2, distances[1])
-    mine, near, last_part = near_blocks(basis, fermion, last_blocks, unit, distances[2:], far2)
     beside, last = swapped(mine, distances[2]), previous(last_part)
 
     def runs(column, blocks):

time: 53.3 us -> 53.3 us (level)
  starting transfers between devices: 12.5 us -> 11.7 us
  waiting for transfers between devices: 26.7 us -> 27.5 us
    ppermute x8, starting transfers between devices: 5.4 us -> 4.61 us  [swapped(): lax.ppermute(block, 'slab', [(i, i ^ distance) for i in range(lax.axis_si...]
    ppermute x8, waiting for transfers between devices: 21.4 us -> 22.1 us  [swapped(): lax.ppermute(block, 'slab', [(i, i ^ distance) for i in range(lax.axis_si...]
  transfers between devices with their start and end apart: 10 -> 10, of which waited for: 7 -> 7; matrix products, arithmetic and copies ran while one was open for 0% -> 0% of each run, Pallas kernels for 14% -> 15%
where the time goes in v9:
time: 53.3 us; the launch traced here: 53.2 us
  waiting for transfers between devices  27.5 us (52%)
  Pallas kernels  13.9 us (26%)
  starting transfers between devices  11.7 us (22%)
    ppermute x8, waiting for transfers between devices, swapped(): lax.ppermute(block, 'slab', [(i, i ^ distance) for i in range(lax.axis_si...  22.1 us
    pallas_call x8, Pallas kernels, kernel_call(): pl.pallas_call(kernel, out_shape=shapes, in_specs=specs, out_specs=out_sp...  13.9 us
    ppermute x2, starting transfers between devices, previous(): lax.ppermute(block, 'sec', [((i + 1) % count, i) for i in range(count)])  7.06 us
    ppermute x2, waiting for transfers between devices, previous(): lax.ppermute(block, 'sec', [((i + 1) % count, i) for i in range(count)])  5.39 us
    ppermute x8, starting transfers between devices, swapped(): lax.ppermute(block, 'slab', [(i, i ^ distance) for i in range(lax.axis_si...  4.61 us
  transfers between devices with their start and end apart: 10, of which 7 were waited for; matrix products, arithmetic and copies ran while one was open for 0% of the time, Pallas kernels for 15%

profile of v9, /device:TPU:0, one launch (start us, length us, event | category | flops | bytes accessed | tf_op | source)
XLA Modules:
  0.0 53.2 jit_solution(3443082282404520611)
XLA Ops:
  0.0 0.0 copy-start
  0.0 0.0 copy-start.1
  0.0 3.7 %part.1 = (bf16[4,256,512]{2,1,0:T(8,128)(2,1)S(1)}, bf16[2,3,256,256]{3,2,1,0:T(8,128)(2,1)S(1)}) custom-call(bf16[2,1024,1024]{2,1,0:T(8,128)(2,1)} %refs_0_.7, bf16[3,2,1024,256]{3,2,1,0:T(8,128)(2,1)} %refs_1_.5), custom_call_target="tpu_custom_call" | custom-call | tf_op jit(solution)/shard_map/part/pallas_call | solution.py:34
  3.7 3.9 %collective-permute-start.3 = (bf16[4,256,512]{2,1,0:T(8,128)(2,1)S(1)}, bf16[4,256,512]{2,1,0:T(8,128)(2,1)S(1)}, u32[]{:S(2)}, u32[]{:S(2)}) collective-permute-start(bf16[4,256,512]{2,1,0:T(8,128)(2,1)S(1)} %get-tuple-element.29), channel_id=1, source_target_pairs={{4,0},{8,4},{12,8},{16,12},{20,16},{24,20},{28,24},{0,28},{5,1},{9... | collective-permute-start | bytes 3145736 | tf_op jit(solution)/shard_map/ppermute | solution.py:64
  7.6 0.0 copy-done
  7.6 0.0 copy-done.1
  7.6 1.5 %collective-permute-start.1 = (bf16[2,3,256,256]{3,2,1,0:T(8,128)(2,1)S(1)}, bf16[2,3,256,256]{3,2,1,0:T(8,128)(2,1)S(1)}, u32[]{:S(2)}, u32[]{:S(2)}) collective-permute-start(bf16[2,3,256,256]{3,2,1,0:T(8,128)(2,1)S(1)} %far.1.refs_2_), channel_id=1, source_target_pairs={{0,2},{1,3},{2,0},{3,1},{4,6},{5,7},{6,4},{7,5},{8,10},{9,11},{10,... | collective-permute-start | bytes 2359304 | tf_op jit(solution)/shard_map/ppermute | solution.py:68
  9.1 3.0 %near.1 = (bf16[2,3,256,256]{3,2,1,0:T(8,128)(2,1)S(1)}, bf16[2,3,256,256]{3,2,1,0:T(8,128)(2,1)S(1)}, bf16[2,3,256,256]{3,2,1,0:T(8,128)(2,1)S(1)}, bf16[13,256,128]{2,1,0:T(8,128)(2,1)S(1)}) custom-call(bf16[2,1024,1024]{2,1,0:T(8,128)(2,1)S(1)} %copy-done, bf16[3,2,1024,256]{3,2,1,0:T(8,128)(2,1)S(1)} %copy-done.1, bf16[2,3,256,256]{3,2,1,0:T(8,128)(2,1)S(1)} %far.1.refs_2_), custom_call_target="tpu_custom_call" | custom-call | tf_op jit(solution)/shard_map/near/pallas_call | solution.py:34
  12.1 0.1 collective-permute-start.2
  12.2 3.1 %collective-permute-start.6 = (bf16[13,256,128]{2,1,0:T(8,128)(2,1)S(1)}, bf16[13,256,128]{2,1,0:T(8,128)(2,1)S(1)}, u32[]{:S(2)}, u32[]{:S(2)}) collective-permute-start(bf16[13,256,128]{2,1,0:T(8,128)(2,1)S(1)} %get-tuple-element.35), channel_id=1, source_target_pairs={{4,0},{8,4},{12,8},{16,12},{20,16},{24,20},{28,24},{0,28},{5,1},{9... | collective-permute-start | bytes 2555912 | tf_op jit(solution)/shard_map/ppermute | solution.py:64
  15.4 0.3 collective-permute-start
  15.7 12.4 %collective-permute-done.1.refs_2_.refs_1_ = bf16[2,3,256,256]{3,2,1,0:T(8,128)(2,1)S(1)} collective-permute-done((bf16[2,3,256,256]{3,2,1,0:T(8,128)(2,1)S(1)}, bf16[2,3,256,256]{3,2,1,0:T(8,128)(2,1)S(1)}, u32[]{:S(2)}, u32[]{:S(2)}) %collective-permute-start.1) | collective-permute-done | bytes 786464 | tf_op jit(solution)/shard_map/ppermute | solution.py:68
  28.1 0.0 collective-permute-done.2.refs_1_.refs_2_
  28.1 3.1 %collective-permute-done.3.refs_0_ = bf16[4,256,512]{2,1,0:T(8,128)(2,1)S(1)} collective-permute-done((bf16[4,256,512]{2,1,0:T(8,128)(2,1)S(1)}, bf16[4,256,512]{2,1,0:T(8,128)(2,1)S(1)}, u32[]{:S(2)}, u32[]{:S(2)}) %collective-permute-start.3) | collective-permute-done | bytes 1048608 | tf_op jit(solution)/shard_map/ppermute | solution.py:64
  31.2 0.1 cut.1
  31.2 0.1 collective-permute-start.4
  31.3 0.5 collective-permute-start.5
  31.8 1.4 %collective-permute-done.4.refs_5_ = bf16[4,256,256]{2,1,0:T(8,128)(2,1)S(1)} collective-permute-done((bf16[4,256,256]{2,1,0:T(8,128)(2,1)S(1)}, bf16[4,256,256]{2,1,0:T(8,128)(2,1)S(1)}, u32[]{:S(2)}, u32[]{:S(2)}) %collective-permute-start.4) | collective-permute-done | bytes 524320 | tf_op jit(solution)/shard_map/ppermute | solution.py:68
  33.2 0.7 %collective-permute-done.5.refs_7_ = bf16[4,256,256]{2,1,0:T(8,128)(2,1)S(1)} collective-permute-done((bf16[4,256,256]{2,1,0:T(8,128)(2,1)S(1)}, bf16[4,256,256]{2,1,0:T(8,128)(2,1)S(1)}, u32[]{:S(2)}, u32[]{:S(2)}) %collective-permute-start.5) | collective-permute-done | bytes 524320 | tf_op jit(solution)/shard_map/ppermute | solution.py:68
  34.0 0.0 copy-start.2
  34.0 1.5 %gather.1 = (bf16[2,3,256,1024]{3,2,1,0:T(8,128)(2,1)S(1)}, bf16[4,2,2,256,512]{4,3,2,1,0:T(8,128)(2,1)S(1)}, bf16[4,2,2,256,512]{4,3,2,1,0:T(8,128)(2,1)S(1)}, bf16[3,256,128]{2,1,0:T(8,128)(2,1)S(1)}) custom-call(bf16[2,1024,1024]{2,1,0:T(8,128)(2,1)S(1)} %copy-done, bf16[2,3,256,256]{3,2,1,0:T(8,128)(2,1)S(1)} %collective-permute-done.1.refs_2_.refs_1_, ...), custom_call_target="tpu_custom_call" | custom-call | tf_op jit(solution)/shard_map/gather/pallas_call | solution.py:34
  35.5 1.6 %collective-permute-start.7 = (bf16[3,256,128]{2,1,0:T(8,128)(2,1)S(1)}, bf16[3,256,128]{2,1,0:T(8,128)(2,1)S(1)}, u32[]{:S(2)}, u32[]{:S(2)}) collective-permute-start(bf16[3,256,128]{2,1,0:T(8,128)(2,1)S(1)} %get-tuple-element.36), channel_id=1, source_target_pairs={{0,2},{1,3},{2,0},{3,1},{4,6},{5,7},{6,4},{7,5},{8,10},{9,11},{10,... | collective-permute-start | bytes 589832 | tf_op jit(solution)/shard_map/ppermute | solution.py:68
  37.1 6.8 %collective-permute-done.refs_1_ = bf16[2,3,256,256]{3,2,1,0:T(8,128)(2,1)S(1)} collective-permute-done((bf16[2,3,256,256]{3,2,1,0:T(8,128)(2,1)S(1)}, bf16[2,3,256,256]{3,2,1,0:T(8,128)(2,1)S(1)}, u32[]{:S(2)}, u32[]{:S(2)}) %collective-permute-start) | collective-permute-done | bytes 786464 | tf_op jit(solution)/shard_map/ppermute | solution.py:68
  43.9 0.0 copy-done.2
  43.9 2.0 %early.1 = (bf16[2,3,256,1024]{3,2,1,0:T(8,128)(2,1)S(1)}, bf16[3,2,256,512]{3,2,1,0:T(8,128)(2,1)S(1)}) custom-call(s32[2,3]{1,0:T(2,128)S(1)} %bitcast.1, bf16[2,3,256,256]{3,2,1,0:T(8,128)(2,1)S(1)} %collective-permute-done.refs_1_, bf16[4,2,2,256,512]{4,3,2,1,0:T(8,128)(2,1)S(1)} %get-tuple-element.32.refs_2_, ...), custom_call_target="tpu_custom_call", output_to_operand_aliasing={{0}: (3, {})} | custom-call | tf_op jit(solution)/shard_map/early/pallas_call | solution.py:34
  46.0 2.3 %collective-permute-done.6.refs_2_ = bf16[13,256,128]{2,1,0:T(8,128)(2,1)S(1)} collective-permute-done((bf16[13,256,128]{2,1,0:T(8,128)(2,1)S(1)}, bf16[13,256,128]{2,1,0:T(8,128)(2,1)S(1)}, u32[]{:S(2)}, u32[]{:S(2)}) %collective-permute-start.6) | collective-permute-done | bytes 852000 | tf_op jit(solution)/shard_map/ppermute | solution.py:64
  48.3 0.0 collective-permute-done.7.refs_3_
  48.3 0.0 collective-permute-start.8
  48.3 0.5 collective-permute-start.9
  48.8 1.4 %own_rows.1 = (f32[3,2,256,512]{3,2,1,0:T(8,128)S(1)}, bf16[4,2,2,256,512]{4,3,2,1,0:T(8,128)(2,1)S(1)}) custom-call(s32[2,3]{1,0:T(2,128)S(1)} %bitcast.2, bf16[2,3,256,1024]{3,2,1,0:T(8,128)(2,1)S(1)} %get-tuple-element.34.refs_1_, bf16[13,256,128]{2,1,0:T(8,128)(2,1)S(1)} %collective-permute-done.6.refs_2_, ...), custom_call_target="tpu_custom_call", output_to_operand_aliasing={{1}: (4, {})} | custom-call | tf_op jit(solution)/shard_map/own_rows/pallas_call | solution.py:34
  50.1 0.8 %collective-permute-done.9.refs_5_ = bf16[3,256,128]{2,1,0:T(8,128)(2,1)S(1)} collective-permute-done((bf16[3,256,128]{2,1,0:T(8,128)(2,1)S(1)}, bf16[3,256,128]{2,1,0:T(8,128)(2,1)S(1)}, u32[]{:S(2)}, u32[]{:S(2)}) %collective-permute-start.9) | collective-permute-done | bytes 196640 | tf_op jit(solution)/shard_map/ppermute | solution.py:68
  50.9 0.0 collective-permute-done.8.refs_4_
  50.9 2.2 %late.1 = (bf16[3,2,256,1024]{3,2,1,0:T(8,128)(2,1)}, bf16[4,2,2,256,512]{4,3,2,1,0:T(8,128)(2,1)S(1)}) custom-call(s32[2,3]{1,0:T(2,128)S(1)} %bitcast.3, bf16[2,3,256,1024]{3,2,1,0:T(8,128)(2,1)S(1)} %get-tuple-element.34.refs_1_, f32[3,2,256,512]{3,2,1,0:T(8,128)S(1)} %get-tuple-element.41.refs_2_, ...), custom_call_target="tpu_custom_call", output_to_operand_aliasing={{1}: (6, {})} | custom-call | tf_op jit(solution)/shard_map/late/pallas_call | solution.py:34
  (1 shorter events, 0.0 us)
Async XLA Ops:
  0.0 7.6 %copy-start = (bf16[2,1024,1024]{2,1,0:T(8,128)(2,1)S(1)}, bf16[2,1024,1024]{2,1,0:T(8,128)(2,1)}, u32[]{:S(2)}) copy-start(bf16[2,1024,1024]{2,1,0:T(8,128)(2,1)} %refs_0_.7) | copy-start | bytes 12582916
  0.0 7.6 %copy-start.1 = (bf16[3,2,1024,256]{3,2,1,0:T(8,128)(2,1)S(1)}, bf16[3,2,1024,256]{3,2,1,0:T(8,128)(2,1)}, u32[]{:S(2)}) copy-start(bf16[3,2,1024,256]{3,2,1,0:T(8,128)(2,1)} %refs_1_.5) | copy-start | bytes 9437188
  3.7 27.5 %collective-permute-start.3 = (bf16[4,256,512]{2,1,0:T(8,128)(2,1)S(1)}, bf16[4,256,512]{2,1,0:T(8,128)(2,1)S(1)}, u32[]{:S(2)}, u32[]{:S(2)}) collective-permute-start(bf16[4,256,512]{2,1,0:T(8,128)(2,1)S(1)} %get-tuple-element.29), channel_id=1, source_target_pairs={{4,0},{8,4},{12,8},{16,12},{20,16},{24,20},{28,24},{0,28},{5,1},{9... | collective-permute-start | bytes 3145736 | tf_op jit(solution)/shard_map/ppermute | solution.py:64
  7.6 20.5 %collective-permute-start.1 = (bf16[2,3,256,256]{3,2,1,0:T(8,128)(2,1)S(1)}, bf16[2,3,256,256]{3,2,1,0:T(8,128)(2,1)S(1)}, u32[]{:S(2)}, u32[]{:S(2)}) collective-permute-start(bf16[2,3,256,256]{3,2,1,0:T(8,128)(2,1)S(1)} %far.1.refs_2_), channel_id=1, source_target_pairs={{0,2},{1,3},{2,0},{3,1},{4,6},{5,7},{6,4},{7,5},{8,10},{9,11},{10,... | collective-permute-start | bytes 2359304 | tf_op jit(solution)/shard_map/ppermute | solution.py:68
  12.1 15.9 %collective-permute-start.2 = (bf16[2,3,256,256]{3,2,1,0:T(8,128)(2,1)S(1)}, bf16[2,3,256,256]{3,2,1,0:T(8,128)(2,1)S(1)}, u32[]{:S(2)}, u32[]{:S(2)}) collective-permute-start(bf16[2,3,256,256]{3,2,1,0:T(8,128)(2,1)S(1)} %get-tuple-element.27), channel_id=1, source_target_pairs={{0,1},{1,0},{2,3},{3,2},{4,5},{5,4},{6,7},{7,6},{8,9},{9,8},{10,11... | collective-permute-start | bytes 2359304 | tf_op jit(solution)/shard_map/ppermute | solution.py:68
  12.2 36.1 %collective-permute-start.6 = (bf16[13,256,128]{2,1,0:T(8,128)(2,1)S(1)}, bf16[13,256,128]{2,1,0:T(8,128)(2,1)S(1)}, u32[]{:S(2)}, u32[]{:S(2)}) collective-permute-start(bf16[13,256,128]{2,1,0:T(8,128)(2,1)S(1)} %get-tuple-element.35), channel_id=1, source_target_pairs={{4,0},{8,4},{12,8},{16,12},{20,16},{24,20},{28,24},{0,28},{5,1},{9... | collective-permute-start | bytes 2555912 | tf_op jit(solution)/shard_map/ppermute | solution.py:64
  15.4 28.6 %collective-permute-start = (bf16[2,3,256,256]{3,2,1,0:T(8,128)(2,1)S(1)}, bf16[2,3,256,256]{3,2,1,0:T(8,128)(2,1)S(1)}, u32[]{:S(2)}, u32[]{:S(2)}) collective-permute-start(bf16[2,3,256,256]{3,2,1,0:T(8,128)(2,1)S(1)} %get-tuple-element.26), channel_id=1, source_target_pairs={{0,3},{1,2},{2,1},{3,0},{4,7},{5,6},{6,5},{7,4},{8,11},{9,10},{10,... | collective-permute-start | bytes 2359304 | tf_op jit(solution)/shard_map/ppermute | solution.py:68
  31.2 2.0 %collective-permute-start.4 = (bf16[4,256,256]{2,1,0:T(8,128)(2,1)S(1)}, bf16[4,256,256]{2,1,0:T(8,128)(2,1)S(1)}, u32[]{:S(2)}, u32[]{:S(2)}) collective-permute-start(bf16[4,256,256]{2,1,0:T(8,128)(2,1)S(1)} %get-tuple-element.30.refs_4_), channel_id=1, source_target_pairs={{0,1},{1,0},{2,3},{3,2},{4,5},{5,4},{6,7},{7,6},{8,9},{9,8},{10,11... | collective-permute-start | bytes 1572872 | tf_op jit(solution)/shard_map/ppermute | solution.py:68
  31.3 2.6 %collective-permute-start.5 = (bf16[4,256,256]{2,1,0:T(8,128)(2,1)S(1)}, bf16[4,256,256]{2,1,0:T(8,128)(2,1)S(1)}, u32[]{:S(2)}, u32[]{:S(2)}) collective-permute-start(bf16[4,256,256]{2,1,0:T(8,128)(2,1)S(1)} %get-tuple-element.31.refs_6_), channel_id=1, source_target_pairs={{0,1},{1,0},{2,3},{3,2},{4,5},{5,4},{6,7},{7,6},{8,9},{9,8},{10,11... | collective-permute-start | bytes 1572872 | tf_op jit(solution)/shard_map/ppermute | solution.py:68
  34.0 10.0 %copy-start.2 = (s32[3,2]{0,1:T(2,128)S(1)}, s32[3,2]{0,1:T(2,128)}, u32[]{:S(2)}) copy-start(s32[3,2]{0,1:T(2,128)} %param.5) | copy-start | bytes 76
  35.5 12.8 %collective-permute-start.7 = (bf16[3,256,128]{2,1,0:T(8,128)(2,1)S(1)}, bf16[3,256,128]{2,1,0:T(8,128)(2,1)S(1)}, u32[]{:S(2)}, u32[]{:S(2)}) collective-permute-start(bf16[3,256,128]{2,1,0:T(8,128)(2,1)S(1)} %get-tuple-element.36), channel_id=1, source_target_pairs={{0,2},{1,3},{2,0},{3,1},{4,6},{5,7},{6,4},{7,5},{8,10},{9,11},{10,... | collective-permute-start | bytes 589832 | tf_op jit(solution)/shard_map/ppermute | solution.py:68
  48.3 2.7 %collective-permute-start.8 = (bf16[13,256,128]{2,1,0:T(8,128)(2,1)S(1)}, bf16[13,256,128]{2,1,0:T(8,128)(2,1)S(1)}, u32[]{:S(2)}, u32[]{:S(2)}) collective-permute-start(bf16[13,256,128]{2,1,0:T(8,128)(2,1)S(1)} %collective-permute-done.6.refs_2_), channel_id=1, source_target_pairs={{0,1},{1,0},{2,3},{3,2},{4,5},{5,4},{6,7},{7,6},{8,9},{9,8},{10,11... | collective-permute-start | bytes 2555912 | tf_op jit(solution)/shard_map/ppermute | solution.py:68
  48.3 2.7 %collective-permute-start.9 = (bf16[3,256,128]{2,1,0:T(8,128)(2,1)S(1)}, bf16[3,256,128]{2,1,0:T(8,128)(2,1)S(1)}, u32[]{:S(2)}, u32[]{:S(2)}) collective-permute-start(bf16[3,256,128]{2,1,0:T(8,128)(2,1)S(1)} %collective-permute-done.7.refs_3_), channel_id=1, source_target_pairs={{0,1},{1,0},{2,3},{3,2},{4,5},{5,4},{6,7},{7,6},{8,9},{9,8},{10,11... | collective-permute-start | bytes 589832 | tf_op jit(solution)/shard_map/ppermute | solution.py:68

commit v10 on v7

--- a/solution.py
+++ b/solution.py
@@ -424,16 +424,16 @@
         for flavour in range(flavours):
             rest = partial(place, partner, sector, flavour, 1, left, right)
             stage[flavour, sector] = (total[flavour, sector] + rest).astype(jnp.bfloat16)
-            at = 0
-            for number, (start, count) in enumerate(units):
-                copy = pltpu.make_async_copy(
-                    stage.at[flavour, sector, :, pl.ds(at, count * unit)],
-                    out.at[flavour, sector, :, pl.ds(first_column(start, place, unit), count * unit)],
-                    out_sems.at[sector * flavours + flavour, number],
-                )
-                copy.start()
-                out_copies.append(copy)
-                at += count * unit
+        at = 0
+        for number, (start, count) in enumerate(units):
+            copy = pltpu.make_async_copy(
+                stage.at[:, sector, :, pl.ds(at, count * unit)],
+                out.at[:, sector, :, pl.ds(first_column(start, place, unit), count * unit)],
+                out_sems.at[sector * flavours, number],
+            )
+            copy.start()
+            out_copies.append(copy)
+            at += count * unit
     for copy in out_copies:
         copy.wait()
 

time: 53.3 us -> 53.7 us (level)
  transfers between devices with their start and end apart: 10 -> 10, of which waited for: 7 -> 7; matrix products, arithmetic and copies ran while one was open for 0% -> 0% of each run, Pallas kernels for 14% -> 13%
where the time goes in v10:
time: 53.7 us; the launch traced here: 53.5 us
  waiting for transfers between devices  26.7 us (50%)
  Pallas kernels  14.2 us (26%)
  starting transfers between devices  12.5 us (23%)
    ppermute x8, waiting for transfers between devices, swapped(): lax.ppermute(block, 'slab', [(i, i ^ distance) for i in range(lax.axis_si...  21.4 us
    pallas_call x8, Pallas kernels, kernel_call(): pl.pallas_call(kernel, out_shape=shapes, in_specs=specs, out_specs=out_sp...  14.2 us
    ppermute x2, starting transfers between devices, previous(): lax.ppermute(block, 'sec', [((i + 1) % count, i) for i in range(count)])  7.12 us
    ppermute x8, starting transfers between devices, swapped(): lax.ppermute(block, 'slab', [(i, i ^ distance) for i in range(lax.axis_si...  5.4 us
    ppermute x2, waiting for transfers between devices, previous(): lax.ppermute(block, 'sec', [((i + 1) % count, i) for i in range(count)])  5.39 us
  transfers between devices with their start and end apart: 10, of which 7 were waited for; matrix products, arithmetic and copies ran while one was open for 0% of the time, Pallas kernels for 13%

profile of v10, /device:TPU:0, one launch (start us, length us, event | category | flops | bytes accessed | tf_op | source)
XLA Modules:
  0.0 53.5 jit_solution(989134909209207814)
XLA Ops:
  0.0 0.0 copy-start
  0.0 0.0 copy-start.1
  0.0 4.4 %part.1 = (bf16[4,256,512]{2,1,0:T(8,128)(2,1)S(1)}, bf16[2,3,256,256]{3,2,1,0:T(8,128)(2,1)S(1)}, bf16[2,3,256,256]{3,2,1,0:T(8,128)(2,1)S(1)}) custom-call(bf16[2,1024,1024]{2,1,0:T(8,128)(2,1)} %refs_0_.7, bf16[3,2,1024,256]{3,2,1,0:T(8,128)(2,1)} %refs_1_.5), custom_call_target="tpu_custom_call" | custom-call | tf_op jit(solution)/shard_map/part/pallas_call | solution.py:34
  4.4 3.2 %collective-permute-start.3 = (bf16[4,256,512]{2,1,0:T(8,128)(2,1)S(1)}, bf16[4,256,512]{2,1,0:T(8,128)(2,1)S(1)}, u32[]{:S(2)}, u32[]{:S(2)}) collective-permute-start(bf16[4,256,512]{2,1,0:T(8,128)(2,1)S(1)} %get-tuple-element.33), channel_id=1, source_target_pairs={{4,0},{8,4},{12,8},{16,12},{20,16},{24,20},{28,24},{0,28},{5,1},{9... | collective-permute-start | bytes 3145736 | tf_op jit(solution)/shard_map/ppermute | solution.py:64
  7.6 0.0 copy-done
  7.6 0.0 copy-done.1
  7.6 1.5 %collective-permute-start.1 = (bf16[2,3,256,256]{3,2,1,0:T(8,128)(2,1)S(1)}, bf16[2,3,256,256]{3,2,1,0:T(8,128)(2,1)S(1)}, u32[]{:S(2)}, u32[]{:S(2)}) collective-permute-start(bf16[2,3,256,256]{3,2,1,0:T(8,128)(2,1)S(1)} %get-tuple-element.30.refs_2_), channel_id=1, source_target_pairs={{0,2},{1,3},{2,0},{3,1},{4,6},{5,7},{6,4},{7,5},{8,10},{9,11},{10,... | collective-permute-start | bytes 2359304 | tf_op jit(solution)/shard_map/ppermute | solution.py:68
  9.1 2.2 %near.1 = (bf16[2,3,256,256]{3,2,1,0:T(8,128)(2,1)S(1)}, bf16[2,3,256,256]{3,2,1,0:T(8,128)(2,1)S(1)}, bf16[13,256,128]{2,1,0:T(8,128)(2,1)S(1)}) custom-call(bf16[2,1024,1024]{2,1,0:T(8,128)(2,1)S(1)} %copy-done, bf16[3,2,1024,256]{3,2,1,0:T(8,128)(2,1)S(1)} %copy-done.1, bf16[2,3,256,256]{3,2,1,0:T(8,128)(2,1)S(1)} %get-tuple-element.30.refs_2_), custom_call_target="tpu_custom_call" | custom-call | tf_op jit(solution)/shard_map/near/pallas_call | solution.py:34
  11.3 0.1 collective-permute-start.2
  11.4 3.9 %collective-permute-start.6 = (bf16[13,256,128]{2,1,0:T(8,128)(2,1)S(1)}, bf16[13,256,128]{2,1,0:T(8,128)(2,1)S(1)}, u32[]{:S(2)}, u32[]{:S(2)}) collective-permute-start(bf16[13,256,128]{2,1,0:T(8,128)(2,1)S(1)} %get-tuple-element.39), channel_id=1, source_target_pairs={{4,0},{8,4},{12,8},{16,12},{20,16},{24,20},{28,24},{0,28},{5,1},{9... | collective-permute-start | bytes 2555912 | tf_op jit(solution)/shard_map/ppermute | solution.py:64
  15.3 0.4 collective-permute-start
  15.7 12.4 %collective-permute-done.1.refs_2_.refs_1_ = bf16[2,3,256,256]{3,2,1,0:T(8,128)(2,1)S(1)} collective-permute-done((bf16[2,3,256,256]{3,2,1,0:T(8,128)(2,1)S(1)}, bf16[2,3,256,256]{3,2,1,0:T(8,128)(2,1)S(1)}, u32[]{:S(2)}, u32[]{:S(2)}) %collective-permute-start.1) | collective-permute-done | bytes 786464 | tf_op jit(solution)/shard_map/ppermute | solution.py:68
  28.1 0.0 collective-permute-done.2.refs_1_.refs_2_
  28.1 3.1 %collective-permute-done.3.refs_0_ = bf16[4,256,512]{2,1,0:T(8,128)(2,1)S(1)} collective-permute-done((bf16[4,256,512]{2,1,0:T(8,128)(2,1)S(1)}, bf16[4,256,512]{2,1,0:T(8,128)(2,1)S(1)}, u32[]{:S(2)}, u32[]{:S(2)}) %collective-permute-start.3) | collective-permute-done | bytes 1048608 | tf_op jit(solution)/shard_map/ppermute | solution.py:64
  31.2 0.1 cut.1
  31.2 0.1 collective-permute-start.4
  31.3 0.5 collective-permute-start.5
  31.8 1.4 %collective-permute-done.4.refs_5_ = bf16[4,256,256]{2,1,0:T(8,128)(2,1)S(1)} collective-permute-done((bf16[4,256,256]{2,1,0:T(8,128)(2,1)S(1)}, bf16[4,256,256]{2,1,0:T(8,128)(2,1)S(1)}, u32[]{:S(2)}, u32[]{:S(2)}) %collective-permute-start.4) | collective-permute-done | bytes 524320 | tf_op jit(solution)/shard_map/ppermute | solution.py:68
  33.2 0.7 %collective-permute-done.5.refs_7_ = bf16[4,256,256]{2,1,0:T(8,128)(2,1)S(1)} collective-permute-done((bf16[4,256,256]{2,1,0:T(8,128)(2,1)S(1)}, bf16[4,256,256]{2,1,0:T(8,128)(2,1)S(1)}, u32[]{:S(2)}, u32[]{:S(2)}) %collective-permute-start.5) | collective-permute-done | bytes 524320 | tf_op jit(solution)/shard_map/ppermute | solution.py:68
  34.0 0.0 copy-start.2
  34.0 1.5 %gather.1 = (bf16[2,3,256,1024]{3,2,1,0:T(8,128)(2,1)S(1)}, bf16[4,2,2,256,512]{4,3,2,1,0:T(8,128)(2,1)S(1)}, bf16[4,2,2,256,512]{4,3,2,1,0:T(8,128)(2,1)S(1)}, bf16[3,256,128]{2,1,0:T(8,128)(2,1)S(1)}) custom-call(bf16[2,1024,1024]{2,1,0:T(8,128)(2,1)S(1)} %copy-done, bf16[2,3,256,256]{3,2,1,0:T(8,128)(2,1)S(1)} %collective-permute-done.1.refs_2_.refs_1_, ...), custom_call_target="tpu_custom_call" | custom-call | tf_op jit(solution)/shard_map/gather/pallas_call | solution.py:34
  35.5 2.4 %collective-permute-start.7 = (bf16[3,256,128]{2,1,0:T(8,128)(2,1)S(1)}, bf16[3,256,128]{2,1,0:T(8,128)(2,1)S(1)}, u32[]{:S(2)}, u32[]{:S(2)}) collective-permute-start(bf16[3,256,128]{2,1,0:T(8,128)(2,1)S(1)} %get-tuple-element.40), channel_id=1, source_target_pairs={{0,2},{1,3},{2,0},{3,1},{4,6},{5,7},{6,4},{7,5},{8,10},{9,11},{10,... | collective-permute-start | bytes 589832 | tf_op jit(solution)/shard_map/ppermute | solution.py:68
  37.9 6.1 %collective-permute-done.refs_1_ = bf16[2,3,256,256]{3,2,1,0:T(8,128)(2,1)S(1)} collective-permute-done((bf16[2,3,256,256]{3,2,1,0:T(8,128)(2,1)S(1)}, bf16[2,3,256,256]{3,2,1,0:T(8,128)(2,1)S(1)}, u32[]{:S(2)}, u32[]{:S(2)}) %collective-permute-start) | collective-permute-done | bytes 786464 | tf_op jit(solution)/shard_map/ppermute | solution.py:68
  43.9 0.0 copy-done.2
  44.0 2.0 %early.1 = (bf16[2,3,256,1024]{3,2,1,0:T(8,128)(2,1)S(1)}, bf16[3,2,256,512]{3,2,1,0:T(8,128)(2,1)S(1)}) custom-call(s32[2,3]{1,0:T(2,128)S(1)} %bitcast.1, bf16[2,3,256,256]{3,2,1,0:T(8,128)(2,1)S(1)} %collective-permute-done.refs_1_, bf16[4,2,2,256,512]{4,3,2,1,0:T(8,128)(2,1)S(1)} %get-tuple-element.36.refs_2_, ...), custom_call_target="tpu_custom_call", output_to_operand_aliasing={{0}: (3, {})} | custom-call | tf_op jit(solution)/shard_map/early/pallas_call | solution.py:34
  46.0 2.3 %collective-permute-done.6.refs_2_ = bf16[13,256,128]{2,1,0:T(8,128)(2,1)S(1)} collective-permute-done((bf16[13,256,128]{2,1,0:T(8,128)(2,1)S(1)}, bf16[13,256,128]{2,1,0:T(8,128)(2,1)S(1)}, u32[]{:S(2)}, u32[]{:S(2)}) %collective-permute-start.6) | collective-permute-done | bytes 852000 | tf_op jit(solution)/shard_map/ppermute | solution.py:64
  48.3 0.0 collective-permute-done.7.refs_3_
  48.3 0.0 collective-permute-start.8
  48.3 0.5 collective-permute-start.9
  48.8 1.4 %own_rows.1 = (f32[3,2,256,512]{3,2,1,0:T(8,128)S(1)}, bf16[4,2,2,256,512]{4,3,2,1,0:T(8,128)(2,1)S(1)}) custom-call(s32[2,3]{1,0:T(2,128)S(1)} %bitcast.2, bf16[2,3,256,1024]{3,2,1,0:T(8,128)(2,1)S(1)} %get-tuple-element.38.refs_1_, bf16[13,256,128]{2,1,0:T(8,128)(2,1)S(1)} %collective-permute-done.6.refs_2_, ...), custom_call_target="tpu_custom_call", output_to_operand_aliasing={{1}: (4, {})} | custom-call | tf_op jit(solution)/shard_map/own_rows/pallas_call | solution.py:34
  50.2 0.8 %collective-permute-done.9.refs_5_ = bf16[3,256,128]{2,1,0:T(8,128)(2,1)S(1)} collective-permute-done((bf16[3,256,128]{2,1,0:T(8,128)(2,1)S(1)}, bf16[3,256,128]{2,1,0:T(8,128)(2,1)S(1)}, u32[]{:S(2)}, u32[]{:S(2)}) %collective-permute-start.9) | collective-permute-done | bytes 196640 | tf_op jit(solution)/shard_map/ppermute | solution.py:68
  51.0 0.0 collective-permute-done.8.refs_4_
  51.0 2.6 %late.1 = (bf16[3,2,256,1024]{3,2,1,0:T(8,128)(2,1)}, bf16[4,2,2,256,512]{4,3,2,1,0:T(8,128)(2,1)S(1)}) custom-call(s32[2,3]{1,0:T(2,128)S(1)} %bitcast.3, bf16[2,3,256,1024]{3,2,1,0:T(8,128)(2,1)S(1)} %get-tuple-element.38.refs_1_, f32[3,2,256,512]{3,2,1,0:T(8,128)S(1)} %get-tuple-element.45.refs_2_, ...), custom_call_target="tpu_custom_call", output_to_operand_aliasing={{1}: (6, {})} | custom-call | tf_op jit(solution)/shard_map/late/pallas_call | solution.py:34
  (1 shorter events, 0.0 us)
Async XLA Ops:
  0.0 7.6 %copy-start = (bf16[2,1024,1024]{2,1,0:T(8,128)(2,1)S(1)}, bf16[2,1024,1024]{2,1,0:T(8,128)(2,1)}, u32[]{:S(2)}) copy-start(bf16[2,1024,1024]{2,1,0:T(8,128)(2,1)} %refs_0_.7) | copy-start | bytes 12582916
  0.0 7.6 %copy-start.1 = (bf16[3,2,1024,256]{3,2,1,0:T(8,128)(2,1)S(1)}, bf16[3,2,1024,256]{3,2,1,0:T(8,128)(2,1)}, u32[]{:S(2)}) copy-start(bf16[3,2,1024,256]{3,2,1,0:T(8,128)(2,1)} %refs_1_.5) | copy-start | bytes 9437188
  4.4 26.8 %collective-permute-start.3 = (bf16[4,256,512]{2,1,0:T(8,128)(2,1)S(1)}, bf16[4,256,512]{2,1,0:T(8,128)(2,1)S(1)}, u32[]{:S(2)}, u32[]{:S(2)}) collective-permute-start(bf16[4,256,512]{2,1,0:T(8,128)(2,1)S(1)} %get-tuple-element.33), channel_id=1, source_target_pairs={{4,0},{8,4},{12,8},{16,12},{20,16},{24,20},{28,24},{0,28},{5,1},{9... | collective-permute-start | bytes 3145736 | tf_op jit(solution)/shard_map/ppermute | solution.py:64
  7.6 20.5 %collective-permute-start.1 = (bf16[2,3,256,256]{3,2,1,0:T(8,128)(2,1)S(1)}, bf16[2,3,256,256]{3,2,1,0:T(8,128)(2,1)S(1)}, u32[]{:S(2)}, u32[]{:S(2)}) collective-permute-start(bf16[2,3,256,256]{3,2,1,0:T(8,128)(2,1)S(1)} %get-tuple-element.30.refs_2_), channel_id=1, source_target_pairs={{0,2},{1,3},{2,0},{3,1},{4,6},{5,7},{6,4},{7,5},{8,10},{9,11},{10,... | collective-permute-start | bytes 2359304 | tf_op jit(solution)/shard_map/ppermute | solution.py:68
  11.3 16.8 %collective-permute-start.2 = (bf16[2,3,256,256]{3,2,1,0:T(8,128)(2,1)S(1)}, bf16[2,3,256,256]{3,2,1,0:T(8,128)(2,1)S(1)}, u32[]{:S(2)}, u32[]{:S(2)}) collective-permute-start(bf16[2,3,256,256]{3,2,1,0:T(8,128)(2,1)S(1)} %get-tuple-element.31), channel_id=1, source_target_pairs={{0,1},{1,0},{2,3},{3,2},{4,5},{5,4},{6,7},{7,6},{8,9},{9,8},{10,11... | collective-permute-start | bytes 2359304 | tf_op jit(solution)/shard_map/ppermute | solution.py:68
  11.4 36.9 %collective-permute-start.6 = (bf16[13,256,128]{2,1,0:T(8,128)(2,1)S(1)}, bf16[13,256,128]{2,1,0:T(8,128)(2,1)S(1)}, u32[]{:S(2)}, u32[]{:S(2)}) collective-permute-start(bf16[13,256,128]{2,1,0:T(8,128)(2,1)S(1)} %get-tuple-element.39), channel_id=1, source_target_pairs={{4,0},{8,4},{12,8},{16,12},{20,16},{24,20},{28,24},{0,28},{5,1},{9... | collective-permute-start | bytes 2555912 | tf_op jit(solution)/shard_map/ppermute | solution.py:64
  15.3 28.6 %collective-permute-start = (bf16[2,3,256,256]{3,2,1,0:T(8,128)(2,1)S(1)}, bf16[2,3,256,256]{3,2,1,0:T(8,128)(2,1)S(1)}, u32[]{:S(2)}, u32[]{:S(2)}) collective-permute-start(bf16[2,3,256,256]{3,2,1,0:T(8,128)(2,1)S(1)} %get-tuple-element.29), channel_id=1, source_target_pairs={{0,3},{1,2},{2,1},{3,0},{4,7},{5,6},{6,5},{7,4},{8,11},{9,10},{10,... | collective-permute-start | bytes 2359304 | tf_op jit(solution)/shard_map/ppermute | solution.py:68
  31.2 2.0 %collective-permute-start.4 = (bf16[4,256,256]{2,1,0:T(8,128)(2,1)S(1)}, bf16[4,256,256]{2,1,0:T(8,128)(2,1)S(1)}, u32[]{:S(2)}, u32[]{:S(2)}) collective-permute-start(bf16[4,256,256]{2,1,0:T(8,128)(2,1)S(1)} %get-tuple-element.34.refs_4_), channel_id=1, source_target_pairs={{0,1},{1,0},{2,3},{3,2},{4,5},{5,4},{6,7},{7,6},{8,9},{9,8},{10,11... | collective-permute-start | bytes 1572872 | tf_op jit(solution)/shard_map/ppermute | solution.py:68
  31.3 2.6 %collective-permute-start.5 = (bf16[4,256,256]{2,1,0:T(8,128)(2,1)S(1)}, bf16[4,256,256]{2,1,0:T(8,128)(2,1)S(1)}, u32[]{:S(2)}, u32[]{:S(2)}) collective-permute-start(bf16[4,256,256]{2,1,0:T(8,128)(2,1)S(1)} %get-tuple-element.35.refs_6_), channel_id=1, source_target_pairs={{0,1},{1,0},{2,3},{3,2},{4,5},{5,4},{6,7},{7,6},{8,9},{9,8},{10,11... | collective-permute-start | bytes 1572872 | tf_op jit(solution)/shard_map/ppermute | solution.py:68
  34.0 10.0 %copy-start.2 = (s32[3,2]{0,1:T(2,128)S(1)}, s32[3,2]{0,1:T(2,128)}, u32[]{:S(2)}) copy-start(s32[3,2]{0,1:T(2,128)} %param.5) | copy-start | bytes 76
  35.5 12.8 %collective-permute-start.7 = (bf16[3,256,128]{2,1,0:T(8,128)(2,1)S(1)}, bf16[3,256,128]{2,1,0:T(8,128)(2,1)S(1)}, u32[]{:S(2)}, u32[]{:S(2)}) collective-permute-start(bf16[3,256,128]{2,1,0:T(8,128)(2,1)S(1)} %get-tuple-element.40), channel_id=1, source_target_pairs={{0,2},{1,3},{2,0},{3,1},{4,6},{5,7},{6,4},{7,5},{8,10},{9,11},{10,... | collective-permute-start | bytes 589832 | tf_op jit(solution)/shard_map/ppermute | solution.py:68
  48.3 2.7 %collective-permute-start.8 = (bf16[13,256,128]{2,1,0:T(8,128)(2,1)S(1)}, bf16[13,256,128]{2,1,0:T(8,128)(2,1)S(1)}, u32[]{:S(2)}, u32[]{:S(2)}) collective-permute-start(bf16[13,256,128]{2,1,0:T(8,128)(2,1)S(1)} %collective-permute-done.6.refs_2_), channel_id=1, source_target_pairs={{0,1},{1,0},{2,3},{3,2},{4,5},{5,4},{6,7},{7,6},{8,9},{9,8},{10,11... | collective-permute-start | bytes 2555912 | tf_op jit(solution)/shard_map/ppermute | solution.py:68
  48.3 2.7 %collective-permute-start.9 = (bf16[3,256,128]{2,1,0:T(8,128)(2,1)S(1)}, bf16[3,256,128]{2,1,0:T(8,128)(2,1)S(1)}, u32[]{:S(2)}, u32[]{:S(2)}) collective-permute-start(bf16[3,256,128]{2,1,0:T(8,128)(2,1)S(1)} %collective-permute-done.7.refs_3_), channel_id=1, source_target_pairs={{0,1},{1,0},{2,3},{3,2},{4,5},{5,4},{6,7},{7,6},{8,9},{9,8},{10,11... | collective-permute-start | bytes 589832 | tf_op jit(solution)/shard_map/ppermute | solution.py:68
